TPU v7x, 32 devices: a whole 2x2x4 slice. The times are simulated.
32 devices in a mesh: rx: 4 (over x, core), ry: 8 (over z, y).
Axes of the slice: x: 2, y: 2, z: 4, core: 2. Of those that a mesh axis runs over, the one named last changes fastest.
Arguments:
- noisy_input: bfloat16 [36864, 12, 128], P(('rx', 'ry')), may hold values from -6 to 6
- adjacency: bfloat16 [288, 6, 128, 128], P(('rx', 'ry')), may hold values from -0.21875 to 0.21875
- neighbours: int32 [288, 6], P(('rx', 'ry')), may hold values from 0 to 8, as said below
- norm_gain: float32 [128], replicated, may hold values from 0.1 to 1.9
- w_mix: bfloat16 [128, 128], replicated, may hold values from -0.5 to 0.5
- pool_weight: bfloat16 [36864], P(('rx', 'ry')), may hold values from 0.049804688 to 0.29882812
- cluster: int32 [36864], P(('rx', 'ry')), may hold values from 0 to 143, as said below
- owner_ids: int32 [4608, 1], P(('rx', 'ry')), may hold values from 0 to 31; in each aligned block of 144 rows (0 to 143, 144 to 287, ...) at most 9 rows name the same one
- w_coarse: bfloat16 [128, 128], replicated, may hold values from -0.5 to 0.5
- w_region: bfloat16 [128, 128], replicated, may hold values from -0.5 to 0.5
- w_out: bfloat16 [128, 128], replicated, may hold values from -0.5 to 0.5
Outputs:
- denoised: bfloat16 [36864, 12, 128], P(('rx', 'ry'))
Inputs may be any that keep to these rules, and one draw needn't show every extreme that they name: `neighbours`: the 6 codes of one block are different. `cluster`: among the 1152 nodes of one device's square each value is taken by exactly 8 nodes. `owner_ids`: in each aligned block of 144 rows no value is named by more than 9 rows, and one value is named by exactly 9 rows in some or all blocks; every value is named by some row.
All inputs are finite; a program needn't handle non-finite values.
Results may differ from a plain program's by a relative error of at most 0.015.
Values may be sent and summed in bfloat16 or wider, within the bound.
A program may use at most 128 MiB of HBM per device.

v0:
```python
import jax
import jax.numpy as jnp
from jax import lax
from jax.sharding import PartitionSpec as P

GB = 3
BLK = 128


def with_halo(block, sides, width):
    for axis, dim in sides:
        count = lax.axis_size(axis)
        forward = [(i, i + 1) for i in range(count - 1)]
        backward = [(target, source) for source, target in forward]
        low = lax.ppermute(
            lax.slice_in_dim(block, block.shape[dim] - width, None, axis=dim), axis, forward
        )
        high = lax.ppermute(lax.slice_in_dim(block, 0, width, axis=dim), axis, backward)
        block = jnp.concatenate([low, block, high], axis=dim)
    return block


def diffuse(values_in, adjacency, offsets):
    features = values_in.shape[1] * values_in.shape[2]
    grid_blocks = values_in.reshape(GB, GB, BLK, features)
    extended = with_halo(grid_blocks, (("rx", 0), ("ry", 1)), 1)
    padded_side = GB + 2
    flat_blocks = extended.reshape(padded_side * padded_side, BLK, features)
    positions = jnp.arange(GB * GB, dtype=jnp.int32)
    across = positions // GB
    within = positions % GB
    block_index = (across[:, None] + offsets // 3) * padded_side + within[:, None] + offsets % 3
    gathered = flat_blocks[block_index]
    summed = jnp.einsum("bkij,bkjf->bif", adjacency, gathered, preferred_element_type=jnp.float32)
    return summed.reshape(values_in.shape)


def on_device(
    noisy_input,
    adjacency,
    neighbours,
    norm_gain,
    w_mix,
    pool_weight,
    cluster,
    owner_ids,
    w_coarse,
    w_region,
    w_out,
):
    node_rows, steps_count, channels = noisy_input.shape
    features = steps_count * channels
    diffused = diffuse(noisy_input, adjacency, neighbours).astype(jnp.bfloat16)
    scaled = diffused.astype(jnp.float32)
    mean_square = jnp.mean(scaled * scaled, axis=-1, keepdims=True)
    normed = (scaled * lax.rsqrt(mean_square + 1e-06) * norm_gain).astype(jnp.bfloat16)
    mixed = jnp.dot(
        normed.reshape(-1, channels), w_mix, preferred_element_type=jnp.float32
    ).reshape(noisy_input.shape)
    encoded = (noisy_input.astype(jnp.float32) + jax.nn.silu(mixed)).astype(jnp.bfloat16)
    coarse_count = owner_ids.shape[0]
    coarse_iota = jnp.arange(coarse_count, dtype=jnp.int32)
    pooling = jnp.where(
        cluster[None, :] == coarse_iota[:, None], pool_weight[None, :], jnp.zeros((), jnp.bfloat16)
    )
    pooled = jnp.dot(
        pooling, encoded.reshape(node_rows, features), preferred_element_type=jnp.float32
    ).astype(jnp.bfloat16)
    row_devices = lax.axis_size("rx")
    col_devices = lax.axis_size("ry")
    devices = row_devices * col_devices
    capacity = max(2, 2 * coarse_count // devices)
    targets = owner_ids[:, 0]
    owner_hot = (targets[:, None] == jnp.arange(devices, dtype=jnp.int32)[None, :]).astype(
        jnp.float32
    )
    denominator = float(coarse_count)
    earlier = jnp.cumsum(owner_hot, axis=0) - owner_hot
    slot_rank = jnp.sum(earlier * owner_hot, axis=1).astype(jnp.int32)
    destination = targets * capacity + slot_rank
    dispatch = (
        destination[None, :] == jnp.arange(devices * capacity, dtype=jnp.int32)[:, None]
    ).astype(jnp.bfloat16)
    outgoing = jnp.dot(dispatch, pooled, preferred_element_type=jnp.float32).astype(jnp.bfloat16)
    outgoing = outgoing.reshape(devices * capacity, steps_count, channels)
    arrived = lax.all_to_all(outgoing, ("rx", "ry"), split_axis=0, concat_axis=0, tiled=True)
    projected = jnp.einsum("rsc,cd->rsd", arrived, w_coarse, preferred_element_type=jnp.float32)
    lifted = jax.nn.silu(projected).astype(jnp.bfloat16)
    region = (jnp.sum(lifted.astype(jnp.float32), axis=0) / denominator).astype(jnp.bfloat16)
    reach = jnp.dot(region, w_region, preferred_element_type=jnp.float32)
    came_back = lax.all_to_all(
        (arrived.astype(jnp.float32) + lifted.astype(jnp.float32) + reach[None]).astype(
            jnp.bfloat16
        ),
        ("rx", "ry"),
        split_axis=0,
        concat_axis=0,
        tiled=True,
    )
    restored = jnp.dot(
        dispatch.T,
        came_back.reshape(devices * capacity, features),
        preferred_element_type=jnp.float32,
    ).astype(jnp.bfloat16)
    unpooling = (cluster[:, None] == coarse_iota[None, :]).astype(jnp.bfloat16)
    spread_back = jnp.dot(unpooling, restored, preferred_element_type=jnp.float32).reshape(
        noisy_input.shape
    )
    decoder_in = (encoded.astype(jnp.float32) + spread_back).astype(jnp.bfloat16)
    second = diffuse(decoder_in, adjacency, neighbours).astype(jnp.bfloat16)
    output = jnp.dot(
        second.reshape(-1, channels), w_out, preferred_element_type=jnp.float32
    ).reshape(noisy_input.shape)
    return (decoder_in.astype(jnp.float32) + jax.nn.silu(output)).astype(jnp.bfloat16)


def solution(mesh):
    in_specs = (
        P(("rx", "ry"), None, None),
        P(("rx", "ry"), None, None, None),
        P(("rx", "ry"), None),
        P(),
        P(),
        P(("rx", "ry")),
        P(("rx", "ry")),
        P(("rx", "ry"), None),
        P(),
        P(),
        P(),
    )
    out_specs = P(("rx", "ry"), None, None)
    return jax.shard_map(
        on_device, mesh=mesh, in_specs=in_specs, out_specs=out_specs, check_vma=False
    )
```

profile of v0, /device:TPU:9, one launch (start us, length us, event | category | flops | bytes accessed | tf_op | source)
XLA Modules:
  0.0 473.2 jit_solution(718769418087339097)
XLA Ops:
  0.0 3.0 fusion.41
  3.0 0.8 copy.95
  3.8 1.7 slice.46
  5.4 3.7 collective-permute-start
  9.1 2.1 copy.97
  11.2 1.7 slice.48
  12.9 1.9 collective-permute-start.1
  14.8 12.9 %copy.96 = bf16[1152,12,128]{2,1,0:T(8,128)(2,1)} copy(bf16[1152,12,128]{2,0,1:T(8,128)(2,1)} %param.11) | data formatting | bytes 7077888 | tf_op args[0]
  27.7 7.3 %reshape.108 = bf16[3,3,128,1536]{3,2,1,0:T(8,128)(2,1)} reshape(bf16[1152,12,128]{2,1,0:T(8,128)(2,1)} %copy.96) | data formatting | bytes 7077888 | tf_op jit(solution)/shard_map/reshape | solution.py:25
  35.1 1.3 constant_dynamic-update-slice_fusion.2
  36.4 2.2 constant_dynamic-update-slice_fusion.1
  38.7 0.1 constant_dynamic-update-slice_fusion
  38.8 2.5 fusion.39
  41.2 1.2 copy-done.3
  42.5 3.1 collective-permute-start.2
  45.6 3.2 collective-permute-start.3
  48.8 5.7 %copy.94 = bf16[1152,12,128]{0,2,1:T(8,128)(2,1)} copy(bf16[1152,12,128]{2,0,1:T(8,128)(2,1)} %param.11) | data formatting | bytes 7077888 | tf_op args[0]
  54.6 0.1 copy.98
  54.8 0.6 reduce-window.6
  55.4 0.2 slice_reduce_fusion
  55.8 74.5 %collective-permute-done.2 = bf16[5,1,128,1536]{3,2,1,0:T(8,128)(2,1)} collective-permute-done((bf16[5,1,128,1536]{3,2,1,0:T(8,128)(2,1)}, bf16[5,1,128,1536]{3,2,1,0:T(8,128)(2,1)}, u32[]{:S(2)}, u32[]{:S(2)}) %collective-permute-start.2) | collective-permute-done | bytes 1966112 | tf_op jit(solution)/shard_map/ppermute | solution.py:15
  130.3 1.8 collective-permute-done.3
  132.1 9.5 %pad_maximum_fusion = bf16[5,5,128,1536]{3,2,1,0:T(8,128)(2,1)} fusion(bf16[5,1,128,1536]{3,2,1,0:T(8,128)(2,1)} %collective-permute-done.3, bf16[5,3,128,1536]{3,2,1,0:T(8,128)(2,1)} %copy-done.3, bf16[5,1,128,1536]{3,2,1,0:T(8,128)(2,1)} %collective-permute-done.2), kind=kLoop, calls=%fused_computation.2 | loop fusion | flops 9830400 | bytes 19660800 | tf_op jit(solution)/shard_map/concatenate | solution.py:19
  141.6 13.1 %gather_fusion = bf16[54,128,1536]{2,1,0:T(8,128)(2,1)} fusion(bf16[25,128,1536]{2,1,0:T(8,128)(2,1)} %bitcast.62, s32[1024]{0:T(1024)S(1)} %pad_clamp_fusion), kind=kCustom, calls=%fused_computation | custom fusion | bytes 42467544 | tf_op jit(solution)/shard_map/gather | solution.py:33
  154.7 12.4 %convert_bitcast_fusion = f32[9,128,1536]{1,2,0:T(8,128)} fusion(bf16[9,6,128,1536]{3,2,1,0:T(8,128)(2,1)} %bitcast.63, bf16[9,6,128,128]{3,2,1,0:T(8,128)(2,1)S(1)} %copy-done), kind=kOutput, calls=%fused_computation.8 | convolution fusion | flops 2721447936 | bytes 30081024 | tf_op jit(solution)/shard_map/bkij,bkjf->bif/dot_general | solution.py:34
  167.1 8.0 %copy.100 = f32[9,128,1536]{2,1,0:T(8,128)} copy(f32[9,128,1536]{1,2,0:T(8,128)} %convert_bitcast_fusion) | data formatting | bytes 14155776 | tf_op jit(solution)/shard_map/convert_element_type | solution.py:54
  175.1 9.1 %reshape.118 = f32[1152,12,128]{2,1,0:T(8,128)} reshape(f32[9,128,1536]{2,1,0:T(8,128)} %copy.100) | data formatting | bytes 14155776 | tf_op jit(solution)/shard_map/convert_element_type | solution.py:54
  184.2 5.1 %multiply_reduce_fusion = f32[1152,12]{1,0:T(8,128)S(1)} fusion(f32[1152,12,128]{2,1,0:T(8,128)} %reshape.118), kind=kLoop, calls=%fused_computation.5 | loop fusion | flops 3525120 | bytes 7133184 | tf_op jit(solution)/shard_map/reduce_sum | solution.py:55
  189.3 0.2 copy.101
  189.6 0.2 copy.102
  189.8 7.4 %multiply_convert_fusion = bf16[1152,12,128]{2,1,0:T(8,128)(2,1)S(1)} fusion(f32[1152,12,128]{2,1,0:T(8,128)} %reshape.118, f32[128]{0:T(128)S(1)} %copy-done.9, f32[1152,12]{1,0:T(8,128)S(1)} %copy.102), kind=kLoop, calls=%fused_computation.4 | loop fusion | flops 5308416 | bytes 10672640 | tf_op jit(solution)/shard_map/convert_element_type | solution.py:56
  197.3 4.7 add_convert_fusion.2
  202.0 4.5 convolution_convert_fusion
  206.4 1.7 reshape.113
  208.1 33.8 %all_to_all.10 = bf16[288,12,128]{2,1,0:T(8,128)(2,1)S(1)} all-to-all(bf16[288,12,128]{2,1,0:T(8,128)(2,1)S(1)} %reshape.113), channel_id=1, replica_groups=mesh['rx'=4,'ry'=8] {'rx','ry'}, dimensions={0} | all-to-all | bytes 1769472 | tf_op jit(solution)/shard_map/all_to_all | solution.py:86
  242.0 0.7 convert_reduce_fusion
  242.7 0.1 fusion.33
  242.8 0.3 fusion.4
  243.1 0.4 copy.109
  243.5 32.5 %all_to_all.11 = bf16[288,12,128]{2,1,0:T(8,128)(2,1)S(1)} all-to-all(bf16[288,12,128]{2,1,0:T(8,128)(2,1)S(1)} %copy.109), channel_id=1, replica_groups=mesh['rx'=4,'ry'=8] {'rx','ry'}, dimensions={0} | all-to-all | bytes 1769472 | tf_op jit(solution)/shard_map/all_to_all | solution.py:91
  276.0 4.7 fusion.5
  280.6 4.9 %add_convert_fusion.1 = bf16[1152,12,128]{0,2,1:T(8,128)(2,1)S(1)} fusion(f32[1152,12,128]{0,2,1:T(8,128)} %bitcast.64, bf16[1152,12,128]{0,2,1:T(8,128)(2,1)} %add_convert_fusion.2), kind=kLoop, calls=%fused_computation.10 | loop fusion | flops 5308416 | bytes 14155776 | tf_op jit(solution)/shard_map/convert_element_type | solution.py:109
  285.5 1.8 copy-done.2
  287.3 1.9 fusion.40
  289.2 3.3 reshape.145
  292.5 2.2 copy.128
  294.7 2.5 collective-permute-start.4
  297.1 3.3 reshape.147
  300.4 2.2 copy.130
  302.6 2.9 collective-permute-start.5
  305.6 8.5 %reshape.146 = bf16[3,3,128,1536]{2,1,0,3:T(4,128)(2,1)} reshape(bf16[1152,12,128]{0,2,1:T(8,128)(2,1)} %copy-done.2) | data formatting | bytes 7077888 | tf_op jit(solution)/shard_map/reshape | solution.py:25
  314.1 8.0 %copy.129 = bf16[3,3,128,1536]{3,2,1,0:T(8,128)(2,1)} copy(bf16[3,3,128,1536]{2,1,0,3:T(4,128)(2,1)} %reshape.146) | data formatting | bytes 7077888 | tf_op jit(solution)/shard_map/reshape | solution.py:25
  322.1 2.2 pad_maximum_fusion.4
  324.3 2.0 collective-permute-start.6
  326.3 4.5 collective-permute-start.7
  330.8 80.2 %collective-permute-done.6 = bf16[5,1,128,1536]{3,2,1,0:T(8,128)(2,1)S(1)} collective-permute-done((bf16[5,1,128,1536]{3,2,1,0:T(8,128)(2,1)S(1)}, bf16[5,1,128,1536]{3,2,1,0:T(8,128)(2,1)S(1)}, u32[]{:S(2)}, u32[]{:S(2)}) %collective-permute-start.6) | collective-permute-done | bytes 1966112 | tf_op jit(solution)/shard_map/ppermute | solution.py:15
  411.0 2.9 collective-permute-done.7
  413.9 6.6 %pad_maximum_fusion.1 = bf16[5,5,128,1536]{3,2,1,0:T(8,128)(2,1)} fusion(bf16[5,1,128,1536]{3,2,1,0:T(8,128)(2,1)S(1)} %collective-permute-done.7, bf16[1,3,128,1536]{3,2,1,0:T(8,128)(2,1)S(1)} %collective-permute-done.5, bf16[3,3,128,1536]{3,2,1,0:T(8,128)(2,1)S(1)} %copy-done.1, bf16[1,3,128,1536]{3,2,1,0:T(8,128)(2,1)} %collective-permute-done.4, ...), kind=kLoop, calls=%fused_computation.3 | loop fusion | flops 19660800 | bytes 19660800 | tf_op jit(solution)/shard_map/concatenate | solution.py:19
  420.6 13.1 %gather_fusion.1 = bf16[54,128,1536]{2,1,0:T(8,128)(2,1)} fusion(bf16[25,128,1536]{2,1,0:T(8,128)(2,1)} %bitcast.61, s32[1024]{0:T(1024)S(1)} %pad_clamp_fusion), kind=kCustom, calls=%fused_computation.1 | custom fusion | bytes 42467544 | tf_op jit(solution)/shard_map/gather | solution.py:33
  433.6 11.8 %fusion.2 = bf16[9,128,1536]{1,2,0:T(8,128)(2,1)} fusion(bf16[9,6,128,1536]{3,2,1,0:T(8,128)(2,1)} %bitcast.65, bf16[9,6,128,128]{3,2,1,0:T(8,128)(2,1)S(1)} %copy-done), kind=kOutput, calls=%fused_computation.14 | convolution fusion | flops 2719678464 | bytes 26542080 | tf_op jit(solution)/shard_map/bkij,bkjf->bif/dot_general | solution.py:34
  445.4 5.8 %copy.115 = bf16[9,128,1536]{2,1,0:T(8,128)(2,1)} copy(bf16[9,128,1536]{1,2,0:T(8,128)(2,1)} %fusion.2) | data formatting | bytes 7077888 | tf_op jit(solution)/shard_map/convert_element_type | solution.py:110
  451.2 7.4 %convert_element_type.112 = bf16[1152,12,128]{2,1,0:T(8,128)(2,1)} reshape(bf16[9,128,1536]{2,1,0:T(8,128)(2,1)} %copy.115) | data formatting | bytes 7077888 | tf_op jit(solution)/shard_map/convert_element_type | solution.py:110
  458.6 8.4 %add_convert_fusion = bf16[1152,12,128]{0,2,1:T(8,128)(2,1)} fusion(bf16[1152,12,128]{0,2,1:T(8,128)(2,1)} %copy-done.2, bf16[1152,12,128]{2,1,0:T(8,128)(2,1)} %convert_element_type.112, bf16[128,128]{1,0:T(8,128)(2,1)S(1)} %copy-done.12), kind=kOutput, calls=%fused_computation.9 | convolution fusion | flops 465371136 | bytes 10649600 | tf_op jit(solution)/shard_map/dot_general | solution.py:111
  467.0 5.8 %copy.119 = bf16[1152,12,128]{2,0,1:T(8,128)(2,1)} copy(bf16[1152,12,128]{0,2,1:T(8,128)(2,1)} %add_convert_fusion) | data formatting | bytes 7077888 | tf_op jit(solution)/shard_map/convert_element_type | solution.py:114
  (42 shorter events, 0.5 us)
Async XLA Ops:
  0.0 154.7 %copy-start = (bf16[9,6,128,128]{3,2,1,0:T(8,128)(2,1)S(1)}, bf16[9,6,128,128]{3,2,1,0:T(8,128)(2,1)}, u32[]{:S(2)}) copy-start(bf16[9,6,128,128]{3,2,1,0:T(8,128)(2,1)} %param.12) | copy-start | bytes 5308420
  5.4 29.6 %collective-permute-start = (bf16[1,3,128,1536]{3,2,1,0:T(8,128)(2,1)}, bf16[1,3,128,1536]{3,2,1,0:T(8,128)(2,1)}, u32[]{:S(2)}, u32[]{:S(2)}) collective-permute-start(bf16[1,3,128,1536]{3,2,1,0:T(8,128)(2,1)} %slice.46), channel_id=1, source_target_pairs={{0,8},{8,16},{16,24},{1,9},{9,17},{17,25},{2,10},{10,18},{18,26},{... | collective-permute-start | bytes 3538952 | tf_op jit(solution)/shard_map/ppermute | solution.py:15
  12.9 25.8 %collective-permute-start.1 = (bf16[1,3,128,1536]{3,2,1,0:T(8,128)(2,1)}, bf16[1,3,128,1536]{3,2,1,0:T(8,128)(2,1)S(1)}, u32[]{:S(2)}, u32[]{:S(2)}) collective-permute-start(bf16[1,3,128,1536]{3,2,1,0:T(8,128)(2,1)} %slice.48), channel_id=1, source_target_pairs={{8,0},{16,8},{24,16},{9,1},{17,9},{25,17},{10,2},{18,10},{26,18},{... | collective-permute-start | bytes 3538952 | tf_op jit(solution)/shard_map/ppermute | solution.py:18
  38.8 3.7 copy-start.3
  42.5 87.8 %collective-permute-start.2 = (bf16[5,1,128,1536]{3,2,1,0:T(8,128)(2,1)}, bf16[5,1,128,1536]{3,2,1,0:T(8,128)(2,1)}, u32[]{:S(2)}, u32[]{:S(2)}) collective-permute-start(bf16[5,1,128,1536]{3,2,1,0:T(8,128)(2,1)} %get-tuple-element.7), channel_id=1, source_target_pairs={{0,1},{1,2},{2,3},{3,4},{4,5},{5,6},{6,7},{8,9},{9,10},{10,11},{11... | collective-permute-start | bytes 5898248 | tf_op jit(solution)/shard_map/ppermute | solution.py:15
  45.6 9.0 %copy-start.8 = (s32[9,6]{0,1:T(8,128)S(1)}, s32[9,6]{0,1:T(8,128)}, u32[]{:S(2)}) copy-start(s32[9,6]{0,1:T(8,128)} %param.13) | copy-start | bytes 652
  45.6 9.2 %copy-start.6 = (s32[144,1]{0,1:T(1,128)S(1)}, s32[144,1]{0,1:T(1,128)}, u32[]{:S(2)}) copy-start(s32[144,1]{0,1:T(1,128)} %param.18) | copy-start | bytes 1732
  45.6 86.5 %collective-permute-start.3 = (bf16[5,1,128,1536]{3,2,1,0:T(8,128)(2,1)}, bf16[5,1,128,1536]{3,2,1,0:T(8,128)(2,1)}, u32[]{:S(2)}, u32[]{:S(2)}) collective-permute-start(bf16[5,1,128,1536]{3,2,1,0:T(8,128)(2,1)} %get-tuple-element.8), channel_id=1, source_target_pairs={{1,0},{2,1},{3,2},{4,3},{5,4},{6,5},{7,6},{9,8},{10,9},{11,10},{12... | collective-permute-start | bytes 5898248 | tf_op jit(solution)/shard_map/ppermute | solution.py:18
  184.2 5.6 %copy-start.9 = (f32[128]{0:T(128)S(1)}, f32[128]{0:T(128)}, u32[]{:S(2)}) copy-start(f32[128]{0:T(128)} %param.14) | copy-start | bytes 1540
  189.8 7.4 %copy-start.4 = (bf16[1152,12,128]{0,2,1:T(8,128)(2,1)S(1)}, bf16[1152,12,128]{0,2,1:T(8,128)(2,1)}, u32[]{:S(2)}) copy-start(bf16[1152,12,128]{0,2,1:T(8,128)(2,1)} %copy.94) | copy-start | bytes 10616836
  189.8 7.4 %copy-start.10 = (bf16[128,128]{1,0:T(8,128)(2,1)S(1)}, bf16[128,128]{1,0:T(8,128)(2,1)}, u32[]{:S(2)}) copy-start(bf16[128,128]{1,0:T(8,128)(2,1)} %param.15) | copy-start | bytes 98308
  197.3 4.7 copy-start.7
  197.3 4.7 copy-start.13
  202.0 40.0 %copy-start.11 = (bf16[128,128]{1,0:T(8,128)(2,1)S(1)}, bf16[128,128]{1,0:T(8,128)(2,1)}, u32[]{:S(2)}) copy-start(bf16[128,128]{1,0:T(8,128)(2,1)} %param.19) | copy-start | bytes 98308
  242.0 0.8 copy-start.5
  285.5 1.8 copy-start.2
  294.7 27.4 %collective-permute-start.4 = (bf16[1,3,128,1536]{3,2,1,0:T(8,128)(2,1)}, bf16[1,3,128,1536]{3,2,1,0:T(8,128)(2,1)}, u32[]{:S(2)}, u32[]{:S(2)}) collective-permute-start(bf16[1,3,128,1536]{3,2,1,0:T(8,128)(2,1)} %copy.128), channel_id=1, source_target_pairs={{0,8},{8,16},{16,24},{1,9},{9,17},{17,25},{2,10},{10,18},{18,26},{... | collective-permute-start | bytes 3538952 | tf_op jit(solution)/shard_map/ppermute | solution.py:15
  302.6 19.5 %collective-permute-start.5 = (bf16[1,3,128,1536]{3,2,1,0:T(8,128)(2,1)}, bf16[1,3,128,1536]{3,2,1,0:T(8,128)(2,1)S(1)}, u32[]{:S(2)}, u32[]{:S(2)}) collective-permute-start(bf16[1,3,128,1536]{3,2,1,0:T(8,128)(2,1)} %copy.130), channel_id=1, source_target_pairs={{8,0},{16,8},{24,16},{9,1},{17,9},{25,17},{10,2},{18,10},{26,18},{... | collective-permute-start | bytes 3538952 | tf_op jit(solution)/shard_map/ppermute | solution.py:18
  322.1 91.8 %copy-start.1 = (bf16[3,3,128,1536]{3,2,1,0:T(8,128)(2,1)S(1)}, bf16[3,3,128,1536]{3,2,1,0:T(8,128)(2,1)}, u32[]{:S(2)}) copy-start(bf16[3,3,128,1536]{3,2,1,0:T(8,128)(2,1)} %copy.129) | copy-start | bytes 10616836
  324.3 86.7 %collective-permute-start.6 = (bf16[5,1,128,1536]{3,2,1,0:T(8,128)(2,1)S(1)}, bf16[5,1,128,1536]{3,2,1,0:T(8,128)(2,1)S(1)}, u32[]{:S(2)}, u32[]{:S(2)}) collective-permute-start(bf16[5,1,128,1536]{3,2,1,0:T(8,128)(2,1)S(1)} %get-tuple-element.5), channel_id=1, source_target_pairs={{0,1},{1,2},{2,3},{3,4},{4,5},{5,6},{6,7},{8,9},{9,10},{10,11},{11... | collective-permute-start | bytes 5898248 | tf_op jit(solution)/shard_map/ppermute | solution.py:15
  326.3 87.6 %collective-permute-start.7 = (bf16[5,1,128,1536]{3,2,1,0:T(8,128)(2,1)S(1)}, bf16[5,1,128,1536]{3,2,1,0:T(8,128)(2,1)S(1)}, u32[]{:S(2)}, u32[]{:S(2)}) collective-permute-start(bf16[5,1,128,1536]{3,2,1,0:T(8,128)(2,1)S(1)} %get-tuple-element.6), channel_id=1, source_target_pairs={{1,0},{2,1},{3,2},{4,3},{5,4},{6,5},{7,6},{9,8},{10,9},{11,10},{12... | collective-permute-start | bytes 5898248 | tf_op jit(solution)/shard_map/ppermute | solution.py:18
  451.2 7.4 %copy-start.12 = (bf16[128,128]{1,0:T(8,128)(2,1)S(1)}, bf16[128,128]{1,0:T(8,128)(2,1)}, u32[]{:S(2)}) copy-start(bf16[128,128]{1,0:T(8,128)(2,1)} %param.21) | copy-start | bytes 98308
where the time goes:
time: 483 us; the launch traced here: 473 us
  waiting for transfers between devices  160 us (33%)
  local copies, waits for them, and re-layouts  139 us (29%)
  blocking collectives  66.3 us (14%)
  matrix products  47.2 us (10%)
  other arithmetic  36.8 us (8%)
  starting transfers between devices  23.8 us (5%)
    ppermute x4, waiting for transfers between devices, with_halo(): lax.ppermute(lax.slice_in_dim(block, block.shape[dim] - width, None, axis...  155 us
    all_to_all x1, blocking collectives, on_device(): lax.all_to_all(outgoing, ('rx', 'ry'), split_axis=0, concat_axis=0, tiled...  33.8 us
    all_to_all x1, blocking collectives, on_device(): lax.all_to_all((arrived.astype(jnp.float32) + lifted.astype(jnp.float32)...  32.5 us
    gather x2, local copies, waits for them, and re-layouts, diffuse(): gathered = flat_blocks[block_index]  26.1 us
    unnamed x32, local copies, waits for them, and re-layouts  25.4 us
    dot_general x2, matrix products, diffuse(): jnp.einsum('bkij,bkjf->bif', adjacency, gathered, preferred_element_type=...  24.2 us
    reshape x3, local copies, waits for them, and re-layouts, diffuse(): grid_blocks = values_in.reshape(GB, GB, BLK, features)  23.9 us
    convert_element_type x2, local copies, waits for them, and re-layouts, on_device(): scaled = diffused.astype(jnp.float32)  17.1 us
  transfers between devices with their start and end apart: 8, of which 4 were waited for; matrix products, arithmetic and copies ran while one was open for 12% of the time, Pallas kernels for 0%

commit v1 on v0

v1 whole, which is shorter than its diff:
```python
import functools
import jax
import jax.numpy as jnp
from jax import lax
from jax.experimental import pallas as pl
from jax.experimental.pallas import tpu as pltpu
from jax.sharding import PartitionSpec as P

GB = 3
BLK = 128
SIDE = GB + 2
CHUNKS = 2
LANES_STEPS = 2


def silu(v):
    return v / (1.0 + jnp.exp(-v))


def dot32(a, b):
    return jnp.dot(a, b, preferred_element_type=jnp.float32)


def extended_sources(own, rx_lo, rx_hi, ry_lo, ry_hi, co_lo, co_hi):
    sources = []
    for r in range(SIDE):
        for c in range(SIDE):
            if r in (0, SIDE - 1):
                row, corner = (rx_lo, co_lo) if r == 0 else (rx_hi, co_hi)
                if c in (0, SIDE - 1):
                    sources.append((corner, 0 if c == 0 else 1))
                else:
                    sources.append((row, c - 1))
            elif c in (0, SIDE - 1):
                sources.append((ry_lo if c == 0 else ry_hi, r - 1))
            else:
                sources.append((own, (r - 1) * GB + c - 1))
    return sources


def diffuse_block(b, index, adjacency, ext):
    lhs = jnp.concatenate([adjacency[b, n] for n in range(adjacency.shape[1])], axis=1)
    rhs = jnp.concatenate(
        [ext[index[b * adjacency.shape[1] + n]] for n in range(adjacency.shape[1])], axis=0
    )
    return dot32(lhs, rhs)


def encode_kernel(
    index,
    own,
    rx_lo,
    rx_hi,
    ry_lo,
    ry_hi,
    co_lo,
    co_hi,
    adjacency,
    gain,
    w_mix,
    weight_row,
    cluster_row,
    cluster_col,
    owner_row,
    w_coarse,
    u_ref,
    partial_ref,
    ext,
    enc,
):
    steps = own.shape[0]
    coarse = owner_row.shape[1]
    nodes = cluster_row.shape[1]
    devices = partial_ref.shape[1]
    for p, (ref, k) in enumerate(
        extended_sources(own, rx_lo, rx_hi, ry_lo, ry_hi, co_lo, co_hi)
    ):
        for t in range(steps):
            ext[p, :, t * BLK : (t + 1) * BLK] = ref[t, k]
    pooled = jnp.zeros((coarse, steps * BLK), jnp.float32)
    for b in range(GB * GB):
        summed = diffuse_block(b, index, adjacency, ext)
        for t in range(steps):
            scaled = summed[:, t * BLK : (t + 1) * BLK].astype(jnp.bfloat16).astype(jnp.float32)
            mean_square = jnp.mean(scaled * scaled, axis=-1, keepdims=True)
            normed = (scaled * lax.rsqrt(mean_square + 1e-06) * gain[...]).astype(jnp.bfloat16)
            mixed = dot32(normed, w_mix[...])
            enc[b, :, t * BLK : (t + 1) * BLK] = (
                own[t, b].astype(jnp.float32) + silu(mixed)
            ).astype(jnp.bfloat16)
        lanes = slice(b * BLK, (b + 1) * BLK)
        rows = lax.broadcasted_iota(jnp.int32, (coarse, BLK), 0)
        pooling = jnp.where(
            rows == cluster_row[:, lanes], weight_row[:, lanes], 0.0
        ).astype(jnp.bfloat16)
        pooled = pooled + dot32(pooling, enc[b])
    pooled = pooled.astype(jnp.bfloat16)
    owner_hot = (
        lax.broadcasted_iota(jnp.int32, (devices, coarse), 0) == owner_row[...]
    ).astype(jnp.float32).astype(jnp.bfloat16)
    bases = []
    for t in range(steps):
        piece = pooled[:, t * BLK : (t + 1) * BLK]
        lifted = silu(dot32(piece, w_coarse[...])).astype(jnp.bfloat16)
        partial_ref[t] = dot32(owner_hot, lifted)
        bases.append((piece.astype(jnp.float32) + lifted.astype(jnp.float32)).astype(jnp.bfloat16))
    base = jnp.concatenate(bases, axis=1)
    for b in range(GB * GB):
        hot = (
            lax.broadcasted_iota(jnp.int32, (BLK, coarse), 1)
            == cluster_col[b * BLK : (b + 1) * BLK, :]
        ).astype(jnp.float32).astype(jnp.bfloat16)
        u = (enc[b].astype(jnp.float32) + dot32(hot, base)).astype(jnp.bfloat16)
        for t in range(steps):
            u_ref[t, b] = u[:, t * BLK : (t + 1) * BLK]


def decode_kernel(
    denominator,
    index,
    own,
    rx_lo,
    rx_hi,
    ry_lo,
    ry_hi,
    co_lo,
    co_hi,
    adjacency,
    region_sum,
    owner_ext,
    w_region,
    w_out,
    *rest,
):
    out_ref, ext = rest[-2:]
    steps = own.shape[0]
    devices = region_sum.shape[1]
    reaches = []
    for t in range(steps):
        region = (region_sum[t] / denominator).astype(jnp.bfloat16)
        reaches.append(dot32(region, w_region[...]).astype(jnp.bfloat16))
    reach = jnp.concatenate(reaches, axis=1)
    for p, (ref, k) in enumerate(
        extended_sources(own, rx_lo, rx_hi, ry_lo, ry_hi, co_lo, co_hi)
    ):
        hot = (
            lax.broadcasted_iota(jnp.int32, (BLK, devices), 1)
            == owner_ext[p * BLK : (p + 1) * BLK, :]
        ).astype(jnp.float32).astype(jnp.bfloat16)
        added = dot32(hot, reach)
        for t in range(steps):
            lanes = slice(t * BLK, (t + 1) * BLK)
            ext[p, :, lanes] = (ref[t, k].astype(jnp.float32) + added[:, lanes]).astype(
                jnp.bfloat16
            )
    for b in range(GB * GB):
        second = diffuse_block(b, index, adjacency, ext).astype(jnp.bfloat16)
        centre = (b // GB + 1) * SIDE + b % GB + 1
        for t in range(steps):
            lanes = slice(t * BLK, (t + 1) * BLK)
            mixed = dot32(second[:, lanes], w_out[...])
            out_ref[t, b] = (ext[centre, :, lanes].astype(jnp.float32) + silu(mixed)).astype(
                jnp.bfloat16
            )


def stepped(array, per, offset=0):
    tail = array.shape[1:]
    zeros = (0,) * len(tail)
    return pl.BlockSpec((per,) + tail, lambda i, _: (i + offset,) + zeros)


def whole(array):
    zeros = (0,) * array.ndim
    return pl.BlockSpec(array.shape, lambda i, _: zeros)


def halo(field):
    steps = field.shape[0]
    square = field.reshape(steps, GB, GB, BLK, BLK)

    def shifted(value, axis, up):
        count = lax.axis_size(axis)
        pairs = [(i, i + 1) if up else (i + 1, i) for i in range(count - 1)]
        return lax.ppermute(value, axis, pairs)

    ry_lo = shifted(square[:, :, GB - 1], "ry", True)
    ry_hi = shifted(square[:, :, 0], "ry", False)
    rx_lo = shifted(square[:, GB - 1], "rx", True)
    rx_hi = shifted(square[:, 0], "rx", False)
    co_lo = shifted(jnp.stack([ry_lo[:, GB - 1], ry_hi[:, GB - 1]], axis=1), "rx", True)
    co_hi = shifted(jnp.stack([ry_lo[:, 0], ry_hi[:, 0]], axis=1), "rx", False)
    return rx_lo, rx_hi, ry_lo, ry_hi, co_lo, co_hi


def on_device(
    noisy_input,
    adjacency,
    neighbours,
    norm_gain,
    w_mix,
    pool_weight,
    cluster,
    owner_ids,
    w_coarse,
    w_region,
    w_out,
):
    node_rows, steps_count, channels = noisy_input.shape
    coarse = owner_ids.shape[0]
    row_devices = lax.axis_size("rx")
    col_devices = lax.axis_size("ry")
    devices = row_devices * col_devices
    blocks = GB * GB
    noisy = noisy_input.transpose(1, 0, 2).reshape(steps_count, blocks, BLK, channels)
    positions = jnp.arange(blocks, dtype=jnp.int32)
    index = (
        (positions // GB)[:, None] + neighbours // 3
    ) * SIDE + (positions % GB)[:, None] + neighbours % 3
    index = index.reshape(-1)

    targets = owner_ids[:, 0]
    owner_of = jnp.sum(
        jnp.where(
            cluster[:, None] == jnp.arange(coarse, dtype=jnp.int32)[None, :], targets[None, :], 0
        ),
        axis=1,
    )
    everyone = lax.all_gather(owner_of.reshape(blocks, BLK), ("rx", "ry"), axis=0, tiled=True)
    ext_rows = jnp.arange(SIDE * SIDE, dtype=jnp.int32)
    grid_row = lax.axis_index("rx") * GB + ext_rows // SIDE - 1
    grid_col = lax.axis_index("ry") * GB + ext_rows % SIDE - 1
    inside = (
        (grid_row >= 0)
        & (grid_row < row_devices * GB)
        & (grid_col >= 0)
        & (grid_col < col_devices * GB)
    )
    grid_row = jnp.clip(grid_row, 0, row_devices * GB - 1)
    grid_col = jnp.clip(grid_col, 0, col_devices * GB - 1)
    place = (
        (grid_row // GB * col_devices + grid_col // GB) * blocks
        + grid_row % GB * GB
        + grid_col % GB
    )
    owner_ext = jnp.where(inside[:, None], everyone[place], -1).reshape(SIDE * SIDE * BLK, 1)

    chunk = steps_count // CHUNKS
    per = LANES_STEPS
    grid = chunk // per
    gain = norm_gain.reshape(1, channels)
    weight_row = pool_weight.astype(jnp.float32).reshape(1, node_rows)
    cluster_row = cluster.reshape(1, node_rows)
    cluster_col = cluster.reshape(node_rows, 1)
    owner_row = targets.reshape(1, coarse)
    ext_scratch = pltpu.VMEM((SIDE * SIDE, BLK, per * BLK), jnp.bfloat16)
    params = pltpu.CompilerParams(vmem_limit_bytes=48 * 1024 * 1024)
    cost = pl.CostEstimate(flops=5_000_000_000 // CHUNKS, bytes_accessed=16_000_000 // CHUNKS, transcendentals=0)

    first = [halo(noisy[c * chunk : (c + 1) * chunk]) for c in range(CHUNKS)]
    fields, sums, second = [], [], []
    for c in range(CHUNKS):
        constants = (
            adjacency, gain, w_mix, weight_row, cluster_row, cluster_col, owner_row, w_coarse,
        )
        u, partial = pl.pallas_call(
            encode_kernel,
            grid_spec=pltpu.PrefetchScalarGridSpec(
                num_scalar_prefetch=1,
                grid=(grid,),
                in_specs=[stepped(noisy, per, c * grid)]
                + [stepped(part, per) for part in first[c]]
                + [whole(part) for part in constants],
                out_specs=[
                    pl.BlockSpec((per, blocks, BLK, channels), lambda i, _: (i, 0, 0, 0)),
                    pl.BlockSpec((per, devices, channels), lambda i, _: (i, 0, 0)),
                ],
                scratch_shapes=[
                    ext_scratch,
                    pltpu.VMEM((blocks, BLK, per * BLK), jnp.bfloat16),
                ],
            ),
            out_shape=[
                jax.ShapeDtypeStruct((chunk, blocks, BLK, channels), jnp.bfloat16),
                jax.ShapeDtypeStruct((chunk, devices, channels), jnp.float32),
            ],
            compiler_params=params,
            cost_estimate=cost,
            name="encode",
        )(index, noisy, *first[c], *constants)
        fields.append(u)
        sums.append(partial)
        second.append(halo(u))
    region_sum = lax.psum(jnp.concatenate(sums, axis=0), ("rx", "ry"))

    out = None
    for c in range(CHUNKS):
        shared = (owner_ext, w_region, w_out)
        extra = () if out is None else (out,)
        operands = (index, fields[c], *second[c], adjacency, region_sum, *shared, *extra)
        out = pl.pallas_call(
            functools.partial(decode_kernel, float(coarse)),
            grid_spec=pltpu.PrefetchScalarGridSpec(
                num_scalar_prefetch=1,
                grid=(grid,),
                in_specs=[stepped(fields[c], per)]
                + [stepped(part, per) for part in second[c]]
                + [whole(adjacency), stepped(region_sum, per, c * grid)]
                + [whole(part) for part in shared]
                + [pl.BlockSpec(memory_space=pl.ANY)] * len(extra),
                out_specs=pl.BlockSpec(
                    (per, blocks, BLK, channels), lambda i, _, c=c: (i + c * grid, 0, 0, 0)
                ),
                scratch_shapes=[ext_scratch],
            ),
            out_shape=jax.ShapeDtypeStruct((steps_count, blocks, BLK, channels), jnp.bfloat16),
            input_output_aliases={len(operands) - 1: 0} if extra else {},
            compiler_params=params,
            cost_estimate=cost,
            name="decode",
        )(*operands)
    return out.reshape(steps_count, node_rows, channels).transpose(1, 0, 2)


def solution(mesh):
    in_specs = (
        P(("rx", "ry"), None, None),
        P(("rx", "ry"), None, None, None),
        P(("rx", "ry"), None),
        P(),
        P(),
        P(("rx", "ry")),
        P(("rx", "ry")),
        P(("rx", "ry"), None),
        P(),
        P(),
        P(),
    )
    out_specs = P(("rx", "ry"), None, None)
    return jax.shard_map(
        on_device, mesh=mesh, in_specs=in_specs, out_specs=out_specs, check_vma=False
    )
```

time: 483 us -> 339 us (0.70); the launches traced: 473 us -> 336 us
  local copies, waits for them, and re-layouts: 139 us -> 18.4 us
  waiting for transfers between devices: 160 us -> 91.8 us
  Pallas kernels: 0 us -> 54.4 us
  starting transfers between devices: 23.8 us -> 77.5 us
  matrix products: 47.2 us -> 0 us
  other arithmetic: 36.8 us -> 3.7 us
  between operations: 0.78 us -> 14.2 us
  blocking collectives: 66.3 us -> 75.9 us
    ppermute x8 -> x24, waiting for transfers between devices: 160 us -> 18.5 us  [shifted(): return lax.ppermute(value, axis, pairs)]
    all_gather x0 -> x1, blocking collectives: none -> 75.9 us  [on_device(): lax.all_gather(owner_of.reshape(blocks, BLK), ('rx', 'ry'), axis=0, tiled...]
    psum x0 -> x1, waiting for transfers between devices: none -> 73.3 us  [on_device(): region_sum = lax.psum(jnp.concatenate(sums, axis=0), ('rx', 'ry'))]
    all_to_all x2 -> x0, blocking collectives: 66.3 us -> none  [the longest x1 33.8 us: on_device(): lax.all_to_all(outgoing, ('rx', 'ry'), split_axis=0, concat_axis=0, tiled...]
    pallas_call x0 -> x4, Pallas kernels: none -> 54.4 us  [the longest x2 28.2 us: on_device(): pl.pallas_call(encode_kernel, grid_spec=pltpu.PrefetchScalarGridSpec(num_...]
    ppermute x8 -> x24, starting transfers between devices: 23.8 us -> 77.5 us  [shifted(): return lax.ppermute(value, axis, pairs)]
    dot_general x8 -> x0, matrix products: 47.2 us -> none  [the longest x2 24.2 us: diffuse(): jnp.einsum('bkij,bkjf->bif', adjacency, gathered, preferred_element_type=...]
    convert_element_type x6 -> x0, local copies, waits for them, and re-layouts: 36.4 us -> none  [the longest x2 17.1 us: on_device(): scaled = diffused.astype(jnp.float32)]
  transfers between devices with their start and end apart: 8 -> 25, of which waited for: 4 -> 4; matrix products, arithmetic and copies ran while one was open for 12% -> 4% of each run, Pallas kernels for 0% -> 12%
where the time goes in v1:
time: 339 us; the launch traced here: 336 us
  waiting for transfers between devices  91.8 us (27%)
  starting transfers between devices  77.5 us (23%)
  blocking collectives  75.9 us (22%)
  Pallas kernels  54.4 us (16%)
  local copies, waits for them, and re-layouts  18.4 us (5%)
  between operations  14.2 us (4%)
  other arithmetic  3.7 us (1%)
    ppermute x24, starting transfers between devices, shifted(): return lax.ppermute(value, axis, pairs)  77.5 us
    all_gather x1, blocking collectives, on_device(): lax.all_gather(owner_of.reshape(blocks, BLK), ('rx', 'ry'), axis=0, tiled...  75.9 us
    psum x1, waiting for transfers between devices, on_device(): region_sum = lax.psum(jnp.concatenate(sums, axis=0), ('rx', 'ry'))  73.3 us
    pallas_call x2, Pallas kernels, on_device(): pl.pallas_call(encode_kernel, grid_spec=pltpu.PrefetchScalarGridSpec(num_...  28.2 us
    pallas_call x2, Pallas kernels, on_device(): pl.pallas_call(functools.partial(decode_kernel, float(coarse)), grid_spec...  26.2 us
    ppermute x24, waiting for transfers between devices, shifted(): return lax.ppermute(value, axis, pairs)  18.5 us
  transfers between devices with their start and end apart: 25, of which 4 were waited for; matrix products, arithmetic and copies ran while one was open for 4% of the time, Pallas kernels for 12%

profile of v1, /device:TPU:9, one launch (start us, length us, event | category | flops | bytes accessed | tf_op | source)
XLA Modules:
  0.0 335.9 jit_solution(12256873176109868408)
XLA Ops:
  6.5 2.2 fusion.19
  8.8 0.0 copy-start.26
  8.8 1.2 slice_bitcast_fusion.4
  10.0 3.1 collective-permute-start.14
  13.2 3.0 collective-permute-start.15
  16.2 1.2 slice_bitcast_fusion.6
  17.4 4.4 %collective-permute-start.12 = (bf16[6,3,128,128]{3,2,1,0:T(8,128)(2,1)}, bf16[6,3,128,128]{3,2,1,0:T(8,128)(2,1)S(1)}, u32[]{:S(2)}, u32[]{:S(2)}) collective-permute-start(bf16[6,3,128,128]{3,2,1,0:T(8,128)(2,1)} %get-tuple-element.22), channel_id=1, source_target_pairs={{0,8},{8,16},{16,24},{1,9},{9,17},{17,25},{2,10},{10,18},{18,26},{... | collective-permute-start | bytes 1769480 | tf_op jit(solution)/shard_map/ppermute | solution.py:185
  21.8 1.9 collective-permute-start.13
  23.7 1.1 slice_bitcast_fusion.12
  24.9 2.2 collective-permute-start.2
  27.1 0.2 reshape.283.cluster_col
  27.4 0.1 copy.64
  27.5 0.1 reshape.257.index
  27.6 0.2 select_reduce_fusion
  27.8 75.9 %all-gather = s32[32,9,128]{2,1,0:T(8,128)S(1)} all-gather(s32[1,9,128]{2,1,0:T(8,128)S(1)} %bitcast.106), channel_id=1, replica_groups=mesh['rx'=4,'ry'=8] {'rx','ry'}, dimensions={0}, use_global_device_ids=true | all-gather | bytes 152064 | tf_op jit(solution)/shard_map/all_gather | solution.py:229
  103.7 0.6 gather_fusion
  104.3 1.4 slice_bitcast_fusion.14
  105.8 5.4 %collective-permute-start.3 = (bf16[6,3,128,128]{3,2,1,0:T(8,128)(2,1)S(1)}, bf16[6,3,128,128]{3,2,1,0:T(8,128)(2,1)S(1)}, u32[]{:S(2)}, u32[]{:S(2)}) collective-permute-start(bf16[6,3,128,128]{3,2,1,0:T(8,128)(2,1)S(1)} %copy-done.27), channel_id=1, source_target_pairs={{1,0},{2,1},{3,2},{4,3},{5,4},{6,5},{7,6},{9,8},{10,9},{11,10},{12... | collective-permute-start | bytes 1769480 | tf_op jit(solution)/shard_map/ppermute | solution.py:185
  111.2 9.0 %collective-permute-start = (bf16[6,3,128,128]{3,2,1,0:T(8,128)(2,1)S(1)}, bf16[6,3,128,128]{3,2,1,0:T(8,128)(2,1)S(1)}, u32[]{:S(2)}, u32[]{:S(2)}) collective-permute-start(bf16[6,3,128,128]{3,2,1,0:T(8,128)(2,1)S(1)} %get-tuple-element.30), channel_id=1, source_target_pairs={{0,8},{8,16},{16,24},{1,9},{9,17},{17,25},{2,10},{10,18},{18,26},{... | collective-permute-start | bytes 1769480 | tf_op jit(solution)/shard_map/ppermute | solution.py:185
  120.3 0.0 copy-start.18
  120.3 1.9 collective-permute-start.16
  122.3 0.0 copy-start.25
  122.4 5.0 %collective-permute-start.17 = (bf16[6,2,128,128]{3,2,1,0:T(8,128)(2,1)S(1)}, bf16[6,2,128,128]{3,2,1,0:T(8,128)(2,1)S(1)}, u32[]{:S(2)}, u32[]{:S(2)}) collective-permute-start(bf16[6,2,128,128]{3,2,1,0:T(8,128)(2,1)S(1)} %pad_maximum_fusion.5), channel_id=1, source_target_pairs={{8,0},{16,8},{24,16},{9,1},{17,9},{25,17},{10,2},{18,10},{26,18},{... | collective-permute-start | bytes 1179656 | tf_op jit(solution)/shard_map/ppermute | solution.py:185
  127.6 1.9 collective-permute-start.1
  129.5 1.9 collective-permute-start.5
  131.5 4.2 %collective-permute-start.4 = (bf16[6,2,128,128]{3,2,1,0:T(8,128)(2,1)S(1)}, bf16[6,2,128,128]{3,2,1,0:T(8,128)(2,1)S(1)}, u32[]{:S(2)}, u32[]{:S(2)}) collective-permute-start(bf16[6,2,128,128]{3,2,1,0:T(8,128)(2,1)S(1)} %pad_maximum_fusion), channel_id=1, source_target_pairs={{0,8},{8,16},{16,24},{1,9},{9,17},{17,25},{2,10},{10,18},{18,26},{... | collective-permute-start | bytes 1179656 | tf_op jit(solution)/shard_map/ppermute | solution.py:185
  135.7 14.2 %encode.3 = (bf16[6,9,128,128]{3,2,1,0:T(8,128)(2,1)S(1)}, f32[6,32,128]{2,1,0:T(8,128)S(1)}) custom-call(s32[54]{0:T(128)S(1)} %reshape.257.index, bf16[12,9,128,128]{3,2,1,0:T(8,128)(2,1)} %bitcast.103, bf16[6,3,128,128]{3,2,1,0:T(8,128)(2,1)S(1)} %collective-permute-done.12.rx_lo, bf16[6,3,128,128]{3,2,1,0:T(8,128)(2,1)} %collective-permute-done.13.rx_hi, ...), custom_call_target="tpu_custom_call" | custom-call | flops 2500000000 | bytes 8000000 | tf_op jit(solution)/shard_map/encode/pallas_call | solution.py:266
  149.9 1.4 slice_bitcast_fusion
  151.3 2.0 collective-permute-start.20
  153.3 1.1 slice_bitcast_fusion.2
  154.5 4.5 %collective-permute-start.21 = (bf16[6,3,128,128]{3,2,1,0:T(8,128)(2,1)}, bf16[6,3,128,128]{3,2,1,0:T(8,128)(2,1)S(1)}, u32[]{:S(2)}, u32[]{:S(2)}) collective-permute-start(bf16[6,3,128,128]{3,2,1,0:T(8,128)(2,1)} %get-tuple-element.15), channel_id=1, source_target_pairs={{1,0},{2,1},{3,2},{4,3},{5,4},{6,5},{7,6},{9,8},{10,9},{11,10},{12... | collective-permute-start | bytes 1769480 | tf_op jit(solution)/shard_map/ppermute | solution.py:185
  159.0 14.1 %encode.2 = (bf16[6,9,128,128]{3,2,1,0:T(8,128)(2,1)S(1)}, f32[6,32,128]{2,1,0:T(8,128)S(1)}) custom-call(s32[54]{0:T(128)S(1)} %reshape.257.index, bf16[12,9,128,128]{3,2,1,0:T(8,128)(2,1)} %bitcast.104, bf16[6,3,128,128]{3,2,1,0:T(8,128)(2,1)S(1)} %collective-permute-done.rx_lo, bf16[6,3,128,128]{3,2,1,0:T(8,128)(2,1)S(1)} %collective-permute-done.1.rx_hi, ...), custom_call_target="tpu_custom_call" | custom-call | flops 2500000000 | bytes 8000000 | tf_op jit(solution)/shard_map/encode/pallas_call | solution.py:266
  173.1 0.8 pad_maximum_fusion.8
  173.9 0.0 all-reduce.2.cloned.1.call-update
  173.9 2.7 collective-permute-start.18
  176.6 1.9 collective-permute-start.19
  178.5 0.1 slice_bitcast_fusion.8
  178.7 1.9 collective-permute-start.8
  180.6 1.1 slice_bitcast_fusion.10
  181.7 4.3 %collective-permute-start.9 = (bf16[6,3,128,128]{3,2,1,0:T(8,128)(2,1)S(1)}, bf16[6,3,128,128]{3,2,1,0:T(8,128)(2,1)S(1)}, u32[]{:S(2)}, u32[]{:S(2)}) collective-permute-start(bf16[6,3,128,128]{3,2,1,0:T(8,128)(2,1)S(1)} %get-tuple-element.23), channel_id=1, source_target_pairs={{1,0},{2,1},{3,2},{4,3},{5,4},{6,5},{7,6},{9,8},{10,9},{11,10},{12... | collective-permute-start | bytes 1769480 | tf_op jit(solution)/shard_map/ppermute | solution.py:185
  186.0 4.2 %collective-permute-start.6 = (bf16[6,3,128,128]{3,2,1,0:T(8,128)(2,1)}, bf16[6,3,128,128]{3,2,1,0:T(8,128)(2,1)}, u32[]{:S(2)}, u32[]{:S(2)}) collective-permute-start(bf16[6,3,128,128]{3,2,1,0:T(8,128)(2,1)} %get-tuple-element.26), channel_id=1, source_target_pairs={{0,8},{8,16},{16,24},{1,9},{9,17},{17,25},{2,10},{10,18},{18,26},{... | collective-permute-start | bytes 1769480 | tf_op jit(solution)/shard_map/ppermute | solution.py:185
  190.3 15.7 %collective-permute-done.8.ry_lo = bf16[6,3,128,128]{3,2,1,0:T(8,128)(2,1)S(1)} collective-permute-done((bf16[6,3,128,128]{3,2,1,0:T(8,128)(2,1)S(1)}, bf16[6,3,128,128]{3,2,1,0:T(8,128)(2,1)S(1)}, u32[]{:S(2)}, u32[]{:S(2)}) %collective-permute-start.8) | collective-permute-done | bytes 589856 | tf_op jit(solution)/shard_map/ppermute | solution.py:185
  206.0 1.9 collective-permute-start.7
  208.0 1.4 collective-permute-done.9.ry_hi
  209.3 2.3 collective-permute-start.23
  211.7 0.8 pad_maximum_fusion.6
  212.5 0.0 copy-start.10
  212.5 3.4 %collective-permute-start.22 = (bf16[6,2,128,128]{3,2,1,0:T(8,128)(2,1)}, bf16[6,2,128,128]{3,2,1,0:T(8,128)(2,1)}, u32[]{:S(2)}, u32[]{:S(2)}) collective-permute-start(bf16[6,2,128,128]{3,2,1,0:T(8,128)(2,1)} %pad_maximum_fusion.6), channel_id=1, source_target_pairs={{0,8},{8,16},{16,24},{1,9},{9,17},{17,25},{2,10},{10,18},{18,26},{... | collective-permute-start | bytes 1179656 | tf_op jit(solution)/shard_map/ppermute | solution.py:185
  215.9 0.8 pad_maximum_fusion.3
  216.7 0.8 pad_maximum_fusion.2
  217.5 0.8 copy-done.12
  218.3 1.9 collective-permute-start.11
  220.2 1.4 collective-permute-done.23.co_hi
  221.6 0.8 copy-done.16
  222.4 2.4 collective-permute-start.10
  224.8 0.1 select_bitcast_fusion
  224.9 0.5 copy.102
  225.5 73.3 %all-reduce.2.cloned.1.call-done.region_sum = f32[12,32,128]{2,1,0:T(8,128)} async-done(((f32[12,32,128]{2,1,0:T(8,128)}), f32[12,32,128]{2,1,0:T(8,128)}) %all-reduce.2.cloned.1.call-update) | async-done | bytes 196624 | tf_op jit(solution)/shard_map/psum | solution.py:294
  298.8 0.9 copy-done.8
  299.7 1.1 copy-done.11
  300.8 1.1 copy-done.13
  301.9 1.0 copy-done.17
  302.9 12.8 %decode.2.rest_0_ = bf16[12,9,128,128]{3,2,1,0:T(8,128)(2,1)} custom-call(s32[54]{0:T(128)S(1)} %reshape.257.index, bf16[6,9,128,128]{3,2,1,0:T(8,128)(2,1)} %copy-done.1, bf16[6,3,128,128]{3,2,1,0:T(8,128)(2,1)S(1)} %copy-done.11, bf16[6,3,128,128]{3,2,1,0:T(8,128)(2,1)S(1)} %copy-done.13, bf16[6,3,128,128]{3,2,1,0:T(8,128)(2,1)S(1)} %copy-done.3, ...), custom_call_target="tpu_custom_call" | custom-call | flops 2500000000 | bytes 8000000 | tf_op jit(solution)/shard_map/decode/pallas_call | solution.py:301
  315.7 13.4 %decode.3 = bf16[12,9,128,128]{3,2,1,0:T(8,128)(2,1)} custom-call(s32[54]{0:T(128)S(1)} %reshape.257.index, bf16[6,9,128,128]{3,2,1,0:T(8,128)(2,1)} %copy-done, bf16[6,3,128,128]{3,2,1,0:T(8,128)(2,1)} %collective-permute-done.6.rx_lo, bf16[6,3,128,128]{3,2,1,0:T(8,128)(2,1)} %collective-permute-done.7.rx_hi, ...), custom_call_target="tpu_custom_call", output_to_operand_aliasing={{}: (13, {})} | custom-call | flops 2500000000 | bytes 8000000 | tf_op jit(solution)/shard_map/decode/pallas_call | solution.py:301
  (96 shorter events, 0.7 us)
Async XLA Ops:
  6.5 292.2 %all-reduce.2.cloned.1.call-start = ((), (), s32[]{:S(2)}) async-start(), calls=%async_computation | async-start | bytes 393216 | tf_op jit(solution)/shard_map/psum | solution.py:294
  8.8 18.3 %copy-start.26 = (bf16[6,1152,128]{2,1,0:T(8,128)(2,1)}, bf16[6,1152,128]{2,1,0:T(8,128)(2,1)S(1)}, u32[]{:S(2)}) copy-start(bf16[6,1152,128]{2,1,0:T(8,128)(2,1)S(1)} %get-tuple-element.14) | copy-start | bytes 5308420
  10.0 95.7 %collective-permute-start.14 = (bf16[6,3,128,128]{3,2,1,0:T(8,128)(2,1)}, bf16[6,3,128,128]{3,2,1,0:T(8,128)(2,1)S(1)}, u32[]{:S(2)}, u32[]{:S(2)}) collective-permute-start(bf16[6,3,128,128]{3,2,1,0:T(8,128)(2,1)} %get-tuple-element.20), channel_id=1, source_target_pairs={{0,1},{1,2},{2,3},{3,4},{4,5},{5,6},{6,7},{8,9},{9,10},{10,11},{11... | collective-permute-start | bytes 1769480 | tf_op jit(solution)/shard_map/ppermute | solution.py:185
  13.2 98.0 %collective-permute-start.15 = (bf16[6,3,128,128]{3,2,1,0:T(8,128)(2,1)}, bf16[6,3,128,128]{3,2,1,0:T(8,128)(2,1)S(1)}, u32[]{:S(2)}, u32[]{:S(2)}) collective-permute-start(bf16[6,3,128,128]{3,2,1,0:T(8,128)(2,1)} %get-tuple-element.19), channel_id=1, source_target_pairs={{1,0},{2,1},{3,2},{4,3},{5,4},{6,5},{7,6},{9,8},{10,9},{11,10},{12... | collective-permute-start | bytes 1769480 | tf_op jit(solution)/shard_map/ppermute | solution.py:185
  17.4 9.7 %copy-start.28 = (s32[1152]{0:T(1024)S(1)}, s32[1152]{0:T(1024)}, u32[]{:S(2)}) copy-start(s32[1152]{0:T(1024)} %param.17) | copy-start | bytes 13828
  17.4 10.0 %copy-start.29 = (s32[9,6]{0,1:T(8,128)S(1)}, s32[9,6]{0,1:T(8,128)}, u32[]{:S(2)}) copy-start(s32[9,6]{0,1:T(8,128)} %param.13) | copy-start | bytes 652
  17.4 10.2 %copy-start.30 = (bf16[1152]{0:T(1024)(128)(2,1)S(1)}, bf16[1152]{0:T(1024)(128)(2,1)}, u32[]{:S(2)}) copy-start(bf16[1152]{0:T(1024)(128)(2,1)} %param.16) | copy-start | bytes 6916
  17.4 10.2 %copy-start.22 = (s32[144,1]{0,1:T(1,128)S(1)}, s32[144,1]{0,1:T(1,128)}, u32[]{:S(2)}) copy-start(s32[144,1]{0,1:T(1,128)} %param.18) | copy-start | bytes 1732
  17.4 110.2 %collective-permute-start.12 = (bf16[6,3,128,128]{3,2,1,0:T(8,128)(2,1)}, bf16[6,3,128,128]{3,2,1,0:T(8,128)(2,1)S(1)}, u32[]{:S(2)}, u32[]{:S(2)}) collective-permute-start(bf16[6,3,128,128]{3,2,1,0:T(8,128)(2,1)} %get-tuple-element.22), channel_id=1, source_target_pairs={{0,8},{8,16},{16,24},{1,9},{9,17},{17,25},{2,10},{10,18},{18,26},{... | collective-permute-start | bytes 1769480 | tf_op jit(solution)/shard_map/ppermute | solution.py:185
  21.8 107.7 %collective-permute-start.13 = (bf16[6,3,128,128]{3,2,1,0:T(8,128)(2,1)}, bf16[6,3,128,128]{3,2,1,0:T(8,128)(2,1)}, u32[]{:S(2)}, u32[]{:S(2)}) collective-permute-start(bf16[6,3,128,128]{3,2,1,0:T(8,128)(2,1)} %get-tuple-element.21), channel_id=1, source_target_pairs={{8,0},{16,8},{24,16},{9,1},{17,9},{25,17},{10,2},{18,10},{26,18},{... | collective-permute-start | bytes 1769480 | tf_op jit(solution)/shard_map/ppermute | solution.py:185
  24.9 95.5 %collective-permute-start.2 = (bf16[6,3,128,128]{3,2,1,0:T(8,128)(2,1)}, bf16[6,3,128,128]{3,2,1,0:T(8,128)(2,1)S(1)}, u32[]{:S(2)}, u32[]{:S(2)}) collective-permute-start(bf16[6,3,128,128]{3,2,1,0:T(8,128)(2,1)} %get-tuple-element.28), channel_id=1, source_target_pairs={{0,1},{1,2},{2,3},{3,4},{4,5},{5,6},{6,7},{8,9},{9,10},{10,11},{11... | collective-permute-start | bytes 1769480 | tf_op jit(solution)/shard_map/ppermute | solution.py:185
  27.3 108.3 %copy-start.14 = (s32[1152,1]{1,0:T(8,128)}, s32[1152,1]{1,0:T(8,128)S(1)}, u32[]{:S(2)}) copy-start(s32[1152,1]{1,0:T(8,128)S(1)} %reshape.283.cluster_col) | copy-start | bytes 13828
  104.3 1.5 copy-start.27
  105.8 16.6 %collective-permute-start.3 = (bf16[6,3,128,128]{3,2,1,0:T(8,128)(2,1)S(1)}, bf16[6,3,128,128]{3,2,1,0:T(8,128)(2,1)S(1)}, u32[]{:S(2)}, u32[]{:S(2)}) collective-permute-start(bf16[6,3,128,128]{3,2,1,0:T(8,128)(2,1)S(1)} %copy-done.27), channel_id=1, source_target_pairs={{1,0},{2,1},{3,2},{4,3},{5,4},{6,5},{7,6},{9,8},{10,9},{11,10},{12... | collective-permute-start | bytes 1769480 | tf_op jit(solution)/shard_map/ppermute | solution.py:185
  111.2 43.2 %collective-permute-start = (bf16[6,3,128,128]{3,2,1,0:T(8,128)(2,1)S(1)}, bf16[6,3,128,128]{3,2,1,0:T(8,128)(2,1)S(1)}, u32[]{:S(2)}, u32[]{:S(2)}) collective-permute-start(bf16[6,3,128,128]{3,2,1,0:T(8,128)(2,1)S(1)} %get-tuple-element.30), channel_id=1, source_target_pairs={{0,8},{8,16},{16,24},{1,9},{9,17},{17,25},{2,10},{10,18},{18,26},{... | collective-permute-start | bytes 1769480 | tf_op jit(solution)/shard_map/ppermute | solution.py:185
  120.3 7.2 %copy-start.18 = (bf16[6,3,128,128]{3,2,1,0:T(8,128)(2,1)}, bf16[6,3,128,128]{3,2,1,0:T(8,128)(2,1)S(1)}, u32[]{:S(2)}) copy-start(bf16[6,3,128,128]{3,2,1,0:T(8,128)(2,1)S(1)} %collective-permute-done.2.ry_lo) | copy-start | bytes 1769476
  120.3 11.1 %collective-permute-start.16 = (bf16[6,2,128,128]{3,2,1,0:T(8,128)(2,1)S(1)}, bf16[6,2,128,128]{3,2,1,0:T(8,128)(2,1)S(1)}, u32[]{:S(2)}, u32[]{:S(2)}) collective-permute-start(bf16[6,2,128,128]{3,2,1,0:T(8,128)(2,1)S(1)} %pad_maximum_fusion.4), channel_id=1, source_target_pairs={{0,8},{8,16},{16,24},{1,9},{9,17},{17,25},{2,10},{10,18},{18,26},{... | collective-permute-start | bytes 1179656 | tf_op jit(solution)/shard_map/ppermute | solution.py:185
  122.3 13.4 %copy-start.23 = (bf16[128,128]{1,0:T(8,128)(2,1)S(1)}, bf16[128,128]{1,0:T(8,128)(2,1)}, u32[]{:S(2)}) copy-start(bf16[128,128]{1,0:T(8,128)(2,1)} %w_mix.3) | copy-start | bytes 98308
  122.3 13.4 %copy-start.24 = (bf16[128,128]{1,0:T(8,128)(2,1)S(1)}, bf16[128,128]{1,0:T(8,128)(2,1)}, u32[]{:S(2)}) copy-start(bf16[128,128]{1,0:T(8,128)(2,1)} %w_coarse.3) | copy-start | bytes 98308
  122.3 13.4 %copy-start.25 = (f32[128]{0:T(128)S(1)}, f32[128]{0:T(128)}, u32[]{:S(2)}) copy-start(f32[128]{0:T(128)} %param.14) | copy-start | bytes 1540
  122.4 13.2 %collective-permute-start.17 = (bf16[6,2,128,128]{3,2,1,0:T(8,128)(2,1)S(1)}, bf16[6,2,128,128]{3,2,1,0:T(8,128)(2,1)S(1)}, u32[]{:S(2)}, u32[]{:S(2)}) collective-permute-start(bf16[6,2,128,128]{3,2,1,0:T(8,128)(2,1)S(1)} %pad_maximum_fusion.5), channel_id=1, source_target_pairs={{8,0},{16,8},{24,16},{9,1},{17,9},{25,17},{10,2},{18,10},{26,18},{... | collective-permute-start | bytes 1179656 | tf_op jit(solution)/shard_map/ppermute | solution.py:185
  127.6 31.4 %collective-permute-start.1 = (bf16[6,3,128,128]{3,2,1,0:T(8,128)(2,1)S(1)}, bf16[6,3,128,128]{3,2,1,0:T(8,128)(2,1)S(1)}, u32[]{:S(2)}, u32[]{:S(2)}) collective-permute-start(bf16[6,3,128,128]{3,2,1,0:T(8,128)(2,1)S(1)} %get-tuple-element.29), channel_id=1, source_target_pairs={{8,0},{16,8},{24,16},{9,1},{17,9},{25,17},{10,2},{18,10},{26,18},{... | collective-permute-start | bytes 1769480 | tf_op jit(solution)/shard_map/ppermute | solution.py:185
  129.5 29.4 %collective-permute-start.5 = (bf16[6,2,128,128]{3,2,1,0:T(8,128)(2,1)S(1)}, bf16[6,2,128,128]{3,2,1,0:T(8,128)(2,1)S(1)}, u32[]{:S(2)}, u32[]{:S(2)}) collective-permute-start(bf16[6,2,128,128]{3,2,1,0:T(8,128)(2,1)S(1)} %pad_maximum_fusion.1), channel_id=1, source_target_pairs={{8,0},{16,8},{24,16},{9,1},{17,9},{25,17},{10,2},{18,10},{26,18},{... | collective-permute-start | bytes 1179656 | tf_op jit(solution)/shard_map/ppermute | solution.py:185
  131.5 27.5 %collective-permute-start.4 = (bf16[6,2,128,128]{3,2,1,0:T(8,128)(2,1)S(1)}, bf16[6,2,128,128]{3,2,1,0:T(8,128)(2,1)S(1)}, u32[]{:S(2)}, u32[]{:S(2)}) collective-permute-start(bf16[6,2,128,128]{3,2,1,0:T(8,128)(2,1)S(1)} %pad_maximum_fusion), channel_id=1, source_target_pairs={{0,8},{8,16},{16,24},{1,9},{9,17},{17,25},{2,10},{10,18},{18,26},{... | collective-permute-start | bytes 1179656 | tf_op jit(solution)/shard_map/ppermute | solution.py:185
  149.9 4.6 %copy-start.1 = (bf16[6,9,128,128]{3,2,1,0:T(8,128)(2,1)}, bf16[6,9,128,128]{3,2,1,0:T(8,128)(2,1)S(1)}, u32[]{:S(2)}) copy-start(bf16[6,9,128,128]{3,2,1,0:T(8,128)(2,1)S(1)} %get-tuple-element.12.own) | copy-start | bytes 5308420
  151.3 7.7 %copy-start.15 = (s32[1152,1]{1,0:T(8,128)S(1)}, s32[1152,1]{1,0:T(8,128)}, u32[]{:S(2)}) copy-start(s32[1152,1]{1,0:T(8,128)} %copy-done.14) | copy-start | bytes 13828
  151.3 7.7 %copy-start.19 = (bf16[6,3,128,128]{3,2,1,0:T(8,128)(2,1)S(1)}, bf16[6,3,128,128]{3,2,1,0:T(8,128)(2,1)}, u32[]{:S(2)}) copy-start(bf16[6,3,128,128]{3,2,1,0:T(8,128)(2,1)} %copy-done.18) | copy-start | bytes 1769476
  151.3 30.4 %collective-permute-start.20 = (bf16[6,3,128,128]{3,2,1,0:T(8,128)(2,1)}, bf16[6,3,128,128]{3,2,1,0:T(8,128)(2,1)S(1)}, u32[]{:S(2)}, u32[]{:S(2)}) collective-permute-start(bf16[6,3,128,128]{3,2,1,0:T(8,128)(2,1)} %get-tuple-element.16), channel_id=1, source_target_pairs={{0,1},{1,2},{2,3},{3,4},{4,5},{5,6},{6,7},{8,9},{9,10},{10,11},{11... | collective-permute-start | bytes 1769480 | tf_op jit(solution)/shard_map/ppermute | solution.py:185
  154.5 31.6 %collective-permute-start.21 = (bf16[6,3,128,128]{3,2,1,0:T(8,128)(2,1)}, bf16[6,3,128,128]{3,2,1,0:T(8,128)(2,1)S(1)}, u32[]{:S(2)}, u32[]{:S(2)}) collective-permute-start(bf16[6,3,128,128]{3,2,1,0:T(8,128)(2,1)} %get-tuple-element.15), channel_id=1, source_target_pairs={{1,0},{2,1},{3,2},{4,3},{5,4},{6,5},{7,6},{9,8},{10,9},{11,10},{12... | collective-permute-start | bytes 1769480 | tf_op jit(solution)/shard_map/ppermute | solution.py:185
  173.1 8.6 %copy-start = (bf16[6,9,128,128]{3,2,1,0:T(8,128)(2,1)}, bf16[6,9,128,128]{3,2,1,0:T(8,128)(2,1)S(1)}, u32[]{:S(2)}) copy-start(bf16[6,9,128,128]{3,2,1,0:T(8,128)(2,1)S(1)} %get-tuple-element.9.own) | copy-start | bytes 5308420
  173.9 38.6 %collective-permute-start.18 = (bf16[6,3,128,128]{3,2,1,0:T(8,128)(2,1)}, bf16[6,3,128,128]{3,2,1,0:T(8,128)(2,1)S(1)}, u32[]{:S(2)}, u32[]{:S(2)}) collective-permute-start(bf16[6,3,128,128]{3,2,1,0:T(8,128)(2,1)} %get-tuple-element.18), channel_id=1, source_target_pairs={{0,8},{8,16},{16,24},{1,9},{9,17},{17,25},{2,10},{10,18},{18,26},{... | collective-permute-start | bytes 1769480 | tf_op jit(solution)/shard_map/ppermute | solution.py:185
  176.6 40.9 %collective-permute-start.19 = (bf16[6,3,128,128]{3,2,1,0:T(8,128)(2,1)}, bf16[6,3,128,128]{3,2,1,0:T(8,128)(2,1)S(1)}, u32[]{:S(2)}, u32[]{:S(2)}) collective-permute-start(bf16[6,3,128,128]{3,2,1,0:T(8,128)(2,1)} %get-tuple-element.17), channel_id=1, source_target_pairs={{8,0},{16,8},{24,16},{9,1},{17,9},{25,17},{10,2},{18,10},{26,18},{... | collective-permute-start | bytes 1769480 | tf_op jit(solution)/shard_map/ppermute | solution.py:185
  178.7 27.3 %collective-permute-start.8 = (bf16[6,3,128,128]{3,2,1,0:T(8,128)(2,1)S(1)}, bf16[6,3,128,128]{3,2,1,0:T(8,128)(2,1)S(1)}, u32[]{:S(2)}, u32[]{:S(2)}) collective-permute-start(bf16[6,3,128,128]{3,2,1,0:T(8,128)(2,1)S(1)} %get-tuple-element.24), channel_id=1, source_target_pairs={{0,1},{1,2},{2,3},{3,4},{4,5},{5,6},{6,7},{8,9},{9,10},{10,11},{11... | collective-permute-start | bytes 1769480 | tf_op jit(solution)/shard_map/ppermute | solution.py:185
  181.7 29.9 %copy-start.2 = (bf16[6,3,128,128]{3,2,1,0:T(8,128)(2,1)}, bf16[6,3,128,128]{3,2,1,0:T(8,128)(2,1)S(1)}, u32[]{:S(2)}) copy-start(bf16[6,3,128,128]{3,2,1,0:T(8,128)(2,1)S(1)} %collective-permute-done.20.ry_lo) | copy-start | bytes 1769476
  181.7 27.6 %collective-permute-start.9 = (bf16[6,3,128,128]{3,2,1,0:T(8,128)(2,1)S(1)}, bf16[6,3,128,128]{3,2,1,0:T(8,128)(2,1)S(1)}, u32[]{:S(2)}, u32[]{:S(2)}) collective-permute-start(bf16[6,3,128,128]{3,2,1,0:T(8,128)(2,1)S(1)} %get-tuple-element.23), channel_id=1, source_target_pairs={{1,0},{2,1},{3,2},{4,3},{5,4},{6,5},{7,6},{9,8},{10,9},{11,10},{12... | collective-permute-start | bytes 1769480 | tf_op jit(solution)/shard_map/ppermute | solution.py:185
  186.0 26.4 %copy-start.4 = (bf16[6,3,128,128]{3,2,1,0:T(8,128)(2,1)}, bf16[6,3,128,128]{3,2,1,0:T(8,128)(2,1)S(1)}, u32[]{:S(2)}) copy-start(bf16[6,3,128,128]{3,2,1,0:T(8,128)(2,1)S(1)} %collective-permute-done.21.ry_hi) | copy-start | bytes 1769476
  186.0 129.6 %collective-permute-start.6 = (bf16[6,3,128,128]{3,2,1,0:T(8,128)(2,1)}, bf16[6,3,128,128]{3,2,1,0:T(8,128)(2,1)}, u32[]{:S(2)}, u32[]{:S(2)}) collective-permute-start(bf16[6,3,128,128]{3,2,1,0:T(8,128)(2,1)} %get-tuple-element.26), channel_id=1, source_target_pairs={{0,8},{8,16},{16,24},{1,9},{9,17},{17,25},{2,10},{10,18},{18,26},{... | collective-permute-start | bytes 1769480 | tf_op jit(solution)/shard_map/ppermute | solution.py:185
  206.0 11.5 %copy-start.6 = (bf16[6,3,128,128]{3,2,1,0:T(8,128)(2,1)}, bf16[6,3,128,128]{3,2,1,0:T(8,128)(2,1)S(1)}, u32[]{:S(2)}) copy-start(bf16[6,3,128,128]{3,2,1,0:T(8,128)(2,1)S(1)} %collective-permute-done.8.ry_lo) | copy-start | bytes 1769476
  206.0 109.6 %collective-permute-start.7 = (bf16[6,3,128,128]{3,2,1,0:T(8,128)(2,1)}, bf16[6,3,128,128]{3,2,1,0:T(8,128)(2,1)}, u32[]{:S(2)}, u32[]{:S(2)}) collective-permute-start(bf16[6,3,128,128]{3,2,1,0:T(8,128)(2,1)} %get-tuple-element.25), channel_id=1, source_target_pairs={{8,0},{16,8},{24,16},{9,1},{17,9},{25,17},{10,2},{18,10},{26,18},{... | collective-permute-start | bytes 1769480 | tf_op jit(solution)/shard_map/ppermute | solution.py:185
  209.3 12.3 %collective-permute-start.23 = (bf16[6,2,128,128]{3,2,1,0:T(8,128)(2,1)S(1)}, bf16[6,2,128,128]{3,2,1,0:T(8,128)(2,1)S(1)}, u32[]{:S(2)}, u32[]{:S(2)}) collective-permute-start(bf16[6,2,128,128]{3,2,1,0:T(8,128)(2,1)S(1)} %pad_maximum_fusion.7), channel_id=1, source_target_pairs={{8,0},{16,8},{24,16},{9,1},{17,9},{25,17},{10,2},{18,10},{26,18},{... | collective-permute-start | bytes 1179656 | tf_op jit(solution)/shard_map/ppermute | solution.py:185
  212.4 86.3 %copy-start.3 = (bf16[6,3,128,128]{3,2,1,0:T(8,128)(2,1)S(1)}, bf16[6,3,128,128]{3,2,1,0:T(8,128)(2,1)}, u32[]{:S(2)}) copy-start(bf16[6,3,128,128]{3,2,1,0:T(8,128)(2,1)} %copy-done.2) | copy-start | bytes 1769476
  212.4 86.3 %copy-start.20 = (bf16[128,128]{1,0:T(8,128)(2,1)S(1)}, bf16[128,128]{1,0:T(8,128)(2,1)}, u32[]{:S(2)}) copy-start(bf16[128,128]{1,0:T(8,128)(2,1)} %w_region.3) | copy-start | bytes 98308
  212.4 86.3 %copy-start.21 = (bf16[128,128]{1,0:T(8,128)(2,1)S(1)}, bf16[128,128]{1,0:T(8,128)(2,1)}, u32[]{:S(2)}) copy-start(bf16[128,128]{1,0:T(8,128)(2,1)} %w_out.3) | copy-start | bytes 98308
  212.5 12.4 %copy-start.10 = (bf16[6,3,128,128]{3,2,1,0:T(8,128)(2,1)}, bf16[6,3,128,128]{3,2,1,0:T(8,128)(2,1)S(1)}, u32[]{:S(2)}) copy-start(bf16[6,3,128,128]{3,2,1,0:T(8,128)(2,1)S(1)} %collective-permute-done.18.rx_lo) | copy-start | bytes 1769476
  212.5 86.3 %copy-start.5 = (bf16[6,3,128,128]{3,2,1,0:T(8,128)(2,1)S(1)}, bf16[6,3,128,128]{3,2,1,0:T(8,128)(2,1)}, u32[]{:S(2)}) copy-start(bf16[6,3,128,128]{3,2,1,0:T(8,128)(2,1)} %copy-done.4) | copy-start | bytes 1769476
  212.5 86.3 %collective-permute-start.22 = (bf16[6,2,128,128]{3,2,1,0:T(8,128)(2,1)}, bf16[6,2,128,128]{3,2,1,0:T(8,128)(2,1)}, u32[]{:S(2)}, u32[]{:S(2)}) collective-permute-start(bf16[6,2,128,128]{3,2,1,0:T(8,128)(2,1)} %pad_maximum_fusion.6), channel_id=1, source_target_pairs={{0,8},{8,16},{16,24},{1,9},{9,17},{17,25},{2,10},{10,18},{18,26},{... | collective-permute-start | bytes 1179656 | tf_op jit(solution)/shard_map/ppermute | solution.py:185
  217.5 0.8 copy-start.12
  218.3 97.3 %collective-permute-start.11 = (bf16[6,2,128,128]{3,2,1,0:T(8,128)(2,1)}, bf16[6,2,128,128]{3,2,1,0:T(8,128)(2,1)}, u32[]{:S(2)}, u32[]{:S(2)}) collective-permute-start(bf16[6,2,128,128]{3,2,1,0:T(8,128)(2,1)} %pad_maximum_fusion.3), channel_id=1, source_target_pairs={{8,0},{16,8},{24,16},{9,1},{17,9},{25,17},{10,2},{18,10},{26,18},{... | collective-permute-start | bytes 1179656 | tf_op jit(solution)/shard_map/ppermute | solution.py:185
  221.6 0.8 copy-start.16
  222.4 93.3 %collective-permute-start.10 = (bf16[6,2,128,128]{3,2,1,0:T(8,128)(2,1)}, bf16[6,2,128,128]{3,2,1,0:T(8,128)(2,1)}, u32[]{:S(2)}, u32[]{:S(2)}) collective-permute-start(bf16[6,2,128,128]{3,2,1,0:T(8,128)(2,1)} %pad_maximum_fusion.2), channel_id=1, source_target_pairs={{0,8},{8,16},{16,24},{1,9},{9,17},{17,25},{2,10},{10,18},{18,26},{... | collective-permute-start | bytes 1179656 | tf_op jit(solution)/shard_map/ppermute | solution.py:185
  298.8 0.9 copy-start.8
  299.7 1.1 copy-start.11
  300.8 1.1 copy-start.13
  301.9 1.0 copy-start.17
  302.8 12.8 %copy-start.7 = (bf16[6,3,128,128]{3,2,1,0:T(8,128)(2,1)S(1)}, bf16[6,3,128,128]{3,2,1,0:T(8,128)(2,1)}, u32[]{:S(2)}) copy-start(bf16[6,3,128,128]{3,2,1,0:T(8,128)(2,1)} %copy-done.6) | copy-start | bytes 1769476
  302.9 12.8 %copy-start.9 = (f32[12,32,128]{2,1,0:T(8,128)S(1)}, f32[12,32,128]{2,1,0:T(8,128)}, u32[]{:S(2)}) copy-start(f32[12,32,128]{2,1,0:T(8,128)} %all-reduce.2.cloned.1.call-done.region_sum) | copy-start | bytes 589828
Sparse Core Ops, SparseCore 0:
  174.0 124.7 all-reduce.1

commit v2 on v1

--- a/solution.py
+++ b/solution.py
@@ -1,4 +1,3 @@
-import functools
 import jax
 import jax.numpy as jnp
 from jax import lax
@@ -116,7 +115,6 @@
 
 
 def decode_kernel(
-    denominator,
     index,
     own,
     rx_lo,
@@ -126,7 +124,7 @@
     co_lo,
     co_hi,
     adjacency,
-    region_sum,
+    region,
     owner_ext,
     w_region,
     w_out,
@@ -134,11 +132,10 @@
 ):
     out_ref, ext = rest[-2:]
     steps = own.shape[0]
-    devices = region_sum.shape[1]
+    devices = region.shape[1]
     reaches = []
     for t in range(steps):
-        region = (region_sum[t] / denominator).astype(jnp.bfloat16)
-        reaches.append(dot32(region, w_region[...]).astype(jnp.bfloat16))
+        reaches.append(dot32(region[t], w_region[...]).astype(jnp.bfloat16))
     reach = jnp.concatenate(reaches, axis=1)
     for p, (ref, k) in enumerate(
         extended_sources(own, rx_lo, rx_hi, ry_lo, ry_hi, co_lo, co_hi)
@@ -175,14 +172,15 @@
     return pl.BlockSpec(array.shape, lambda i, _: zeros)
 
 
+def shifted(value, axis, up):
+    count = lax.axis_size(axis)
+    pairs = [(i, i + 1) if up else (i + 1, i) for i in range(count - 1)]
+    return lax.ppermute(value, axis, pairs)
+
+
 def halo(field):
     steps = field.shape[0]
     square = field.reshape(steps, GB, GB, BLK, BLK)
-
-    def shifted(value, axis, up):
-        count = lax.axis_size(axis)
-        pairs = [(i, i + 1) if up else (i + 1, i) for i in range(count - 1)]
-        return lax.ppermute(value, axis, pairs)
 
     ry_lo = shifted(square[:, :, GB - 1], "ry", True)
     ry_hi = shifted(square[:, :, 0], "ry", False)
@@ -226,24 +224,14 @@
         ),
         axis=1,
     )
-    everyone = lax.all_gather(owner_of.reshape(blocks, BLK), ("rx", "ry"), axis=0, tiled=True)
-    ext_rows = jnp.arange(SIDE * SIDE, dtype=jnp.int32)
-    grid_row = lax.axis_index("rx") * GB + ext_rows // SIDE - 1
-    grid_col = lax.axis_index("ry") * GB + ext_rows % SIDE - 1
-    inside = (
-        (grid_row >= 0)
-        & (grid_row < row_devices * GB)
-        & (grid_col >= 0)
-        & (grid_col < col_devices * GB)
-    )
-    grid_row = jnp.clip(grid_row, 0, row_devices * GB - 1)
-    grid_col = jnp.clip(grid_col, 0, col_devices * GB - 1)
-    place = (
-        (grid_row // GB * col_devices + grid_col // GB) * blocks
-        + grid_row % GB * GB
-        + grid_col % GB
-    )
-    owner_ext = jnp.where(inside[:, None], everyone[place], -1).reshape(SIDE * SIDE * BLK, 1)
+    marks = (owner_of + 1).reshape(GB, GB, BLK)
+    marks = jnp.concatenate(
+        [shifted(marks[:, -1:], "ry", True), marks, shifted(marks[:, :1], "ry", False)], axis=1
+    )
+    marks = jnp.concatenate(
+        [shifted(marks[-1:], "rx", True), marks, shifted(marks[:1], "rx", False)], axis=0
+    )
+    owner_ext = (marks - 1).reshape(SIDE * SIDE * BLK, 1)
 
     chunk = steps_count // CHUNKS
     per = LANES_STEPS
@@ -291,21 +279,35 @@
         fields.append(u)
         sums.append(partial)
         second.append(halo(u))
-    region_sum = lax.psum(jnp.concatenate(sums, axis=0), ("rx", "ry"))
+    mine = lax.all_to_all(
+        jnp.concatenate(sums, axis=0).transpose(1, 0, 2),
+        ("rx", "ry"),
+        split_axis=0,
+        concat_axis=0,
+        tiled=True,
+    )
+    own_region = (jnp.sum(mine, axis=0) / float(coarse)).astype(jnp.bfloat16)
+    region = lax.all_to_all(
+        jnp.broadcast_to(own_region[None], (devices, steps_count, channels)),
+        ("rx", "ry"),
+        split_axis=0,
+        concat_axis=0,
+        tiled=True,
+    ).transpose(1, 0, 2)
 
     out = None
     for c in range(CHUNKS):
         shared = (owner_ext, w_region, w_out)
         extra = () if out is None else (out,)
-        operands = (index, fields[c], *second[c], adjacency, region_sum, *shared, *extra)
+        operands = (index, fields[c], *second[c], adjacency, region, *shared, *extra)
         out = pl.pallas_call(
-            functools.partial(decode_kernel, float(coarse)),
+            decode_kernel,
             grid_spec=pltpu.PrefetchScalarGridSpec(
                 num_scalar_prefetch=1,
                 grid=(grid,),
                 in_specs=[stepped(fields[c], per)]
                 + [stepped(part, per) for part in second[c]]
-                + [whole(adjacency), stepped(region_sum, per, c * grid)]
+                + [whole(adjacency), stepped(region, per, c * grid)]
                 + [whole(part) for part in shared]
                 + [pl.BlockSpec(memory_space=pl.ANY)] * len(extra),
                 out_specs=pl.BlockSpec(

time: 339 us -> 230 us (0.68)
  blocking collectives: 75.9 us -> 0 us
  waiting for transfers between devices: 91.8 us -> 51.7 us
  starting transfers between devices: 77.5 us -> 94 us
  between operations: 14.2 us -> 0.87 us
  local copies, waits for them, and re-layouts: 18.4 us -> 23.5 us
    all_gather x1 -> x0, blocking collectives: 75.9 us -> none  [on_device(): lax.all_gather(owner_of.reshape(blocks, BLK), ('rx', 'ry'), axis=0, tiled...]
    psum x1 -> x0, waiting for transfers between devices: 73.3 us -> none  [on_device(): region_sum = lax.psum(jnp.concatenate(sums, axis=0), ('rx', 'ry'))]
    ppermute x24 -> x28, waiting for transfers between devices: 18.5 us -> 47.5 us  [shifted(): return lax.ppermute(value, axis, pairs)]
    all_to_all x0 -> x2, starting transfers between devices: none -> 9.8 us  [the longest x1 5.82 us: on_device(): lax.all_to_all(jnp.concatenate(sums, axis=0).transpose(1, 0, 2), ('rx', '...]
    ppermute x24 -> x28, starting transfers between devices: 77.5 us -> 84.2 us  [shifted(): return lax.ppermute(value, axis, pairs)]
    all_to_all x0 -> x2, waiting for transfers between devices: none -> 4.25 us  [the longest x1 4.25 us: on_device(): lax.all_to_all(jnp.concatenate(sums, axis=0).transpose(1, 0, 2), ('rx', '...]
  transfers between devices with their start and end apart: 25 -> 30, of which waited for: 4 -> 4; matrix products, arithmetic and copies ran while one was open for 4% -> 8% of each run, Pallas kernels for 12% -> 18%
where the time goes in v2:
time: 230 us; the launch traced here: 228 us
  starting transfers between devices  94 us (41%)
  Pallas kernels  54.7 us (24%)
  waiting for transfers between devices  51.7 us (22%)
  local copies, waits for them, and re-layouts  23.5 us (10%)
  other arithmetic  2.92 us (1%)
    ppermute x28, starting transfers between devices, shifted(): return lax.ppermute(value, axis, pairs)  84.2 us
    ppermute x28, waiting for transfers between devices, shifted(): return lax.ppermute(value, axis, pairs)  47.5 us
    pallas_call x2, Pallas kernels, on_device(): pl.pallas_call(encode_kernel, grid_spec=pltpu.PrefetchScalarGridSpec(num_...  28.2 us
    pallas_call x2, Pallas kernels, on_device(): pl.pallas_call(decode_kernel, grid_spec=pltpu.PrefetchScalarGridSpec(num_...  26.5 us
    squeeze x4, local copies, waits for them, and re-layouts, halo(): rx_hi = shifted(square[:, 0], 'rx', False)  5.94 us
    all_to_all x1, starting transfers between devices, on_device(): lax.all_to_all(jnp.concatenate(sums, axis=0).transpose(1, 0, 2), ('rx', '...  5.82 us
    squeeze x4, local copies, waits for them, and re-layouts, halo(): ry_hi = shifted(square[:, :, 0], 'ry', False)  5.65 us
  transfers between devices with their start and end apart: 30, of which 4 were waited for; matrix products, arithmetic and copies ran while one was open for 8% of the time, Pallas kernels for 18%

profile of v2, /device:TPU:9, one launch (start us, length us, event | category | flops | bytes accessed | tf_op | source)
XLA Modules:
  0.0 227.6 jit_solution(577512368877418509)
XLA Ops:
  0.0 3.4 %fusion.5 = (bf16[6,1152,128]{2,1,0:T(8,128)(2,1)S(1)}, bf16[6,1152,128]{2,1,0:T(8,128)(2,1)}) fusion(bf16[12,1152,128]{2,1,0:T(8,128)(2,1)} %bitcast.97), kind=kLoop, calls=%fused_computation.48 | loop fusion | bytes 7077888 | tf_op jit(solution)/shard_map/slice | solution.py:248
  3.4 0.9 slice_bitcast_fusion.4
  4.4 3.3 %collective-permute-start.14 = (bf16[6,3,128,128]{3,2,1,0:T(8,128)(2,1)}, bf16[6,3,128,128]{3,2,1,0:T(8,128)(2,1)S(1)}, u32[]{:S(2)}, u32[]{:S(2)}) collective-permute-start(bf16[6,3,128,128]{3,2,1,0:T(8,128)(2,1)} %get-tuple-element.20), channel_id=1, source_target_pairs={{0,1},{1,2},{2,3},{3,4},{4,5},{5,6},{6,7},{8,9},{9,10},{10,11},{11... | collective-permute-start | bytes 1769480 | tf_op jit(solution)/shard_map/ppermute | solution.py:178
  7.6 3.0 %collective-permute-start.15 = (bf16[6,3,128,128]{3,2,1,0:T(8,128)(2,1)S(1)}, bf16[6,3,128,128]{3,2,1,0:T(8,128)(2,1)S(1)}, u32[]{:S(2)}, u32[]{:S(2)}) collective-permute-start(bf16[6,3,128,128]{3,2,1,0:T(8,128)(2,1)S(1)} %get-tuple-element.19), channel_id=1, source_target_pairs={{1,0},{2,1},{3,2},{4,3},{5,4},{6,5},{7,6},{9,8},{10,9},{11,10},{12... | collective-permute-start | bytes 1769480 | tf_op jit(solution)/shard_map/ppermute | solution.py:178
  10.7 1.2 slice_bitcast_fusion.6
  11.9 4.2 %collective-permute-start.12 = (bf16[6,3,128,128]{3,2,1,0:T(8,128)(2,1)}, bf16[6,3,128,128]{3,2,1,0:T(8,128)(2,1)S(1)}, u32[]{:S(2)}, u32[]{:S(2)}) collective-permute-start(bf16[6,3,128,128]{3,2,1,0:T(8,128)(2,1)} %get-tuple-element.22), channel_id=1, source_target_pairs={{0,8},{8,16},{16,24},{1,9},{9,17},{17,25},{2,10},{10,18},{18,26},{... | collective-permute-start | bytes 1769480 | tf_op jit(solution)/shard_map/ppermute | solution.py:178
  16.1 0.2 select_reduce_fusion
  16.3 2.2 collective-permute-start.18
  18.6 3.9 %collective-permute-start.19 = (s32[3,1,128]{2,1,0:T(1,128)S(1)}, s32[3,1,128]{2,1,0:T(1,128)S(1)}, u32[]{:S(2)}, u32[]{:S(2)}) collective-permute-start(s32[3,1,128]{2,1,0:T(1,128)S(1)} %get-tuple-element.50), channel_id=1, source_target_pairs={{1,0},{2,1},{3,2},{4,3},{5,4},{6,5},{7,6},{9,8},{10,9},{11,10},{12... | collective-permute-start | bytes 4616 | tf_op jit(solution)/shard_map/ppermute | solution.py:178
  22.5 2.4 %slice_bitcast_fusion.12 = (bf16[6,3,128,128]{3,2,1,0:T(8,128)(2,1)}, bf16[6,3,128,128]{3,2,1,0:T(8,128)(2,1)}) fusion(bf16[6,3,3,128,128]{4,3,2,1,0:T(8,128)(2,1)} %bitcast.93), kind=kLoop, calls=%fused_computation.14 | loop fusion | bytes 2359296 | tf_op jit(solution)/shard_map/squeeze | solution.py:186
  24.9 2.4 %slice_bitcast_fusion.14 = (bf16[6,3,128,128]{3,2,1,0:T(8,128)(2,1)}, bf16[6,3,128,128]{3,2,1,0:T(8,128)(2,1)}) fusion(bf16[6,3,3,128,128]{4,3,2,1,0:T(8,128)(2,1)} %bitcast.94), kind=kLoop, calls=%fused_computation.16 | loop fusion | bytes 2359296 | tf_op jit(solution)/shard_map/squeeze | solution.py:188
  27.4 0.2 reshape.95.cluster_col
  27.6 0.1 copy.66
  27.7 0.1 reshape.81.index
  27.8 4.8 %collective-permute-done.18 = s32[3,1,128]{2,1,0:T(1,128)S(1)} collective-permute-done((s32[3,1,128]{2,1,0:T(1,128)S(1)}, s32[3,1,128]{2,1,0:T(1,128)S(1)}, u32[]{:S(2)}, u32[]{:S(2)}) %collective-permute-start.18) | collective-permute-done | bytes 1568 | tf_op jit(solution)/shard_map/ppermute | solution.py:178
  32.6 3.5 %collective-permute-start.13 = (bf16[6,3,128,128]{3,2,1,0:T(8,128)(2,1)}, bf16[6,3,128,128]{3,2,1,0:T(8,128)(2,1)S(1)}, u32[]{:S(2)}, u32[]{:S(2)}) collective-permute-start(bf16[6,3,128,128]{3,2,1,0:T(8,128)(2,1)} %get-tuple-element.21), channel_id=1, source_target_pairs={{8,0},{16,8},{24,16},{9,1},{17,9},{25,17},{10,2},{18,10},{26,18},{... | collective-permute-start | bytes 1769480 | tf_op jit(solution)/shard_map/ppermute | solution.py:178
  36.1 4.0 %collective-permute-start.2 = (bf16[6,3,128,128]{3,2,1,0:T(8,128)(2,1)}, bf16[6,3,128,128]{3,2,1,0:T(8,128)(2,1)S(1)}, u32[]{:S(2)}, u32[]{:S(2)}) collective-permute-start(bf16[6,3,128,128]{3,2,1,0:T(8,128)(2,1)} %get-tuple-element.28), channel_id=1, source_target_pairs={{0,1},{1,2},{2,3},{3,4},{4,5},{5,6},{6,7},{8,9},{9,10},{10,11},{11... | collective-permute-start | bytes 1769480 | tf_op jit(solution)/shard_map/ppermute | solution.py:178
  40.2 2.1 collective-permute-start.3
  42.4 3.6 %collective-permute-start = (bf16[6,3,128,128]{3,2,1,0:T(8,128)(2,1)}, bf16[6,3,128,128]{3,2,1,0:T(8,128)(2,1)S(1)}, u32[]{:S(2)}, u32[]{:S(2)}) collective-permute-start(bf16[6,3,128,128]{3,2,1,0:T(8,128)(2,1)} %get-tuple-element.30), channel_id=1, source_target_pairs={{0,8},{8,16},{16,24},{1,9},{9,17},{17,25},{2,10},{10,18},{18,26},{... | collective-permute-start | bytes 1769480 | tf_op jit(solution)/shard_map/ppermute | solution.py:178
  46.0 20.0 %collective-permute-done.2.ry_lo = bf16[6,3,128,128]{3,2,1,0:T(8,128)(2,1)S(1)} collective-permute-done((bf16[6,3,128,128]{3,2,1,0:T(8,128)(2,1)}, bf16[6,3,128,128]{3,2,1,0:T(8,128)(2,1)S(1)}, u32[]{:S(2)}, u32[]{:S(2)}) %collective-permute-start.2) | collective-permute-done | bytes 589856 | tf_op jit(solution)/shard_map/ppermute | solution.py:178
  66.1 3.6 %collective-permute-start.16 = (bf16[6,2,128,128]{3,2,1,0:T(8,128)(2,1)S(1)}, bf16[6,2,128,128]{3,2,1,0:T(8,128)(2,1)S(1)}, u32[]{:S(2)}, u32[]{:S(2)}) collective-permute-start(bf16[6,2,128,128]{3,2,1,0:T(8,128)(2,1)S(1)} %pad_maximum_fusion.4), channel_id=1, source_target_pairs={{0,8},{8,16},{16,24},{1,9},{9,17},{17,25},{2,10},{10,18},{18,26},{... | collective-permute-start | bytes 1179656 | tf_op jit(solution)/shard_map/ppermute | solution.py:178
  69.7 0.0 copy-start.18
  69.7 0.0 copy-start.19
  69.8 2.1 collective-permute-start.17
  72.0 1.9 collective-permute-start.1
  73.9 3.6 %collective-permute-start.20 = (s32[1,5,128]{2,1,0:T(8,128)S(1)}, s32[1,5,128]{2,1,0:T(8,128)S(1)}, u32[]{:S(2)}, u32[]{:S(2)}) collective-permute-start(s32[1,5,128]{2,1,0:T(8,128)S(1)} %get-tuple-element.47), channel_id=1, source_target_pairs={{0,8},{8,16},{16,24},{1,9},{9,17},{17,25},{2,10},{10,18},{18,26},{... | collective-permute-start | bytes 7688 | tf_op jit(solution)/shard_map/ppermute | solution.py:178
  77.6 1.9 collective-permute-start.5
  79.5 3.6 %collective-permute-start.4 = (bf16[6,2,128,128]{3,2,1,0:T(8,128)(2,1)S(1)}, bf16[6,2,128,128]{3,2,1,0:T(8,128)(2,1)S(1)}, u32[]{:S(2)}, u32[]{:S(2)}) collective-permute-start(bf16[6,2,128,128]{3,2,1,0:T(8,128)(2,1)S(1)} %pad_maximum_fusion), channel_id=1, source_target_pairs={{0,8},{8,16},{16,24},{1,9},{9,17},{17,25},{2,10},{10,18},{18,26},{... | collective-permute-start | bytes 1179656 | tf_op jit(solution)/shard_map/ppermute | solution.py:178
  83.2 14.1 %encode.3 = (bf16[6,9,128,128]{3,2,1,0:T(8,128)(2,1)S(1)}, f32[6,32,128]{2,1,0:T(8,128)S(1)}) custom-call(s32[54]{0:T(128)S(1)} %reshape.81.index, bf16[12,9,128,128]{3,2,1,0:T(8,128)(2,1)} %bitcast.98, bf16[6,3,128,128]{3,2,1,0:T(8,128)(2,1)S(1)} %collective-permute-done.12.rx_lo, bf16[6,3,128,128]{3,2,1,0:T(8,128)(2,1)S(1)} %collective-permute-done.13.rx_hi, ...), custom_call_target="tpu_custom_call" | custom-call | flops 2500000000 | bytes 8000000 | tf_op jit(solution)/shard_map/encode/pallas_call | solution.py:254
  97.4 1.3 slice_bitcast_fusion
  98.6 1.2 slice_bitcast_fusion.2
  99.8 1.9 collective-permute-start.21
  101.8 4.0 %collective-permute-start.24 = (bf16[6,3,128,128]{3,2,1,0:T(8,128)(2,1)}, bf16[6,3,128,128]{3,2,1,0:T(8,128)(2,1)S(1)}, u32[]{:S(2)}, u32[]{:S(2)}) collective-permute-start(bf16[6,3,128,128]{3,2,1,0:T(8,128)(2,1)} %get-tuple-element.16), channel_id=1, source_target_pairs={{0,1},{1,2},{2,3},{3,4},{4,5},{5,6},{6,7},{8,9},{9,10},{10,11},{11... | collective-permute-start | bytes 1769480 | tf_op jit(solution)/shard_map/ppermute | solution.py:178
  105.8 2.2 collective-permute-start.25
  108.0 14.1 %encode.2 = (bf16[6,9,128,128]{3,2,1,0:T(8,128)(2,1)S(1)}, f32[6,32,128]{2,1,0:T(8,128)S(1)}) custom-call(s32[54]{0:T(128)S(1)} %reshape.81.index, bf16[12,9,128,128]{3,2,1,0:T(8,128)(2,1)} %bitcast.99, bf16[6,3,128,128]{3,2,1,0:T(8,128)(2,1)S(1)} %collective-permute-done.rx_lo, bf16[6,3,128,128]{3,2,1,0:T(8,128)(2,1)S(1)} %collective-permute-done.1.rx_hi, ...), custom_call_target="tpu_custom_call" | custom-call | flops 2500000000 | bytes 8000000 | tf_op jit(solution)/shard_map/encode/pallas_call | solution.py:254
  122.1 1.0 copy.81
  123.1 5.8 %all-to-all-start = ((f32[32,12,128]{2,1,0:T(8,128)}), f32[32,12,128]{2,1,0:T(8,128)S(1)}, u32[]{:S(2)}, u32[]{:S(2)}) async-start(f32[32,12,128]{2,1,0:T(8,128)} %copy.81), calls=%async_computation | async-start | bytes 524288 | tf_op jit(solution)/shard_map/all_to_all | solution.py:282
  129.0 1.1 slice_bitcast_fusion.8
  130.0 1.1 slice_bitcast_fusion.10
  131.2 3.3 %collective-permute-start.22 = (bf16[6,3,128,128]{3,2,1,0:T(8,128)(2,1)}, bf16[6,3,128,128]{3,2,1,0:T(8,128)(2,1)}, u32[]{:S(2)}, u32[]{:S(2)}) collective-permute-start(bf16[6,3,128,128]{3,2,1,0:T(8,128)(2,1)} %get-tuple-element.18), channel_id=1, source_target_pairs={{0,8},{8,16},{16,24},{1,9},{9,17},{17,25},{2,10},{10,18},{18,26},{... | collective-permute-start | bytes 1769480 | tf_op jit(solution)/shard_map/ppermute | solution.py:178
  134.5 4.2 %all-to-all-done = f32[32,12,128]{2,1,0:T(8,128)S(1)} async-done(((f32[32,12,128]{2,1,0:T(8,128)}), f32[32,12,128]{2,1,0:T(8,128)S(1)}, u32[]{:S(2)}, u32[]{:S(2)}) %all-to-all-start) | async-done | bytes 196640 | tf_op jit(solution)/shard_map/all_to_all | solution.py:282
  138.8 0.7 broadcast_in_dim.24
  139.5 4.0 %all-to-all-start.1 = ((bf16[32,12,128]{2,1,0:T(8,128)(2,1)}), bf16[32,12,128]{2,1,0:T(8,128)(2,1)}, u32[]{:S(2)}, u32[]{:S(2)}) async-start(bf16[32,12,128]{2,1,0:T(8,128)(2,1)} %broadcast_in_dim.24), calls=%async_computation.1 | async-start | bytes 262144 | tf_op jit(solution)/shard_map/all_to_all | solution.py:290
  143.5 3.1 %collective-permute-start.8 = (bf16[6,3,128,128]{3,2,1,0:T(8,128)(2,1)}, bf16[6,3,128,128]{3,2,1,0:T(8,128)(2,1)S(1)}, u32[]{:S(2)}, u32[]{:S(2)}) collective-permute-start(bf16[6,3,128,128]{3,2,1,0:T(8,128)(2,1)} %get-tuple-element.24), channel_id=1, source_target_pairs={{0,1},{1,2},{2,3},{3,4},{4,5},{5,6},{6,7},{8,9},{9,10},{10,11},{11... | collective-permute-start | bytes 1769480 | tf_op jit(solution)/shard_map/ppermute | solution.py:178
  146.7 3.1 %collective-permute-start.9 = (bf16[6,3,128,128]{3,2,1,0:T(8,128)(2,1)}, bf16[6,3,128,128]{3,2,1,0:T(8,128)(2,1)S(1)}, u32[]{:S(2)}, u32[]{:S(2)}) collective-permute-start(bf16[6,3,128,128]{3,2,1,0:T(8,128)(2,1)} %get-tuple-element.23), channel_id=1, source_target_pairs={{1,0},{2,1},{3,2},{4,3},{5,4},{6,5},{7,6},{9,8},{10,9},{11,10},{12... | collective-permute-start | bytes 1769480 | tf_op jit(solution)/shard_map/ppermute | solution.py:178
  149.8 22.6 %collective-permute-done.8.ry_lo = bf16[6,3,128,128]{3,2,1,0:T(8,128)(2,1)S(1)} collective-permute-done((bf16[6,3,128,128]{3,2,1,0:T(8,128)(2,1)}, bf16[6,3,128,128]{3,2,1,0:T(8,128)(2,1)S(1)}, u32[]{:S(2)}, u32[]{:S(2)}) %collective-permute-start.8) | collective-permute-done | bytes 589856 | tf_op jit(solution)/shard_map/ppermute | solution.py:178
  172.4 2.9 %collective-permute-start.23 = (bf16[6,3,128,128]{3,2,1,0:T(8,128)(2,1)}, bf16[6,3,128,128]{3,2,1,0:T(8,128)(2,1)S(1)}, u32[]{:S(2)}, u32[]{:S(2)}) collective-permute-start(bf16[6,3,128,128]{3,2,1,0:T(8,128)(2,1)} %get-tuple-element.17), channel_id=1, source_target_pairs={{8,0},{16,8},{24,16},{9,1},{17,9},{25,17},{10,2},{18,10},{26,18},{... | collective-permute-start | bytes 1769480 | tf_op jit(solution)/shard_map/ppermute | solution.py:178
  175.3 1.9 collective-permute-start.27
  177.3 0.8 pad_maximum_fusion.6
  178.2 3.8 %collective-permute-start.6 = (bf16[6,3,128,128]{3,2,1,0:T(8,128)(2,1)}, bf16[6,3,128,128]{3,2,1,0:T(8,128)(2,1)}, u32[]{:S(2)}, u32[]{:S(2)}) collective-permute-start(bf16[6,3,128,128]{3,2,1,0:T(8,128)(2,1)} %get-tuple-element.26), channel_id=1, source_target_pairs={{0,8},{8,16},{16,24},{1,9},{9,17},{17,25},{2,10},{10,18},{18,26},{... | collective-permute-start | bytes 1769480 | tf_op jit(solution)/shard_map/ppermute | solution.py:178
  181.9 1.9 collective-permute-start.7
  183.9 3.6 %collective-permute-start.26 = (bf16[6,2,128,128]{3,2,1,0:T(8,128)(2,1)}, bf16[6,2,128,128]{3,2,1,0:T(8,128)(2,1)}, u32[]{:S(2)}, u32[]{:S(2)}) collective-permute-start(bf16[6,2,128,128]{3,2,1,0:T(8,128)(2,1)} %pad_maximum_fusion.6), channel_id=1, source_target_pairs={{0,8},{8,16},{16,24},{1,9},{9,17},{17,25},{2,10},{10,18},{18,26},{... | collective-permute-start | bytes 1179656 | tf_op jit(solution)/shard_map/ppermute | solution.py:178
  187.5 0.8 pad_maximum_fusion.3
  188.4 0.8 pad_maximum_fusion.2
  189.2 0.8 copy-done.8
  190.0 1.9 collective-permute-start.11
  191.9 0.7 copy-done.12
  192.7 3.8 %collective-permute-start.10 = (bf16[6,2,128,128]{3,2,1,0:T(8,128)(2,1)}, bf16[6,2,128,128]{3,2,1,0:T(8,128)(2,1)}, u32[]{:S(2)}, u32[]{:S(2)}) collective-permute-start(bf16[6,2,128,128]{3,2,1,0:T(8,128)(2,1)} %pad_maximum_fusion.2), channel_id=1, source_target_pairs={{0,8},{8,16},{16,24},{1,9},{9,17},{17,25},{2,10},{10,18},{18,26},{... | collective-permute-start | bytes 1179656 | tf_op jit(solution)/shard_map/ppermute | solution.py:178
  196.5 1.5 sub.20.owner_ext
  198.1 0.9 copy.106
  199.1 1.1 copy-done.9
  200.1 1.0 copy-done.13
  201.1 13.1 %decode.2.rest_0_ = bf16[12,9,128,128]{3,2,1,0:T(8,128)(2,1)} custom-call(s32[54]{0:T(128)S(1)} %reshape.81.index, bf16[6,9,128,128]{3,2,1,0:T(8,128)(2,1)} %copy-done.1, bf16[6,3,128,128]{3,2,1,0:T(8,128)(2,1)} %collective-permute-done.22.rx_lo, bf16[6,3,128,128]{3,2,1,0:T(8,128)(2,1)S(1)} %copy-done.9, bf16[6,3,128,128]{3,2,1,0:T(8,128)(2,1)S(1)} %copy-done.3, ...), custom_call_target="tpu_custom_call" | custom-call | flops 2500000000 | bytes 8000000 | tf_op jit(solution)/shard_map/decode/pallas_call | solution.py:303
  214.3 13.4 %decode.3 = bf16[12,9,128,128]{3,2,1,0:T(8,128)(2,1)} custom-call(s32[54]{0:T(128)S(1)} %reshape.81.index, bf16[6,9,128,128]{3,2,1,0:T(8,128)(2,1)} %copy-done, bf16[6,3,128,128]{3,2,1,0:T(8,128)(2,1)} %collective-permute-done.6.rx_lo, bf16[6,3,128,128]{3,2,1,0:T(8,128)(2,1)} %collective-permute-done.7.rx_hi, ...), custom_call_target="tpu_custom_call", output_to_operand_aliasing={{}: (13, {})} | custom-call | flops 2500000000 | bytes 8000000 | tf_op jit(solution)/shard_map/decode/pallas_call | solution.py:303
  (93 shorter events, 0.7 us)
Async XLA Ops:
  4.4 11.7 %copy-start.16 = (s32[144,1]{0,1:T(1,128)S(1)}, s32[144,1]{0,1:T(1,128)}, u32[]{:S(2)}) copy-start(s32[144,1]{0,1:T(1,128)} %param.18) | copy-start | bytes 1732
  4.4 11.7 %copy-start.21 = (s32[1152]{0:T(1024)S(1)}, s32[1152]{0:T(1024)}, u32[]{:S(2)}) copy-start(s32[1152]{0:T(1024)} %param.17) | copy-start | bytes 13828
  4.4 35.8 %collective-permute-start.14 = (bf16[6,3,128,128]{3,2,1,0:T(8,128)(2,1)}, bf16[6,3,128,128]{3,2,1,0:T(8,128)(2,1)S(1)}, u32[]{:S(2)}, u32[]{:S(2)}) collective-permute-start(bf16[6,3,128,128]{3,2,1,0:T(8,128)(2,1)} %get-tuple-element.20), channel_id=1, source_target_pairs={{0,1},{1,2},{2,3},{3,4},{4,5},{5,6},{6,7},{8,9},{9,10},{10,11},{11... | collective-permute-start | bytes 1769480 | tf_op jit(solution)/shard_map/ppermute | solution.py:178
  7.6 34.7 %collective-permute-start.15 = (bf16[6,3,128,128]{3,2,1,0:T(8,128)(2,1)S(1)}, bf16[6,3,128,128]{3,2,1,0:T(8,128)(2,1)S(1)}, u32[]{:S(2)}, u32[]{:S(2)}) collective-permute-start(bf16[6,3,128,128]{3,2,1,0:T(8,128)(2,1)S(1)} %get-tuple-element.19), channel_id=1, source_target_pairs={{1,0},{2,1},{3,2},{4,3},{5,4},{6,5},{7,6},{9,8},{10,9},{11,10},{12... | collective-permute-start | bytes 1769480 | tf_op jit(solution)/shard_map/ppermute | solution.py:178
  11.9 60.1 %collective-permute-start.12 = (bf16[6,3,128,128]{3,2,1,0:T(8,128)(2,1)}, bf16[6,3,128,128]{3,2,1,0:T(8,128)(2,1)S(1)}, u32[]{:S(2)}, u32[]{:S(2)}) collective-permute-start(bf16[6,3,128,128]{3,2,1,0:T(8,128)(2,1)} %get-tuple-element.22), channel_id=1, source_target_pairs={{0,8},{8,16},{16,24},{1,9},{9,17},{17,25},{2,10},{10,18},{18,26},{... | collective-permute-start | bytes 1769480 | tf_op jit(solution)/shard_map/ppermute | solution.py:178
  16.3 16.3 %collective-permute-start.18 = (s32[3,1,128]{2,1,0:T(1,128)S(1)}, s32[3,1,128]{2,1,0:T(1,128)S(1)}, u32[]{:S(2)}, u32[]{:S(2)}) collective-permute-start(s32[3,1,128]{2,1,0:T(1,128)S(1)} %get-tuple-element.49), channel_id=1, source_target_pairs={{0,1},{1,2},{2,3},{3,4},{4,5},{5,6},{6,7},{8,9},{9,10},{10,11},{11... | collective-permute-start | bytes 4616 | tf_op jit(solution)/shard_map/ppermute | solution.py:178
  18.6 17.5 %collective-permute-start.19 = (s32[3,1,128]{2,1,0:T(1,128)S(1)}, s32[3,1,128]{2,1,0:T(1,128)S(1)}, u32[]{:S(2)}, u32[]{:S(2)}) collective-permute-start(s32[3,1,128]{2,1,0:T(1,128)S(1)} %get-tuple-element.50), channel_id=1, source_target_pairs={{1,0},{2,1},{3,2},{4,3},{5,4},{6,5},{7,6},{9,8},{10,9},{11,10},{12... | collective-permute-start | bytes 4616 | tf_op jit(solution)/shard_map/ppermute | solution.py:178
  24.9 2.4 %copy-start.22 = (s32[9,6]{0,1:T(8,128)S(1)}, s32[9,6]{0,1:T(8,128)}, u32[]{:S(2)}) copy-start(s32[9,6]{0,1:T(8,128)} %param.13) | copy-start | bytes 652
  24.9 2.9 %copy-start.23 = (bf16[1152]{0:T(1024)(128)(2,1)S(1)}, bf16[1152]{0:T(1024)(128)(2,1)}, u32[]{:S(2)}) copy-start(bf16[1152]{0:T(1024)(128)(2,1)} %param.16) | copy-start | bytes 6916
  27.6 55.6 %copy-start.10 = (s32[1152,1]{1,0:T(8,128)}, s32[1152,1]{1,0:T(8,128)S(1)}, u32[]{:S(2)}) copy-start(s32[1152,1]{1,0:T(8,128)S(1)} %reshape.95.cluster_col) | copy-start | bytes 13828
  32.6 41.3 %collective-permute-start.13 = (bf16[6,3,128,128]{3,2,1,0:T(8,128)(2,1)}, bf16[6,3,128,128]{3,2,1,0:T(8,128)(2,1)S(1)}, u32[]{:S(2)}, u32[]{:S(2)}) collective-permute-start(bf16[6,3,128,128]{3,2,1,0:T(8,128)(2,1)} %get-tuple-element.21), channel_id=1, source_target_pairs={{8,0},{16,8},{24,16},{9,1},{17,9},{25,17},{10,2},{18,10},{26,18},{... | collective-permute-start | bytes 1769480 | tf_op jit(solution)/shard_map/ppermute | solution.py:178
  36.1 30.0 %collective-permute-start.2 = (bf16[6,3,128,128]{3,2,1,0:T(8,128)(2,1)}, bf16[6,3,128,128]{3,2,1,0:T(8,128)(2,1)S(1)}, u32[]{:S(2)}, u32[]{:S(2)}) collective-permute-start(bf16[6,3,128,128]{3,2,1,0:T(8,128)(2,1)} %get-tuple-element.28), channel_id=1, source_target_pairs={{0,1},{1,2},{2,3},{3,4},{4,5},{5,6},{6,7},{8,9},{9,10},{10,11},{11... | collective-permute-start | bytes 1769480 | tf_op jit(solution)/shard_map/ppermute | solution.py:178
  40.2 29.6 %collective-permute-start.3 = (bf16[6,3,128,128]{3,2,1,0:T(8,128)(2,1)}, bf16[6,3,128,128]{3,2,1,0:T(8,128)(2,1)S(1)}, u32[]{:S(2)}, u32[]{:S(2)}) collective-permute-start(bf16[6,3,128,128]{3,2,1,0:T(8,128)(2,1)} %get-tuple-element.27), channel_id=1, source_target_pairs={{1,0},{2,1},{3,2},{4,3},{5,4},{6,5},{7,6},{9,8},{10,9},{11,10},{12... | collective-permute-start | bytes 1769480 | tf_op jit(solution)/shard_map/ppermute | solution.py:178
  42.4 57.5 %collective-permute-start = (bf16[6,3,128,128]{3,2,1,0:T(8,128)(2,1)}, bf16[6,3,128,128]{3,2,1,0:T(8,128)(2,1)S(1)}, u32[]{:S(2)}, u32[]{:S(2)}) collective-permute-start(bf16[6,3,128,128]{3,2,1,0:T(8,128)(2,1)} %get-tuple-element.30), channel_id=1, source_target_pairs={{0,8},{8,16},{16,24},{1,9},{9,17},{17,25},{2,10},{10,18},{18,26},{... | collective-permute-start | bytes 1769480 | tf_op jit(solution)/shard_map/ppermute | solution.py:178
  66.1 11.5 %collective-permute-start.16 = (bf16[6,2,128,128]{3,2,1,0:T(8,128)(2,1)S(1)}, bf16[6,2,128,128]{3,2,1,0:T(8,128)(2,1)S(1)}, u32[]{:S(2)}, u32[]{:S(2)}) collective-permute-start(bf16[6,2,128,128]{3,2,1,0:T(8,128)(2,1)S(1)} %pad_maximum_fusion.4), channel_id=1, source_target_pairs={{0,8},{8,16},{16,24},{1,9},{9,17},{17,25},{2,10},{10,18},{18,26},{... | collective-permute-start | bytes 1179656 | tf_op jit(solution)/shard_map/ppermute | solution.py:178
  69.7 2.3 %copy-start.20 = (bf16[6,3,128,128]{3,2,1,0:T(8,128)(2,1)S(1)}, bf16[6,3,128,128]{3,2,1,0:T(8,128)(2,1)}, u32[]{:S(2)}) copy-start(bf16[6,3,128,128]{3,2,1,0:T(8,128)(2,1)} %get-tuple-element.29) | copy-start | bytes 1769476
  69.7 13.5 %copy-start.17 = (bf16[128,128]{1,0:T(8,128)(2,1)S(1)}, bf16[128,128]{1,0:T(8,128)(2,1)}, u32[]{:S(2)}) copy-start(bf16[128,128]{1,0:T(8,128)(2,1)} %w_mix.3) | copy-start | bytes 98308
  69.7 13.5 %copy-start.18 = (bf16[128,128]{1,0:T(8,128)(2,1)S(1)}, bf16[128,128]{1,0:T(8,128)(2,1)}, u32[]{:S(2)}) copy-start(bf16[128,128]{1,0:T(8,128)(2,1)} %w_coarse.3) | copy-start | bytes 98308
  69.7 13.5 %copy-start.19 = (f32[128]{0:T(128)S(1)}, f32[128]{0:T(128)}, u32[]{:S(2)}) copy-start(f32[128]{0:T(128)} %param.14) | copy-start | bytes 1540
  69.8 9.7 %collective-permute-start.17 = (bf16[6,2,128,128]{3,2,1,0:T(8,128)(2,1)S(1)}, bf16[6,2,128,128]{3,2,1,0:T(8,128)(2,1)S(1)}, u32[]{:S(2)}, u32[]{:S(2)}) collective-permute-start(bf16[6,2,128,128]{3,2,1,0:T(8,128)(2,1)S(1)} %pad_maximum_fusion.5), channel_id=1, source_target_pairs={{8,0},{16,8},{24,16},{9,1},{17,9},{25,17},{10,2},{18,10},{26,18},{... | collective-permute-start | bytes 1179656 | tf_op jit(solution)/shard_map/ppermute | solution.py:178
  72.0 29.8 %collective-permute-start.1 = (bf16[6,3,128,128]{3,2,1,0:T(8,128)(2,1)S(1)}, bf16[6,3,128,128]{3,2,1,0:T(8,128)(2,1)S(1)}, u32[]{:S(2)}, u32[]{:S(2)}) collective-permute-start(bf16[6,3,128,128]{3,2,1,0:T(8,128)(2,1)S(1)} %copy-done.20), channel_id=1, source_target_pairs={{8,0},{16,8},{24,16},{9,1},{17,9},{25,17},{10,2},{18,10},{26,18},{... | collective-permute-start | bytes 1769480 | tf_op jit(solution)/shard_map/ppermute | solution.py:178
  73.9 104.2 %collective-permute-start.20 = (s32[1,5,128]{2,1,0:T(8,128)S(1)}, s32[1,5,128]{2,1,0:T(8,128)S(1)}, u32[]{:S(2)}, u32[]{:S(2)}) collective-permute-start(s32[1,5,128]{2,1,0:T(8,128)S(1)} %get-tuple-element.47), channel_id=1, source_target_pairs={{0,8},{8,16},{16,24},{1,9},{9,17},{17,25},{2,10},{10,18},{18,26},{... | collective-permute-start | bytes 7688 | tf_op jit(solution)/shard_map/ppermute | solution.py:178
  77.6 28.2 %collective-permute-start.5 = (bf16[6,2,128,128]{3,2,1,0:T(8,128)(2,1)S(1)}, bf16[6,2,128,128]{3,2,1,0:T(8,128)(2,1)S(1)}, u32[]{:S(2)}, u32[]{:S(2)}) collective-permute-start(bf16[6,2,128,128]{3,2,1,0:T(8,128)(2,1)S(1)} %pad_maximum_fusion.1), channel_id=1, source_target_pairs={{8,0},{16,8},{24,16},{9,1},{17,9},{25,17},{10,2},{18,10},{26,18},{... | collective-permute-start | bytes 1179656 | tf_op jit(solution)/shard_map/ppermute | solution.py:178
  79.5 28.4 %collective-permute-start.4 = (bf16[6,2,128,128]{3,2,1,0:T(8,128)(2,1)S(1)}, bf16[6,2,128,128]{3,2,1,0:T(8,128)(2,1)S(1)}, u32[]{:S(2)}, u32[]{:S(2)}) collective-permute-start(bf16[6,2,128,128]{3,2,1,0:T(8,128)(2,1)S(1)} %pad_maximum_fusion), channel_id=1, source_target_pairs={{0,8},{8,16},{16,24},{1,9},{9,17},{17,25},{2,10},{10,18},{18,26},{... | collective-permute-start | bytes 1179656 | tf_op jit(solution)/shard_map/ppermute | solution.py:178
  97.3 2.5 %copy-start.1 = (bf16[6,9,128,128]{3,2,1,0:T(8,128)(2,1)}, bf16[6,9,128,128]{3,2,1,0:T(8,128)(2,1)S(1)}, u32[]{:S(2)}) copy-start(bf16[6,9,128,128]{3,2,1,0:T(8,128)(2,1)S(1)} %get-tuple-element.12.own) | copy-start | bytes 5308420
  98.6 9.4 %copy-start.11 = (s32[1152,1]{1,0:T(8,128)S(1)}, s32[1152,1]{1,0:T(8,128)}, u32[]{:S(2)}) copy-start(s32[1152,1]{1,0:T(8,128)} %copy-done.10) | copy-start | bytes 13828
  99.8 82.1 %collective-permute-start.21 = (s32[1,5,128]{2,1,0:T(8,128)S(1)}, s32[1,5,128]{2,1,0:T(8,128)S(1)}, u32[]{:S(2)}, u32[]{:S(2)}) collective-permute-start(s32[1,5,128]{2,1,0:T(8,128)S(1)} %get-tuple-element.48), channel_id=1, source_target_pairs={{8,0},{16,8},{24,16},{9,1},{17,9},{25,17},{10,2},{18,10},{26,18},{... | collective-permute-start | bytes 7688 | tf_op jit(solution)/shard_map/ppermute | solution.py:178
  101.8 41.7 %collective-permute-start.24 = (bf16[6,3,128,128]{3,2,1,0:T(8,128)(2,1)}, bf16[6,3,128,128]{3,2,1,0:T(8,128)(2,1)S(1)}, u32[]{:S(2)}, u32[]{:S(2)}) collective-permute-start(bf16[6,3,128,128]{3,2,1,0:T(8,128)(2,1)} %get-tuple-element.16), channel_id=1, source_target_pairs={{0,1},{1,2},{2,3},{3,4},{4,5},{5,6},{6,7},{8,9},{9,10},{10,11},{11... | collective-permute-start | bytes 1769480 | tf_op jit(solution)/shard_map/ppermute | solution.py:178
  105.8 40.9 %collective-permute-start.25 = (bf16[6,3,128,128]{3,2,1,0:T(8,128)(2,1)}, bf16[6,3,128,128]{3,2,1,0:T(8,128)(2,1)S(1)}, u32[]{:S(2)}, u32[]{:S(2)}) collective-permute-start(bf16[6,3,128,128]{3,2,1,0:T(8,128)(2,1)} %get-tuple-element.15), channel_id=1, source_target_pairs={{1,0},{2,1},{3,2},{4,3},{5,4},{6,5},{7,6},{9,8},{10,9},{11,10},{12... | collective-permute-start | bytes 1769480 | tf_op jit(solution)/shard_map/ppermute | solution.py:178
  122.1 8.0 %copy-start = (bf16[6,9,128,128]{3,2,1,0:T(8,128)(2,1)}, bf16[6,9,128,128]{3,2,1,0:T(8,128)(2,1)S(1)}, u32[]{:S(2)}) copy-start(bf16[6,9,128,128]{3,2,1,0:T(8,128)(2,1)S(1)} %get-tuple-element.9.own) | copy-start | bytes 5308420
  123.1 15.6 %all-to-all-start = ((f32[32,12,128]{2,1,0:T(8,128)}), f32[32,12,128]{2,1,0:T(8,128)S(1)}, u32[]{:S(2)}, u32[]{:S(2)}) async-start(f32[32,12,128]{2,1,0:T(8,128)} %copy.81), calls=%async_computation | async-start | bytes 524288 | tf_op jit(solution)/shard_map/all_to_all | solution.py:282
  131.2 52.7 %collective-permute-start.22 = (bf16[6,3,128,128]{3,2,1,0:T(8,128)(2,1)}, bf16[6,3,128,128]{3,2,1,0:T(8,128)(2,1)}, u32[]{:S(2)}, u32[]{:S(2)}) collective-permute-start(bf16[6,3,128,128]{3,2,1,0:T(8,128)(2,1)} %get-tuple-element.18), channel_id=1, source_target_pairs={{0,8},{8,16},{16,24},{1,9},{9,17},{17,25},{2,10},{10,18},{18,26},{... | collective-permute-start | bytes 1769480 | tf_op jit(solution)/shard_map/ppermute | solution.py:178
  139.5 58.6 %all-to-all-start.1 = ((bf16[32,12,128]{2,1,0:T(8,128)(2,1)}), bf16[32,12,128]{2,1,0:T(8,128)(2,1)}, u32[]{:S(2)}, u32[]{:S(2)}) async-start(bf16[32,12,128]{2,1,0:T(8,128)(2,1)} %broadcast_in_dim.24), calls=%async_computation.1 | async-start | bytes 262144 | tf_op jit(solution)/shard_map/all_to_all | solution.py:290
  143.5 33.9 %copy-start.2 = (bf16[6,3,128,128]{3,2,1,0:T(8,128)(2,1)}, bf16[6,3,128,128]{3,2,1,0:T(8,128)(2,1)S(1)}, u32[]{:S(2)}) copy-start(bf16[6,3,128,128]{3,2,1,0:T(8,128)(2,1)S(1)} %collective-permute-done.24.ry_lo) | copy-start | bytes 1769476
  143.5 28.9 %collective-permute-start.8 = (bf16[6,3,128,128]{3,2,1,0:T(8,128)(2,1)}, bf16[6,3,128,128]{3,2,1,0:T(8,128)(2,1)S(1)}, u32[]{:S(2)}, u32[]{:S(2)}) collective-permute-start(bf16[6,3,128,128]{3,2,1,0:T(8,128)(2,1)} %get-tuple-element.24), channel_id=1, source_target_pairs={{0,1},{1,2},{2,3},{3,4},{4,5},{5,6},{6,7},{8,9},{9,10},{10,11},{11... | collective-permute-start | bytes 1769480 | tf_op jit(solution)/shard_map/ppermute | solution.py:178
  146.7 31.5 %copy-start.4 = (bf16[6,3,128,128]{3,2,1,0:T(8,128)(2,1)}, bf16[6,3,128,128]{3,2,1,0:T(8,128)(2,1)S(1)}, u32[]{:S(2)}) copy-start(bf16[6,3,128,128]{3,2,1,0:T(8,128)(2,1)S(1)} %collective-permute-done.25.ry_hi) | copy-start | bytes 1769476
  146.7 28.7 %collective-permute-start.9 = (bf16[6,3,128,128]{3,2,1,0:T(8,128)(2,1)}, bf16[6,3,128,128]{3,2,1,0:T(8,128)(2,1)S(1)}, u32[]{:S(2)}, u32[]{:S(2)}) collective-permute-start(bf16[6,3,128,128]{3,2,1,0:T(8,128)(2,1)} %get-tuple-element.23), channel_id=1, source_target_pairs={{1,0},{2,1},{3,2},{4,3},{5,4},{6,5},{7,6},{9,8},{10,9},{11,10},{12... | collective-permute-start | bytes 1769480 | tf_op jit(solution)/shard_map/ppermute | solution.py:178
  172.4 16.8 %collective-permute-start.23 = (bf16[6,3,128,128]{3,2,1,0:T(8,128)(2,1)}, bf16[6,3,128,128]{3,2,1,0:T(8,128)(2,1)S(1)}, u32[]{:S(2)}, u32[]{:S(2)}) collective-permute-start(bf16[6,3,128,128]{3,2,1,0:T(8,128)(2,1)} %get-tuple-element.17), channel_id=1, source_target_pairs={{8,0},{16,8},{24,16},{9,1},{17,9},{25,17},{10,2},{18,10},{26,18},{... | collective-permute-start | bytes 1769480 | tf_op jit(solution)/shard_map/ppermute | solution.py:178
  175.3 2.0 copy-start.6
  175.3 16.6 %collective-permute-start.27 = (bf16[6,2,128,128]{3,2,1,0:T(8,128)(2,1)S(1)}, bf16[6,2,128,128]{3,2,1,0:T(8,128)(2,1)S(1)}, u32[]{:S(2)}, u32[]{:S(2)}) collective-permute-start(bf16[6,2,128,128]{3,2,1,0:T(8,128)(2,1)S(1)} %pad_maximum_fusion.7), channel_id=1, source_target_pairs={{8,0},{16,8},{24,16},{9,1},{17,9},{25,17},{10,2},{18,10},{26,18},{... | collective-permute-start | bytes 1179656 | tf_op jit(solution)/shard_map/ppermute | solution.py:178
  178.1 20.9 %copy-start.3 = (bf16[6,3,128,128]{3,2,1,0:T(8,128)(2,1)S(1)}, bf16[6,3,128,128]{3,2,1,0:T(8,128)(2,1)}, u32[]{:S(2)}) copy-start(bf16[6,3,128,128]{3,2,1,0:T(8,128)(2,1)} %copy-done.2) | copy-start | bytes 1769476
  178.1 20.9 %copy-start.14 = (bf16[128,128]{1,0:T(8,128)(2,1)S(1)}, bf16[128,128]{1,0:T(8,128)(2,1)}, u32[]{:S(2)}) copy-start(bf16[128,128]{1,0:T(8,128)(2,1)} %w_region.3) | copy-start | bytes 98308
  178.1 20.9 %copy-start.15 = (bf16[128,128]{1,0:T(8,128)(2,1)S(1)}, bf16[128,128]{1,0:T(8,128)(2,1)}, u32[]{:S(2)}) copy-start(bf16[128,128]{1,0:T(8,128)(2,1)} %w_out.3) | copy-start | bytes 98308
  178.1 20.9 %copy-start.5 = (bf16[6,3,128,128]{3,2,1,0:T(8,128)(2,1)S(1)}, bf16[6,3,128,128]{3,2,1,0:T(8,128)(2,1)}, u32[]{:S(2)}) copy-start(bf16[6,3,128,128]{3,2,1,0:T(8,128)(2,1)} %copy-done.4) | copy-start | bytes 1769476
  178.2 36.1 %collective-permute-start.6 = (bf16[6,3,128,128]{3,2,1,0:T(8,128)(2,1)}, bf16[6,3,128,128]{3,2,1,0:T(8,128)(2,1)}, u32[]{:S(2)}, u32[]{:S(2)}) collective-permute-start(bf16[6,3,128,128]{3,2,1,0:T(8,128)(2,1)} %get-tuple-element.26), channel_id=1, source_target_pairs={{0,8},{8,16},{16,24},{1,9},{9,17},{17,25},{2,10},{10,18},{18,26},{... | collective-permute-start | bytes 1769480 | tf_op jit(solution)/shard_map/ppermute | solution.py:178
  181.9 32.3 %collective-permute-start.7 = (bf16[6,3,128,128]{3,2,1,0:T(8,128)(2,1)}, bf16[6,3,128,128]{3,2,1,0:T(8,128)(2,1)}, u32[]{:S(2)}, u32[]{:S(2)}) collective-permute-start(bf16[6,3,128,128]{3,2,1,0:T(8,128)(2,1)} %get-tuple-element.25), channel_id=1, source_target_pairs={{8,0},{16,8},{24,16},{9,1},{17,9},{25,17},{10,2},{18,10},{26,18},{... | collective-permute-start | bytes 1769480 | tf_op jit(solution)/shard_map/ppermute | solution.py:178
  183.9 15.1 %collective-permute-start.26 = (bf16[6,2,128,128]{3,2,1,0:T(8,128)(2,1)}, bf16[6,2,128,128]{3,2,1,0:T(8,128)(2,1)}, u32[]{:S(2)}, u32[]{:S(2)}) collective-permute-start(bf16[6,2,128,128]{3,2,1,0:T(8,128)(2,1)} %pad_maximum_fusion.6), channel_id=1, source_target_pairs={{0,8},{8,16},{16,24},{1,9},{9,17},{17,25},{2,10},{10,18},{18,26},{... | collective-permute-start | bytes 1179656 | tf_op jit(solution)/shard_map/ppermute | solution.py:178
  189.2 0.8 copy-start.8
  190.0 24.2 %collective-permute-start.11 = (bf16[6,2,128,128]{3,2,1,0:T(8,128)(2,1)}, bf16[6,2,128,128]{3,2,1,0:T(8,128)(2,1)}, u32[]{:S(2)}, u32[]{:S(2)}) collective-permute-start(bf16[6,2,128,128]{3,2,1,0:T(8,128)(2,1)} %pad_maximum_fusion.3), channel_id=1, source_target_pairs={{8,0},{16,8},{24,16},{9,1},{17,9},{25,17},{10,2},{18,10},{26,18},{... | collective-permute-start | bytes 1179656 | tf_op jit(solution)/shard_map/ppermute | solution.py:178
  191.9 0.8 copy-start.12
  192.7 21.5 %collective-permute-start.10 = (bf16[6,2,128,128]{3,2,1,0:T(8,128)(2,1)}, bf16[6,2,128,128]{3,2,1,0:T(8,128)(2,1)}, u32[]{:S(2)}, u32[]{:S(2)}) collective-permute-start(bf16[6,2,128,128]{3,2,1,0:T(8,128)(2,1)} %pad_maximum_fusion.2), channel_id=1, source_target_pairs={{0,8},{8,16},{16,24},{1,9},{9,17},{17,25},{2,10},{10,18},{18,26},{... | collective-permute-start | bytes 1179656 | tf_op jit(solution)/shard_map/ppermute | solution.py:178
  199.0 1.1 copy-start.9
  200.1 1.0 copy-start.13
  201.1 13.1 %copy-start.7 = (bf16[6,3,128,128]{3,2,1,0:T(8,128)(2,1)S(1)}, bf16[6,3,128,128]{3,2,1,0:T(8,128)(2,1)}, u32[]{:S(2)}) copy-start(bf16[6,3,128,128]{3,2,1,0:T(8,128)(2,1)} %copy-done.6) | copy-start | bytes 1769476

commit v3 on v2

--- a/solution.py
+++ b/solution.py
@@ -178,14 +178,20 @@
     return lax.ppermute(value, axis, pairs)
 
 
-def halo(field):
+def nothing(*arrays):
+    return sum(array.reshape(-1)[0].astype(jnp.float32) * 0.0 for array in arrays)
+
+
+def halo(field, gate=None):
     steps = field.shape[0]
     square = field.reshape(steps, GB, GB, BLK, BLK)
-
-    ry_lo = shifted(square[:, :, GB - 1], "ry", True)
-    ry_hi = shifted(square[:, :, 0], "ry", False)
-    rx_lo = shifted(square[:, GB - 1], "rx", True)
-    rx_hi = shifted(square[:, 0], "rx", False)
+    sends = [square[:, :, GB - 1], square[:, :, 0], square[:, GB - 1], square[:, 0]]
+    if gate is not None:
+        sends = [(send.astype(jnp.float32) + gate).astype(send.dtype) for send in sends]
+    ry_lo = shifted(sends[0], "ry", True)
+    ry_hi = shifted(sends[1], "ry", False)
+    rx_lo = shifted(sends[2], "rx", True)
+    rx_hi = shifted(sends[3], "rx", False)
     co_lo = shifted(jnp.stack([ry_lo[:, GB - 1], ry_hi[:, GB - 1]], axis=1), "rx", True)
     co_hi = shifted(jnp.stack([ry_lo[:, 0], ry_hi[:, 0]], axis=1), "rx", False)
     return rx_lo, rx_hi, ry_lo, ry_hi, co_lo, co_hi
@@ -224,15 +230,6 @@
         ),
         axis=1,
     )
-    marks = (owner_of + 1).reshape(GB, GB, BLK)
-    marks = jnp.concatenate(
-        [shifted(marks[:, -1:], "ry", True), marks, shifted(marks[:, :1], "ry", False)], axis=1
-    )
-    marks = jnp.concatenate(
-        [shifted(marks[-1:], "rx", True), marks, shifted(marks[:1], "rx", False)], axis=0
-    )
-    owner_ext = (marks - 1).reshape(SIDE * SIDE * BLK, 1)
-
     chunk = steps_count // CHUNKS
     per = LANES_STEPS
     grid = chunk // per
@@ -245,7 +242,10 @@
     params = pltpu.CompilerParams(vmem_limit_bytes=48 * 1024 * 1024)
     cost = pl.CostEstimate(flops=5_000_000_000 // CHUNKS, bytes_accessed=16_000_000 // CHUNKS, transcendentals=0)
 
-    first = [halo(noisy[c * chunk : (c + 1) * chunk]) for c in range(CHUNKS)]
+    first = []
+    for c in range(CHUNKS):
+        gate = nothing(*first[-1][2:4]) if first else None
+        first.append(halo(noisy[c * chunk : (c + 1) * chunk], gate))
     fields, sums, second = [], [], []
     for c in range(CHUNKS):
         constants = (
@@ -279,8 +279,18 @@
         fields.append(u)
         sums.append(partial)
         second.append(halo(u))
+    marks = (owner_of + 1).reshape(GB, GB, BLK) + nothing(sums[0]).astype(jnp.int32)
+    marks = jnp.concatenate(
+        [shifted(marks[:, -1:], "ry", True), marks, shifted(marks[:, :1], "ry", False)], axis=1
+    )
+    marks = jnp.concatenate(
+        [shifted(marks[-1:], "rx", True), marks, shifted(marks[:1], "rx", False)], axis=0
+    )
+    owner_ext = (marks - 1).reshape(SIDE * SIDE * BLK, 1)
+
+    gate = nothing(*second[0][4:6])
     mine = lax.all_to_all(
-        jnp.concatenate(sums, axis=0).transpose(1, 0, 2),
+        jnp.concatenate(sums, axis=0).transpose(1, 0, 2) + gate,
         ("rx", "ry"),
         split_axis=0,
         concat_axis=0,

time: 230 us -> 203 us (0.88)
  waiting for transfers between devices: 51.7 us -> 18.9 us
  starting transfers between devices: 94 us -> 89 us
  other arithmetic: 2.92 us -> 7.68 us
  between operations: 0.87 us -> 4.1 us
  local copies, waits for them, and re-layouts: 23.5 us -> 26.5 us
    ppermute x28, waiting for transfers between devices: 47.5 us -> 16.7 us  [shifted(): return lax.ppermute(value, axis, pairs)]
    squeeze x8 -> x6, local copies, waits for them, and re-layouts: 11.6 us -> 5.57 us  [the longest x3 3.18 us: halo(): square[:, 0]]
    unnamed x48 -> x90, local copies, waits for them, and re-layouts: 3.7 us -> 7.49 us
    ppermute x28, starting transfers between devices: 84.2 us -> 81 us  [shifted(): return lax.ppermute(value, axis, pairs)]
    convert_element_type x0 -> x2, other arithmetic: none -> 2.86 us  [halo(): (send.astype(jnp.float32) + gate).astype(send.dtype)]
    slice x1 -> x6, local copies, waits for them, and re-layouts: 3.44 us -> 6.13 us  [the longest x1 3.44 us: on_device(): first.append(halo(noisy[c * chunk:(c + 1) * chunk], gate))]
  transfers between devices with their start and end apart: 30 -> 30, of which waited for: 4 -> 4; matrix products, arithmetic and copies ran while one was open for 8% -> 11% of each run, Pallas kernels for 18% -> 21%
where the time goes in v3:
time: 203 us; the launch traced here: 201 us
  starting transfers between devices  89 us (44%)
  Pallas kernels  54.6 us (27%)
  local copies, waits for them, and re-layouts  26.5 us (13%)
  waiting for transfers between devices  18.9 us (9%)
  other arithmetic  7.68 us (4%)
  between operations  4.1 us (2%)
    ppermute x28, starting transfers between devices, shifted(): return lax.ppermute(value, axis, pairs)  81 us
    pallas_call x2, Pallas kernels, on_device(): pl.pallas_call(encode_kernel, grid_spec=pltpu.PrefetchScalarGridSpec(num_...  28.5 us
    pallas_call x2, Pallas kernels, on_device(): pl.pallas_call(decode_kernel, grid_spec=pltpu.PrefetchScalarGridSpec(num_...  26.2 us
    ppermute x28, waiting for transfers between devices, shifted(): return lax.ppermute(value, axis, pairs)  16.7 us
    unnamed x90, local copies, waits for them, and re-layouts  7.49 us
    all_to_all x1, starting transfers between devices, on_device(): lax.all_to_all(jnp.broadcast_to(own_region[None], (devices, steps_count,...  4.1 us
  transfers between devices with their start and end apart: 30, of which 4 were waited for; matrix products, arithmetic and copies ran while one was open for 11% of the time, Pallas kernels for 21%

profile of v3, /device:TPU:9, one launch (start us, length us, event | category | flops | bytes accessed | tf_op | source)
XLA Modules:
  0.0 200.8 jit_solution(7997497100423643501)
XLA Ops:
  0.0 3.4 %fusion.10 = (bf16[6,1152,128]{2,1,0:T(8,128)(2,1)S(1)}, bf16[6,1152,128]{2,1,0:T(8,128)(2,1)}) fusion(bf16[12,1152,128]{2,1,0:T(8,128)(2,1)} %bitcast.118), kind=kLoop, calls=%fused_computation.57 | loop fusion | bytes 7077888 | tf_op jit(solution)/shard_map/slice | solution.py:248
  3.4 1.1 slice_bitcast_fusion.13
  4.6 3.3 %collective-permute-start = (bf16[6,3,128,128]{3,2,1,0:T(8,128)(2,1)}, bf16[6,3,128,128]{3,2,1,0:T(8,128)(2,1)S(1)}, u32[]{:S(2)}, u32[]{:S(2)}) collective-permute-start(bf16[6,3,128,128]{3,2,1,0:T(8,128)(2,1)} %get-tuple-element.30), channel_id=1, source_target_pairs={{0,1},{1,2},{2,3},{3,4},{4,5},{5,6},{6,7},{8,9},{9,10},{10,11},{11... | collective-permute-start | bytes 1769480 | tf_op jit(solution)/shard_map/ppermute | solution.py:178
  7.8 3.0 %collective-permute-start.1 = (bf16[6,3,128,128]{3,2,1,0:T(8,128)(2,1)}, bf16[6,3,128,128]{3,2,1,0:T(8,128)(2,1)S(1)}, u32[]{:S(2)}, u32[]{:S(2)}) collective-permute-start(bf16[6,3,128,128]{3,2,1,0:T(8,128)(2,1)} %get-tuple-element.29), channel_id=1, source_target_pairs={{1,0},{2,1},{3,2},{4,3},{5,4},{6,5},{7,6},{9,8},{10,9},{11,10},{12... | collective-permute-start | bytes 1769480 | tf_op jit(solution)/shard_map/ppermute | solution.py:178
  10.9 0.9 slice_bitcast_fusion.4
  11.8 4.2 %collective-permute-start.14 = (bf16[6,3,128,128]{3,2,1,0:T(8,128)(2,1)S(1)}, bf16[6,3,128,128]{3,2,1,0:T(8,128)(2,1)S(1)}, u32[]{:S(2)}, u32[]{:S(2)}) collective-permute-start(bf16[6,3,128,128]{3,2,1,0:T(8,128)(2,1)S(1)} %get-tuple-element.20), channel_id=1, source_target_pairs={{0,8},{8,16},{16,24},{1,9},{9,17},{17,25},{2,10},{10,18},{18,26},{... | collective-permute-start | bytes 1769480 | tf_op jit(solution)/shard_map/ppermute | solution.py:178
  16.0 1.9 collective-permute-start.15
  18.4 0.8 reshape.149.weight_row
  19.3 0.9 select_reduce_fusion
  20.1 12.6 %collective-permute-done.ry_lo = bf16[6,3,128,128]{3,2,1,0:T(8,128)(2,1)S(1)} collective-permute-done((bf16[6,3,128,128]{3,2,1,0:T(8,128)(2,1)}, bf16[6,3,128,128]{3,2,1,0:T(8,128)(2,1)S(1)}, u32[]{:S(2)}, u32[]{:S(2)}) %collective-permute-start) | collective-permute-done | bytes 589856 | tf_op jit(solution)/shard_map/ppermute | solution.py:178
  32.8 2.8 %collective-permute-done.1.ry_hi = bf16[6,3,128,128]{3,2,1,0:T(8,128)(2,1)S(1)} collective-permute-done((bf16[6,3,128,128]{3,2,1,0:T(8,128)(2,1)}, bf16[6,3,128,128]{3,2,1,0:T(8,128)(2,1)S(1)}, u32[]{:S(2)}, u32[]{:S(2)}) %collective-permute-start.1) | collective-permute-done | bytes 589856 | tf_op jit(solution)/shard_map/ppermute | solution.py:178
  35.7 3.5 %collective-permute-start.16 = (bf16[6,2,128,128]{3,2,1,0:T(8,128)(2,1)S(1)}, bf16[6,2,128,128]{3,2,1,0:T(8,128)(2,1)S(1)}, u32[]{:S(2)}, u32[]{:S(2)}) collective-permute-start(bf16[6,2,128,128]{3,2,1,0:T(8,128)(2,1)S(1)} %pad_maximum_fusion.4), channel_id=1, source_target_pairs={{0,8},{8,16},{16,24},{1,9},{9,17},{17,25},{2,10},{10,18},{18,26},{... | collective-permute-start | bytes 1179656 | tf_op jit(solution)/shard_map/ppermute | solution.py:178
  39.2 1.9 collective-permute-start.17
  43.5 1.4 fusion.3
  45.0 2.4 %collective-permute-start.4 = (bf16[6,3,128,128]{3,2,1,0:T(8,128)(2,1)}, bf16[6,3,128,128]{3,2,1,0:T(8,128)(2,1)S(1)}, u32[]{:S(2)}, u32[]{:S(2)}) collective-permute-start(bf16[6,3,128,128]{3,2,1,0:T(8,128)(2,1)} %get-tuple-element.26), channel_id=1, source_target_pairs={{0,1},{1,2},{2,3},{3,4},{4,5},{5,6},{6,7},{8,9},{9,10},{10,11},{11... | collective-permute-start | bytes 1769480 | tf_op jit(solution)/shard_map/ppermute | solution.py:178
  47.4 1.4 fusion.1
  48.8 0.8 copy-done.32
  49.6 3.9 %collective-permute-start.5 = (bf16[6,3,128,128]{3,2,1,0:T(8,128)(2,1)}, bf16[6,3,128,128]{3,2,1,0:T(8,128)(2,1)S(1)}, u32[]{:S(2)}, u32[]{:S(2)}) collective-permute-start(bf16[6,3,128,128]{3,2,1,0:T(8,128)(2,1)} %get-tuple-element.25), channel_id=1, source_target_pairs={{1,0},{2,1},{3,2},{4,3},{5,4},{6,5},{7,6},{9,8},{10,9},{11,10},{12... | collective-permute-start | bytes 1769480 | tf_op jit(solution)/shard_map/ppermute | solution.py:178
  53.5 4.2 %collective-permute-start.2 = (bf16[6,3,128,128]{3,2,1,0:T(8,128)(2,1)}, bf16[6,3,128,128]{3,2,1,0:T(8,128)(2,1)}, u32[]{:S(2)}, u32[]{:S(2)}) collective-permute-start(bf16[6,3,128,128]{3,2,1,0:T(8,128)(2,1)} %get-tuple-element.28), channel_id=1, source_target_pairs={{0,8},{8,16},{16,24},{1,9},{9,17},{17,25},{2,10},{10,18},{18,26},{... | collective-permute-start | bytes 1769480 | tf_op jit(solution)/shard_map/ppermute | solution.py:178
  57.8 1.9 collective-permute-start.3
  59.8 1.1 copy-done.33
  60.8 14.1 %encode.3 = (bf16[6,9,128,128]{3,2,1,0:T(8,128)(2,1)S(1)}, f32[6,32,128]{2,1,0:T(8,128)S(1)}) custom-call(s32[54]{0:T(128)S(1)} %reshape.131.index, bf16[12,9,128,128]{3,2,1,0:T(8,128)(2,1)} %bitcast.119, bf16[6,3,128,128]{3,2,1,0:T(8,128)(2,1)S(1)} %copy-done.33, bf16[6,3,128,128]{3,2,1,0:T(8,128)(2,1)} %collective-permute-done.15.rx_hi, ...), custom_call_target="tpu_custom_call" | custom-call | flops 2500000000 | bytes 8000000 | tf_op jit(solution)/shard_map/encode/pallas_call | solution.py:254
  77.6 2.1 %collective-permute-start.7 = (bf16[6,2,128,128]{3,2,1,0:T(8,128)(2,1)S(1)}, bf16[6,2,128,128]{3,2,1,0:T(8,128)(2,1)S(1)}, u32[]{:S(2)}, u32[]{:S(2)}) collective-permute-start(bf16[6,2,128,128]{3,2,1,0:T(8,128)(2,1)S(1)} %pad_maximum_fusion.1), channel_id=1, source_target_pairs={{8,0},{16,8},{24,16},{9,1},{17,9},{25,17},{10,2},{18,10},{26,18},{... | collective-permute-start | bytes 1179656 | tf_op jit(solution)/shard_map/ppermute | solution.py:178
  79.8 3.6 %collective-permute-start.6 = (bf16[6,2,128,128]{3,2,1,0:T(8,128)(2,1)S(1)}, bf16[6,2,128,128]{3,2,1,0:T(8,128)(2,1)S(1)}, u32[]{:S(2)}, u32[]{:S(2)}) collective-permute-start(bf16[6,2,128,128]{3,2,1,0:T(8,128)(2,1)S(1)} %pad_maximum_fusion), channel_id=1, source_target_pairs={{0,8},{8,16},{16,24},{1,9},{9,17},{17,25},{2,10},{10,18},{18,26},{... | collective-permute-start | bytes 1179656 | tf_op jit(solution)/shard_map/ppermute | solution.py:178
  83.5 1.9 collective-permute-start.18
  85.5 4.4 %collective-permute-start.22 = (s32[3,1,128]{2,1,0:T(1,128)S(1)}, s32[3,1,128]{2,1,0:T(1,128)S(1)}, u32[]{:S(2)}, u32[]{:S(2)}) collective-permute-start(s32[3,1,128]{2,1,0:T(1,128)S(1)} %get-tuple-element.49), channel_id=1, source_target_pairs={{0,1},{1,2},{2,3},{3,4},{4,5},{5,6},{6,7},{8,9},{9,10},{10,11},{11... | collective-permute-start | bytes 4616 | tf_op jit(solution)/shard_map/ppermute | solution.py:178
  89.9 1.9 collective-permute-start.23
  91.8 3.3 %collective-permute-start.19 = (bf16[6,3,128,128]{3,2,1,0:T(8,128)(2,1)S(1)}, bf16[6,3,128,128]{3,2,1,0:T(8,128)(2,1)S(1)}, u32[]{:S(2)}, u32[]{:S(2)}) collective-permute-start(bf16[6,3,128,128]{3,2,1,0:T(8,128)(2,1)S(1)} %get-tuple-element.18), channel_id=1, source_target_pairs={{1,0},{2,1},{3,2},{4,3},{5,4},{6,5},{7,6},{9,8},{10,9},{11,10},{12... | collective-permute-start | bytes 1769480 | tf_op jit(solution)/shard_map/ppermute | solution.py:178
  95.1 1.1 copy-done.18
  96.2 1.1 copy-done.20
  97.3 14.3 %encode.2 = (bf16[6,9,128,128]{3,2,1,0:T(8,128)(2,1)S(1)}, f32[6,32,128]{2,1,0:T(8,128)S(1)}) custom-call(s32[54]{0:T(128)S(1)} %reshape.131.index, bf16[12,9,128,128]{3,2,1,0:T(8,128)(2,1)} %bitcast.120, bf16[6,3,128,128]{3,2,1,0:T(8,128)(2,1)} %collective-permute-done.2.rx_lo, bf16[6,3,128,128]{3,2,1,0:T(8,128)(2,1)} %collective-permute-done.3.rx_hi, ...), custom_call_target="tpu_custom_call" | custom-call | flops 2500000000 | bytes 8000000 | tf_op jit(solution)/shard_map/encode/pallas_call | solution.py:254
  111.6 1.2 slice_bitcast_fusion.6
  112.8 2.1 %collective-permute-start.10 = (bf16[6,3,128,128]{3,2,1,0:T(8,128)(2,1)}, bf16[6,3,128,128]{3,2,1,0:T(8,128)(2,1)S(1)}, u32[]{:S(2)}, u32[]{:S(2)}) collective-permute-start(bf16[6,3,128,128]{3,2,1,0:T(8,128)(2,1)} %get-tuple-element.22), channel_id=1, source_target_pairs={{0,1},{1,2},{2,3},{3,4},{4,5},{5,6},{6,7},{8,9},{9,10},{10,11},{11... | collective-permute-start | bytes 1769480 | tf_op jit(solution)/shard_map/ppermute | solution.py:178
  115.1 1.9 collective-permute-start.21
  117.1 3.6 %collective-permute-start.20 = (bf16[6,2,128,128]{3,2,1,0:T(8,128)(2,1)S(1)}, bf16[6,2,128,128]{3,2,1,0:T(8,128)(2,1)S(1)}, u32[]{:S(2)}, u32[]{:S(2)}) collective-permute-start(bf16[6,2,128,128]{3,2,1,0:T(8,128)(2,1)S(1)} %pad_maximum_fusion.6), channel_id=1, source_target_pairs={{0,8},{8,16},{16,24},{1,9},{9,17},{17,25},{2,10},{10,18},{18,26},{... | collective-permute-start | bytes 1179656 | tf_op jit(solution)/shard_map/ppermute | solution.py:178
  120.8 1.1 slice_bitcast_fusion
  121.9 2.5 %collective-permute-start.26 = (bf16[6,3,128,128]{3,2,1,0:T(8,128)(2,1)}, bf16[6,3,128,128]{3,2,1,0:T(8,128)(2,1)}, u32[]{:S(2)}, u32[]{:S(2)}) collective-permute-start(bf16[6,3,128,128]{3,2,1,0:T(8,128)(2,1)} %get-tuple-element.16), channel_id=1, source_target_pairs={{0,8},{8,16},{16,24},{1,9},{9,17},{17,25},{2,10},{10,18},{18,26},{... | collective-permute-start | bytes 1769480 | tf_op jit(solution)/shard_map/ppermute | solution.py:178
  124.4 4.4 %collective-permute-start.11 = (bf16[6,3,128,128]{3,2,1,0:T(8,128)(2,1)}, bf16[6,3,128,128]{3,2,1,0:T(8,128)(2,1)S(1)}, u32[]{:S(2)}, u32[]{:S(2)}) collective-permute-start(bf16[6,3,128,128]{3,2,1,0:T(8,128)(2,1)} %get-tuple-element.21), channel_id=1, source_target_pairs={{1,0},{2,1},{3,2},{4,3},{5,4},{6,5},{7,6},{9,8},{10,9},{11,10},{12... | collective-permute-start | bytes 1769480 | tf_op jit(solution)/shard_map/ppermute | solution.py:178
  128.8 1.1 slice_bitcast_fusion.8
  130.0 3.0 %collective-permute-start.27 = (bf16[6,3,128,128]{3,2,1,0:T(8,128)(2,1)}, bf16[6,3,128,128]{3,2,1,0:T(8,128)(2,1)S(1)}, u32[]{:S(2)}, u32[]{:S(2)}) collective-permute-start(bf16[6,3,128,128]{3,2,1,0:T(8,128)(2,1)} %get-tuple-element.15), channel_id=1, source_target_pairs={{8,0},{16,8},{24,16},{9,1},{17,9},{25,17},{10,2},{18,10},{26,18},{... | collective-permute-start | bytes 1769480 | tf_op jit(solution)/shard_map/ppermute | solution.py:178
  133.5 2.6 %collective-permute-start.24 = (s32[1,5,128]{2,1,0:T(8,128)S(1)}, s32[1,5,128]{2,1,0:T(8,128)S(1)}, u32[]{:S(2)}, u32[]{:S(2)}) collective-permute-start(s32[1,5,128]{2,1,0:T(8,128)S(1)} %get-tuple-element.47), channel_id=1, source_target_pairs={{0,8},{8,16},{16,24},{1,9},{9,17},{17,25},{2,10},{10,18},{18,26},{... | collective-permute-start | bytes 7688 | tf_op jit(solution)/shard_map/ppermute | solution.py:178
  136.6 0.7 copy-done.15
  138.5 0.8 copy.83
  139.4 4.0 %all-to-all-start = ((f32[32,12,128]{2,1,0:T(8,128)}), f32[32,12,128]{2,1,0:T(8,128)}, u32[]{:S(2)}, u32[]{:S(2)}) async-start(f32[32,12,128]{2,1,0:T(8,128)} %copy.83), calls=%async_computation | async-start | bytes 524288 | tf_op jit(solution)/shard_map/all_to_all | solution.py:292
  143.4 3.5 %collective-permute-start.8 = (bf16[6,3,128,128]{3,2,1,0:T(8,128)(2,1)}, bf16[6,3,128,128]{3,2,1,0:T(8,128)(2,1)}, u32[]{:S(2)}, u32[]{:S(2)}) collective-permute-start(bf16[6,3,128,128]{3,2,1,0:T(8,128)(2,1)} %get-tuple-element.24), channel_id=1, source_target_pairs={{0,8},{8,16},{16,24},{1,9},{9,17},{17,25},{2,10},{10,18},{18,26},{... | collective-permute-start | bytes 1769480 | tf_op jit(solution)/shard_map/ppermute | solution.py:178
  146.8 0.7 fusion.15
  147.6 1.9 collective-permute-start.9
  149.5 0.7 fusion.16
  150.2 0.8 pad_maximum_fusion.3
  151.0 2.2 %all-to-all-done = f32[32,12,128]{2,1,0:T(8,128)} async-done(((f32[32,12,128]{2,1,0:T(8,128)}), f32[32,12,128]{2,1,0:T(8,128)}, u32[]{:S(2)}, u32[]{:S(2)}) %all-to-all-start) | async-done | bytes 196640 | tf_op jit(solution)/shard_map/all_to_all | solution.py:292
  153.2 1.0 reduce_sum.18
  154.2 0.7 broadcast_in_dim.24
  154.8 4.1 %all-to-all-start.1 = ((bf16[32,12,128]{2,1,0:T(8,128)(2,1)}), bf16[32,12,128]{2,1,0:T(8,128)(2,1)}, u32[]{:S(2)}, u32[]{:S(2)}) async-start(bf16[32,12,128]{2,1,0:T(8,128)(2,1)} %broadcast_in_dim.24), calls=%async_computation.1 | async-start | bytes 262144 | tf_op jit(solution)/shard_map/all_to_all | solution.py:300
  159.0 2.3 %collective-permute-start.25 = (s32[1,5,128]{2,1,0:T(8,128)S(1)}, s32[1,5,128]{2,1,0:T(8,128)S(1)}, u32[]{:S(2)}, u32[]{:S(2)}) collective-permute-start(s32[1,5,128]{2,1,0:T(8,128)S(1)} %get-tuple-element.48), channel_id=1, source_target_pairs={{8,0},{16,8},{24,16},{9,1},{17,9},{25,17},{10,2},{18,10},{26,18},{... | collective-permute-start | bytes 7688 | tf_op jit(solution)/shard_map/ppermute | solution.py:178
  161.2 1.9 pad_maximum_fusion.2
  163.1 1.2 collective-permute-done.25
  164.3 1.9 collective-permute-start.13
  166.2 3.8 %collective-permute-start.12 = (bf16[6,2,128,128]{3,2,1,0:T(8,128)(2,1)}, bf16[6,2,128,128]{3,2,1,0:T(8,128)(2,1)}, u32[]{:S(2)}, u32[]{:S(2)}) collective-permute-start(bf16[6,2,128,128]{3,2,1,0:T(8,128)(2,1)} %pad_maximum_fusion.2), channel_id=1, source_target_pairs={{0,8},{8,16},{16,24},{1,9},{9,17},{17,25},{2,10},{10,18},{18,26},{... | collective-permute-start | bytes 1179656 | tf_op jit(solution)/shard_map/ppermute | solution.py:178
  170.1 1.5 sub.20.owner_ext
  171.6 0.9 copy.106
  172.6 1.0 copy-done.14
  173.6 1.0 copy-done.16
  174.6 12.8 %decode.2.rest_0_ = bf16[12,9,128,128]{3,2,1,0:T(8,128)(2,1)} custom-call(s32[54]{0:T(128)S(1)} %reshape.131.index, bf16[6,9,128,128]{3,2,1,0:T(8,128)(2,1)} %copy-done.1, bf16[6,3,128,128]{3,2,1,0:T(8,128)(2,1)} %collective-permute-done.26.rx_lo, bf16[6,3,128,128]{3,2,1,0:T(8,128)(2,1)S(1)} %collective-permute-done.27.rx_hi, ...), custom_call_target="tpu_custom_call" | custom-call | flops 2500000000 | bytes 8000000 | tf_op jit(solution)/shard_map/decode/pallas_call | solution.py:313
  187.5 13.4 %decode.3 = bf16[12,9,128,128]{3,2,1,0:T(8,128)(2,1)} custom-call(s32[54]{0:T(128)S(1)} %reshape.131.index, bf16[6,9,128,128]{3,2,1,0:T(8,128)(2,1)} %copy-done, bf16[6,3,128,128]{3,2,1,0:T(8,128)(2,1)} %collective-permute-done.8.rx_lo, bf16[6,3,128,128]{3,2,1,0:T(8,128)(2,1)} %collective-permute-done.9.rx_hi, ...), custom_call_target="tpu_custom_call", output_to_operand_aliasing={{}: (13, {})} | custom-call | flops 2500000000 | bytes 8000000 | tf_op jit(solution)/shard_map/decode/pallas_call | solution.py:313
  (140 shorter events, 5.1 us)
Async XLA Ops:
  4.6 13.4 %copy-start.43 = (s32[1152]{0:T(1024)S(1)}, s32[1152]{0:T(1024)}, u32[]{:S(2)}) copy-start(s32[1152]{0:T(1024)} %param.17) | copy-start | bytes 13828
  4.6 13.7 %copy-start.44 = (s32[9,6]{0,1:T(8,128)S(1)}, s32[9,6]{0,1:T(8,128)}, u32[]{:S(2)}) copy-start(s32[9,6]{0,1:T(8,128)} %param.13) | copy-start | bytes 652
  4.6 14.7 %copy-start.31 = (s32[144,1]{0,1:T(1,128)S(1)}, s32[144,1]{0,1:T(1,128)}, u32[]{:S(2)}) copy-start(s32[144,1]{0,1:T(1,128)} %param.18) | copy-start | bytes 1732
  4.6 28.2 %collective-permute-start = (bf16[6,3,128,128]{3,2,1,0:T(8,128)(2,1)}, bf16[6,3,128,128]{3,2,1,0:T(8,128)(2,1)S(1)}, u32[]{:S(2)}, u32[]{:S(2)}) collective-permute-start(bf16[6,3,128,128]{3,2,1,0:T(8,128)(2,1)} %get-tuple-element.30), channel_id=1, source_target_pairs={{0,1},{1,2},{2,3},{3,4},{4,5},{5,6},{6,7},{8,9},{9,10},{10,11},{11... | collective-permute-start | bytes 1769480 | tf_op jit(solution)/shard_map/ppermute | solution.py:178
  7.8 27.7 %collective-permute-start.1 = (bf16[6,3,128,128]{3,2,1,0:T(8,128)(2,1)}, bf16[6,3,128,128]{3,2,1,0:T(8,128)(2,1)S(1)}, u32[]{:S(2)}, u32[]{:S(2)}) collective-permute-start(bf16[6,3,128,128]{3,2,1,0:T(8,128)(2,1)} %get-tuple-element.29), channel_id=1, source_target_pairs={{1,0},{2,1},{3,2},{4,3},{5,4},{6,5},{7,6},{9,8},{10,9},{11,10},{12... | collective-permute-start | bytes 1769480 | tf_op jit(solution)/shard_map/ppermute | solution.py:178
  11.8 37.0 %collective-permute-start.14 = (bf16[6,3,128,128]{3,2,1,0:T(8,128)(2,1)S(1)}, bf16[6,3,128,128]{3,2,1,0:T(8,128)(2,1)S(1)}, u32[]{:S(2)}, u32[]{:S(2)}) collective-permute-start(bf16[6,3,128,128]{3,2,1,0:T(8,128)(2,1)S(1)} %get-tuple-element.20), channel_id=1, source_target_pairs={{0,8},{8,16},{16,24},{1,9},{9,17},{17,25},{2,10},{10,18},{18,26},{... | collective-permute-start | bytes 1769480 | tf_op jit(solution)/shard_map/ppermute | solution.py:178
  16.0 37.5 %collective-permute-start.15 = (bf16[6,3,128,128]{3,2,1,0:T(8,128)(2,1)}, bf16[6,3,128,128]{3,2,1,0:T(8,128)(2,1)}, u32[]{:S(2)}, u32[]{:S(2)}) collective-permute-start(bf16[6,3,128,128]{3,2,1,0:T(8,128)(2,1)} %get-tuple-element.19), channel_id=1, source_target_pairs={{8,0},{16,8},{24,16},{9,1},{17,9},{25,17},{10,2},{18,10},{26,18},{... | collective-permute-start | bytes 1769480 | tf_op jit(solution)/shard_map/ppermute | solution.py:178
  18.2 41.5 %copy-start.11 = (s32[1152,1]{1,0:T(8,128)}, s32[1152,1]{1,0:T(8,128)S(1)}, u32[]{:S(2)}) copy-start(s32[1152,1]{1,0:T(8,128)S(1)} %reshape.150.cluster_col) | copy-start | bytes 13828
  18.4 25.1 %copy-start.40 = (bf16[6,1152,128]{2,1,0:T(8,128)(2,1)S(1)}, bf16[6,1152,128]{2,1,0:T(8,128)(2,1)}, u32[]{:S(2)}) copy-start(bf16[6,1152,128]{2,1,0:T(8,128)(2,1)} %get-tuple-element.14) | copy-start | bytes 5308420
  19.3 40.5 %copy-start.29 = (f32[1,1152]{1,0:T(1,128)}, f32[1,1152]{1,0:T(1,128)S(1)}, u32[]{:S(2)}) copy-start(f32[1,1152]{1,0:T(1,128)S(1)} %reshape.149.weight_row) | copy-start | bytes 13828
  32.8 12.2 %copy-start.21 = (bf16[6,3,128,128]{3,2,1,0:T(8,128)(2,1)}, bf16[6,3,128,128]{3,2,1,0:T(8,128)(2,1)S(1)}, u32[]{:S(2)}) copy-start(bf16[6,3,128,128]{3,2,1,0:T(8,128)(2,1)S(1)} %collective-permute-done.ry_lo) | copy-start | bytes 1769476
  35.6 9.4 %copy-start.23 = (bf16[6,3,128,128]{3,2,1,0:T(8,128)(2,1)}, bf16[6,3,128,128]{3,2,1,0:T(8,128)(2,1)S(1)}, u32[]{:S(2)}) copy-start(bf16[6,3,128,128]{3,2,1,0:T(8,128)(2,1)S(1)} %collective-permute-done.1.ry_hi) | copy-start | bytes 1769476
  35.7 22.1 %collective-permute-start.16 = (bf16[6,2,128,128]{3,2,1,0:T(8,128)(2,1)S(1)}, bf16[6,2,128,128]{3,2,1,0:T(8,128)(2,1)S(1)}, u32[]{:S(2)}, u32[]{:S(2)}) collective-permute-start(bf16[6,2,128,128]{3,2,1,0:T(8,128)(2,1)S(1)} %pad_maximum_fusion.4), channel_id=1, source_target_pairs={{0,8},{8,16},{16,24},{1,9},{9,17},{17,25},{2,10},{10,18},{18,26},{... | collective-permute-start | bytes 1179656 | tf_op jit(solution)/shard_map/ppermute | solution.py:178
  39.2 20.5 %collective-permute-start.17 = (bf16[6,2,128,128]{3,2,1,0:T(8,128)(2,1)S(1)}, bf16[6,2,128,128]{3,2,1,0:T(8,128)(2,1)S(1)}, u32[]{:S(2)}, u32[]{:S(2)}) collective-permute-start(bf16[6,2,128,128]{3,2,1,0:T(8,128)(2,1)S(1)} %pad_maximum_fusion.5), channel_id=1, source_target_pairs={{8,0},{16,8},{24,16},{9,1},{17,9},{25,17},{10,2},{18,10},{26,18},{... | collective-permute-start | bytes 1179656 | tf_op jit(solution)/shard_map/ppermute | solution.py:178
  44.9 14.8 %copy-start.34 = (bf16[128,128]{1,0:T(8,128)(2,1)S(1)}, bf16[128,128]{1,0:T(8,128)(2,1)}, u32[]{:S(2)}) copy-start(bf16[128,128]{1,0:T(8,128)(2,1)} %w_mix.3) | copy-start | bytes 98308
  44.9 14.8 %copy-start.36 = (bf16[128,128]{1,0:T(8,128)(2,1)S(1)}, bf16[128,128]{1,0:T(8,128)(2,1)}, u32[]{:S(2)}) copy-start(bf16[128,128]{1,0:T(8,128)(2,1)} %w_coarse.3) | copy-start | bytes 98308
  44.9 14.8 %copy-start.38 = (f32[128]{0:T(128)S(1)}, f32[128]{0:T(128)}, u32[]{:S(2)}) copy-start(f32[128]{0:T(128)} %param.14) | copy-start | bytes 1540
  45.0 14.8 %copy-start.22 = (bf16[6,3,128,128]{3,2,1,0:T(8,128)(2,1)S(1)}, bf16[6,3,128,128]{3,2,1,0:T(8,128)(2,1)}, u32[]{:S(2)}) copy-start(bf16[6,3,128,128]{3,2,1,0:T(8,128)(2,1)} %copy-done.21) | copy-start | bytes 1769476
  45.0 14.8 %copy-start.24 = (bf16[6,3,128,128]{3,2,1,0:T(8,128)(2,1)S(1)}, bf16[6,3,128,128]{3,2,1,0:T(8,128)(2,1)}, u32[]{:S(2)}) copy-start(bf16[6,3,128,128]{3,2,1,0:T(8,128)(2,1)} %copy-done.23) | copy-start | bytes 1769476
  45.0 32.5 %collective-permute-start.4 = (bf16[6,3,128,128]{3,2,1,0:T(8,128)(2,1)}, bf16[6,3,128,128]{3,2,1,0:T(8,128)(2,1)S(1)}, u32[]{:S(2)}, u32[]{:S(2)}) collective-permute-start(bf16[6,3,128,128]{3,2,1,0:T(8,128)(2,1)} %get-tuple-element.26), channel_id=1, source_target_pairs={{0,1},{1,2},{2,3},{3,4},{4,5},{5,6},{6,7},{8,9},{9,10},{10,11},{11... | collective-permute-start | bytes 1769480 | tf_op jit(solution)/shard_map/ppermute | solution.py:178
  49.6 27.8 %collective-permute-start.5 = (bf16[6,3,128,128]{3,2,1,0:T(8,128)(2,1)}, bf16[6,3,128,128]{3,2,1,0:T(8,128)(2,1)S(1)}, u32[]{:S(2)}, u32[]{:S(2)}) collective-permute-start(bf16[6,3,128,128]{3,2,1,0:T(8,128)(2,1)} %get-tuple-element.25), channel_id=1, source_target_pairs={{1,0},{2,1},{3,2},{4,3},{5,4},{6,5},{7,6},{9,8},{10,9},{11,10},{12... | collective-permute-start | bytes 1769480 | tf_op jit(solution)/shard_map/ppermute | solution.py:178
  53.5 31.9 %collective-permute-start.2 = (bf16[6,3,128,128]{3,2,1,0:T(8,128)(2,1)}, bf16[6,3,128,128]{3,2,1,0:T(8,128)(2,1)}, u32[]{:S(2)}, u32[]{:S(2)}) collective-permute-start(bf16[6,3,128,128]{3,2,1,0:T(8,128)(2,1)} %get-tuple-element.28), channel_id=1, source_target_pairs={{0,8},{8,16},{16,24},{1,9},{9,17},{17,25},{2,10},{10,18},{18,26},{... | collective-permute-start | bytes 1769480 | tf_op jit(solution)/shard_map/ppermute | solution.py:178
  57.8 32.1 %collective-permute-start.3 = (bf16[6,3,128,128]{3,2,1,0:T(8,128)(2,1)}, bf16[6,3,128,128]{3,2,1,0:T(8,128)(2,1)}, u32[]{:S(2)}, u32[]{:S(2)}) collective-permute-start(bf16[6,3,128,128]{3,2,1,0:T(8,128)(2,1)} %get-tuple-element.27), channel_id=1, source_target_pairs={{8,0},{16,8},{24,16},{9,1},{17,9},{25,17},{10,2},{18,10},{26,18},{... | collective-permute-start | bytes 1769480 | tf_op jit(solution)/shard_map/ppermute | solution.py:178
  75.0 8.5 %copy-start.1 = (bf16[6,9,128,128]{3,2,1,0:T(8,128)(2,1)}, bf16[6,9,128,128]{3,2,1,0:T(8,128)(2,1)S(1)}, u32[]{:S(2)}) copy-start(bf16[6,9,128,128]{3,2,1,0:T(8,128)(2,1)S(1)} %get-tuple-element.12.own) | copy-start | bytes 5308420
  77.6 7.9 %copy-start.41 = (s32[3,3,128]{2,1,0:T(4,128)S(1)}, s32[3,3,128]{2,1,0:T(4,128)}, u32[]{:S(2)}) copy-start(s32[3,3,128]{2,1,0:T(4,128)} %add.136) | copy-start | bytes 13828
  77.6 17.5 %copy-start.12 = (s32[1152,1]{1,0:T(8,128)S(1)}, s32[1152,1]{1,0:T(8,128)}, u32[]{:S(2)}) copy-start(s32[1152,1]{1,0:T(8,128)} %copy-done.11) | copy-start | bytes 13828
  77.6 17.5 %copy-start.30 = (f32[1,1152]{1,0:T(1,128)S(1)}, f32[1,1152]{1,0:T(1,128)}, u32[]{:S(2)}) copy-start(f32[1,1152]{1,0:T(1,128)} %copy-done.29) | copy-start | bytes 13828
  77.6 17.5 %copy-start.35 = (bf16[128,128]{1,0:T(8,128)(2,1)S(1)}, bf16[128,128]{1,0:T(8,128)(2,1)}, u32[]{:S(2)}) copy-start(bf16[128,128]{1,0:T(8,128)(2,1)} %w_mix.3) | copy-start | bytes 98308
  77.6 17.5 %copy-start.37 = (bf16[128,128]{1,0:T(8,128)(2,1)S(1)}, bf16[128,128]{1,0:T(8,128)(2,1)}, u32[]{:S(2)}) copy-start(bf16[128,128]{1,0:T(8,128)(2,1)} %w_coarse.3) | copy-start | bytes 98308
  77.6 17.5 %copy-start.39 = (f32[128]{0:T(128)S(1)}, f32[128]{0:T(128)}, u32[]{:S(2)}) copy-start(f32[128]{0:T(128)} %param.14) | copy-start | bytes 1540
  77.6 14.1 %collective-permute-start.7 = (bf16[6,2,128,128]{3,2,1,0:T(8,128)(2,1)S(1)}, bf16[6,2,128,128]{3,2,1,0:T(8,128)(2,1)S(1)}, u32[]{:S(2)}, u32[]{:S(2)}) collective-permute-start(bf16[6,2,128,128]{3,2,1,0:T(8,128)(2,1)S(1)} %pad_maximum_fusion.1), channel_id=1, source_target_pairs={{8,0},{16,8},{24,16},{9,1},{17,9},{25,17},{10,2},{18,10},{26,18},{... | collective-permute-start | bytes 1179656 | tf_op jit(solution)/shard_map/ppermute | solution.py:178
  79.8 15.3 %collective-permute-start.6 = (bf16[6,2,128,128]{3,2,1,0:T(8,128)(2,1)S(1)}, bf16[6,2,128,128]{3,2,1,0:T(8,128)(2,1)S(1)}, u32[]{:S(2)}, u32[]{:S(2)}) collective-permute-start(bf16[6,2,128,128]{3,2,1,0:T(8,128)(2,1)S(1)} %pad_maximum_fusion), channel_id=1, source_target_pairs={{0,8},{8,16},{16,24},{1,9},{9,17},{17,25},{2,10},{10,18},{18,26},{... | collective-permute-start | bytes 1179656 | tf_op jit(solution)/shard_map/ppermute | solution.py:178
  83.5 31.4 %collective-permute-start.18 = (bf16[6,3,128,128]{3,2,1,0:T(8,128)(2,1)S(1)}, bf16[6,3,128,128]{3,2,1,0:T(8,128)(2,1)S(1)}, u32[]{:S(2)}, u32[]{:S(2)}) collective-permute-start(bf16[6,3,128,128]{3,2,1,0:T(8,128)(2,1)S(1)} %get-tuple-element.17), channel_id=1, source_target_pairs={{0,1},{1,2},{2,3},{3,4},{4,5},{5,6},{6,7},{8,9},{9,10},{10,11},{11... | collective-permute-start | bytes 1769480 | tf_op jit(solution)/shard_map/ppermute | solution.py:178
  85.5 36.4 %collective-permute-start.22 = (s32[3,1,128]{2,1,0:T(1,128)S(1)}, s32[3,1,128]{2,1,0:T(1,128)S(1)}, u32[]{:S(2)}, u32[]{:S(2)}) collective-permute-start(s32[3,1,128]{2,1,0:T(1,128)S(1)} %get-tuple-element.49), channel_id=1, source_target_pairs={{0,1},{1,2},{2,3},{3,4},{4,5},{5,6},{6,7},{8,9},{9,10},{10,11},{11... | collective-permute-start | bytes 4616 | tf_op jit(solution)/shard_map/ppermute | solution.py:178
  89.9 34.5 %collective-permute-start.23 = (s32[3,1,128]{2,1,0:T(1,128)S(1)}, s32[3,1,128]{2,1,0:T(1,128)S(1)}, u32[]{:S(2)}, u32[]{:S(2)}) collective-permute-start(s32[3,1,128]{2,1,0:T(1,128)S(1)} %get-tuple-element.50), channel_id=1, source_target_pairs={{1,0},{2,1},{3,2},{4,3},{5,4},{6,5},{7,6},{9,8},{10,9},{11,10},{12... | collective-permute-start | bytes 4616 | tf_op jit(solution)/shard_map/ppermute | solution.py:178
  91.8 23.2 %collective-permute-start.19 = (bf16[6,3,128,128]{3,2,1,0:T(8,128)(2,1)S(1)}, bf16[6,3,128,128]{3,2,1,0:T(8,128)(2,1)S(1)}, u32[]{:S(2)}, u32[]{:S(2)}) collective-permute-start(bf16[6,3,128,128]{3,2,1,0:T(8,128)(2,1)S(1)} %get-tuple-element.18), channel_id=1, source_target_pairs={{1,0},{2,1},{3,2},{4,3},{5,4},{6,5},{7,6},{9,8},{10,9},{11,10},{12... | collective-permute-start | bytes 1769480 | tf_op jit(solution)/shard_map/ppermute | solution.py:178
  111.6 17.2 %copy-start = (bf16[6,9,128,128]{3,2,1,0:T(8,128)(2,1)}, bf16[6,9,128,128]{3,2,1,0:T(8,128)(2,1)S(1)}, u32[]{:S(2)}) copy-start(bf16[6,9,128,128]{3,2,1,0:T(8,128)(2,1)S(1)} %get-tuple-element.9.own) | copy-start | bytes 5308420
  112.8 7.9 %copy-start.2 = (bf16[6,9,128,128]{3,2,1,0:T(8,128)(2,1)S(1)}, bf16[6,9,128,128]{3,2,1,0:T(8,128)(2,1)}, u32[]{:S(2)}) copy-start(bf16[6,9,128,128]{3,2,1,0:T(8,128)(2,1)} %copy-done.1) | copy-start | bytes 5308420
  112.8 30.5 %collective-permute-start.10 = (bf16[6,3,128,128]{3,2,1,0:T(8,128)(2,1)}, bf16[6,3,128,128]{3,2,1,0:T(8,128)(2,1)S(1)}, u32[]{:S(2)}, u32[]{:S(2)}) collective-permute-start(bf16[6,3,128,128]{3,2,1,0:T(8,128)(2,1)} %get-tuple-element.22), channel_id=1, source_target_pairs={{0,1},{1,2},{2,3},{3,4},{4,5},{5,6},{6,7},{8,9},{9,10},{10,11},{11... | collective-permute-start | bytes 1769480 | tf_op jit(solution)/shard_map/ppermute | solution.py:178
  115.0 6.9 %copy-start.3 = (bf16[6,3,128,128]{3,2,1,0:T(8,128)(2,1)}, bf16[6,3,128,128]{3,2,1,0:T(8,128)(2,1)S(1)}, u32[]{:S(2)}) copy-start(bf16[6,3,128,128]{3,2,1,0:T(8,128)(2,1)S(1)} %collective-permute-done.18.ry_lo) | copy-start | bytes 1769476
  115.1 14.9 %collective-permute-start.21 = (bf16[6,2,128,128]{3,2,1,0:T(8,128)(2,1)S(1)}, bf16[6,2,128,128]{3,2,1,0:T(8,128)(2,1)S(1)}, u32[]{:S(2)}, u32[]{:S(2)}) collective-permute-start(bf16[6,2,128,128]{3,2,1,0:T(8,128)(2,1)S(1)} %pad_maximum_fusion.7), channel_id=1, source_target_pairs={{8,0},{16,8},{24,16},{9,1},{17,9},{25,17},{10,2},{18,10},{26,18},{... | collective-permute-start | bytes 1179656 | tf_op jit(solution)/shard_map/ppermute | solution.py:178
  117.1 16.4 %collective-permute-start.20 = (bf16[6,2,128,128]{3,2,1,0:T(8,128)(2,1)S(1)}, bf16[6,2,128,128]{3,2,1,0:T(8,128)(2,1)S(1)}, u32[]{:S(2)}, u32[]{:S(2)}) collective-permute-start(bf16[6,2,128,128]{3,2,1,0:T(8,128)(2,1)S(1)} %pad_maximum_fusion.6), channel_id=1, source_target_pairs={{0,8},{8,16},{16,24},{1,9},{9,17},{17,25},{2,10},{10,18},{18,26},{... | collective-permute-start | bytes 1179656 | tf_op jit(solution)/shard_map/ppermute | solution.py:178
  121.9 16.6 %copy-start.28 = (f32[6,32,128]{2,1,0:T(8,128)S(1)}, f32[6,32,128]{2,1,0:T(8,128)}, u32[]{:S(2)}) copy-start(f32[6,32,128]{2,1,0:T(8,128)} %copy-done.27) | copy-start | bytes 294916
  121.9 44.3 %collective-permute-start.26 = (bf16[6,3,128,128]{3,2,1,0:T(8,128)(2,1)}, bf16[6,3,128,128]{3,2,1,0:T(8,128)(2,1)}, u32[]{:S(2)}, u32[]{:S(2)}) collective-permute-start(bf16[6,3,128,128]{3,2,1,0:T(8,128)(2,1)} %get-tuple-element.16), channel_id=1, source_target_pairs={{0,8},{8,16},{16,24},{1,9},{9,17},{17,25},{2,10},{10,18},{18,26},{... | collective-permute-start | bytes 1769480 | tf_op jit(solution)/shard_map/ppermute | solution.py:178
  124.4 23.1 %collective-permute-start.11 = (bf16[6,3,128,128]{3,2,1,0:T(8,128)(2,1)}, bf16[6,3,128,128]{3,2,1,0:T(8,128)(2,1)S(1)}, u32[]{:S(2)}, u32[]{:S(2)}) collective-permute-start(bf16[6,3,128,128]{3,2,1,0:T(8,128)(2,1)} %get-tuple-element.21), channel_id=1, source_target_pairs={{1,0},{2,1},{3,2},{4,3},{5,4},{6,5},{7,6},{9,8},{10,9},{11,10},{12... | collective-permute-start | bytes 1769480 | tf_op jit(solution)/shard_map/ppermute | solution.py:178
  130.0 21.0 %copy-start.13 = (bf16[6,2,128,128]{3,2,1,0:T(8,128)(2,1)}, bf16[6,2,128,128]{3,2,1,0:T(8,128)(2,1)S(1)}, u32[]{:S(2)}) copy-start(bf16[6,2,128,128]{3,2,1,0:T(8,128)(2,1)S(1)} %collective-permute-done.21.co_hi) | copy-start | bytes 1179652
  130.0 42.6 %collective-permute-start.27 = (bf16[6,3,128,128]{3,2,1,0:T(8,128)(2,1)}, bf16[6,3,128,128]{3,2,1,0:T(8,128)(2,1)S(1)}, u32[]{:S(2)}, u32[]{:S(2)}) collective-permute-start(bf16[6,3,128,128]{3,2,1,0:T(8,128)(2,1)} %get-tuple-element.15), channel_id=1, source_target_pairs={{8,0},{16,8},{24,16},{9,1},{17,9},{25,17},{10,2},{18,10},{26,18},{... | collective-permute-start | bytes 1769480 | tf_op jit(solution)/shard_map/ppermute | solution.py:178
  133.5 25.5 %collective-permute-start.24 = (s32[1,5,128]{2,1,0:T(8,128)S(1)}, s32[1,5,128]{2,1,0:T(8,128)S(1)}, u32[]{:S(2)}, u32[]{:S(2)}) collective-permute-start(s32[1,5,128]{2,1,0:T(8,128)S(1)} %get-tuple-element.47), channel_id=1, source_target_pairs={{0,8},{8,16},{16,24},{1,9},{9,17},{17,25},{2,10},{10,18},{18,26},{... | collective-permute-start | bytes 7688 | tf_op jit(solution)/shard_map/ppermute | solution.py:178
  139.4 13.8 %all-to-all-start = ((f32[32,12,128]{2,1,0:T(8,128)}), f32[32,12,128]{2,1,0:T(8,128)}, u32[]{:S(2)}, u32[]{:S(2)}) async-start(f32[32,12,128]{2,1,0:T(8,128)} %copy.83), calls=%async_computation | async-start | bytes 524288 | tf_op jit(solution)/shard_map/all_to_all | solution.py:292
  143.3 19.8 %copy-start.5 = (bf16[6,3,128,128]{3,2,1,0:T(8,128)(2,1)}, bf16[6,3,128,128]{3,2,1,0:T(8,128)(2,1)S(1)}, u32[]{:S(2)}) copy-start(bf16[6,3,128,128]{3,2,1,0:T(8,128)(2,1)S(1)} %collective-permute-done.10.ry_lo) | copy-start | bytes 1769476
  143.4 26.7 %copy-start.42 = (s32[3,3,128]{2,1,0:T(4,128)S(1)}, s32[3,3,128]{2,1,0:T(4,128)}, u32[]{:S(2)}) copy-start(s32[3,3,128]{2,1,0:T(4,128)} %add.136) | copy-start | bytes 13828
  143.4 44.0 %collective-permute-start.8 = (bf16[6,3,128,128]{3,2,1,0:T(8,128)(2,1)}, bf16[6,3,128,128]{3,2,1,0:T(8,128)(2,1)}, u32[]{:S(2)}, u32[]{:S(2)}) collective-permute-start(bf16[6,3,128,128]{3,2,1,0:T(8,128)(2,1)} %get-tuple-element.24), channel_id=1, source_target_pairs={{0,8},{8,16},{16,24},{1,9},{9,17},{17,25},{2,10},{10,18},{18,26},{... | collective-permute-start | bytes 1769480 | tf_op jit(solution)/shard_map/ppermute | solution.py:178
  147.5 22.5 %copy-start.9 = (bf16[6,3,128,128]{3,2,1,0:T(8,128)(2,1)}, bf16[6,3,128,128]{3,2,1,0:T(8,128)(2,1)S(1)}, u32[]{:S(2)}) copy-start(bf16[6,3,128,128]{3,2,1,0:T(8,128)(2,1)S(1)} %collective-permute-done.11.ry_hi) | copy-start | bytes 1769476
  147.6 39.9 %collective-permute-start.9 = (bf16[6,3,128,128]{3,2,1,0:T(8,128)(2,1)}, bf16[6,3,128,128]{3,2,1,0:T(8,128)(2,1)}, u32[]{:S(2)}, u32[]{:S(2)}) collective-permute-start(bf16[6,3,128,128]{3,2,1,0:T(8,128)(2,1)} %get-tuple-element.23), channel_id=1, source_target_pairs={{8,0},{16,8},{24,16},{9,1},{17,9},{25,17},{10,2},{18,10},{26,18},{... | collective-permute-start | bytes 1769480 | tf_op jit(solution)/shard_map/ppermute | solution.py:178
  151.0 21.6 %copy-start.4 = (bf16[6,3,128,128]{3,2,1,0:T(8,128)(2,1)S(1)}, bf16[6,3,128,128]{3,2,1,0:T(8,128)(2,1)}, u32[]{:S(2)}) copy-start(bf16[6,3,128,128]{3,2,1,0:T(8,128)(2,1)} %copy-done.3) | copy-start | bytes 1769476
  151.0 21.6 %copy-start.8 = (bf16[6,3,128,128]{3,2,1,0:T(8,128)(2,1)S(1)}, bf16[6,3,128,128]{3,2,1,0:T(8,128)(2,1)}, u32[]{:S(2)}) copy-start(bf16[6,3,128,128]{3,2,1,0:T(8,128)(2,1)} %copy-done.7) | copy-start | bytes 1769476
  151.0 21.6 %copy-start.25 = (bf16[128,128]{1,0:T(8,128)(2,1)S(1)}, bf16[128,128]{1,0:T(8,128)(2,1)}, u32[]{:S(2)}) copy-start(bf16[128,128]{1,0:T(8,128)(2,1)} %w_region.3) | copy-start | bytes 98308
  151.0 21.6 %copy-start.26 = (bf16[128,128]{1,0:T(8,128)(2,1)S(1)}, bf16[128,128]{1,0:T(8,128)(2,1)}, u32[]{:S(2)}) copy-start(bf16[128,128]{1,0:T(8,128)(2,1)} %w_out.3) | copy-start | bytes 98308
  154.8 16.8 %all-to-all-start.1 = ((bf16[32,12,128]{2,1,0:T(8,128)(2,1)}), bf16[32,12,128]{2,1,0:T(8,128)(2,1)}, u32[]{:S(2)}, u32[]{:S(2)}) async-start(bf16[32,12,128]{2,1,0:T(8,128)(2,1)} %broadcast_in_dim.24), calls=%async_computation.1 | async-start | bytes 262144 | tf_op jit(solution)/shard_map/all_to_all | solution.py:300
  159.0 5.3 %collective-permute-start.25 = (s32[1,5,128]{2,1,0:T(8,128)S(1)}, s32[1,5,128]{2,1,0:T(8,128)S(1)}, u32[]{:S(2)}, u32[]{:S(2)}) collective-permute-start(s32[1,5,128]{2,1,0:T(8,128)S(1)} %get-tuple-element.48), channel_id=1, source_target_pairs={{8,0},{16,8},{24,16},{9,1},{17,9},{25,17},{10,2},{18,10},{26,18},{... | collective-permute-start | bytes 7688 | tf_op jit(solution)/shard_map/ppermute | solution.py:178
  164.3 23.1 %collective-permute-start.13 = (bf16[6,2,128,128]{3,2,1,0:T(8,128)(2,1)}, bf16[6,2,128,128]{3,2,1,0:T(8,128)(2,1)}, u32[]{:S(2)}, u32[]{:S(2)}) collective-permute-start(bf16[6,2,128,128]{3,2,1,0:T(8,128)(2,1)} %pad_maximum_fusion.3), channel_id=1, source_target_pairs={{8,0},{16,8},{24,16},{9,1},{17,9},{25,17},{10,2},{18,10},{26,18},{... | collective-permute-start | bytes 1179656 | tf_op jit(solution)/shard_map/ppermute | solution.py:178
  166.2 21.2 %collective-permute-start.12 = (bf16[6,2,128,128]{3,2,1,0:T(8,128)(2,1)}, bf16[6,2,128,128]{3,2,1,0:T(8,128)(2,1)}, u32[]{:S(2)}, u32[]{:S(2)}) collective-permute-start(bf16[6,2,128,128]{3,2,1,0:T(8,128)(2,1)} %pad_maximum_fusion.2), channel_id=1, source_target_pairs={{0,8},{8,16},{16,24},{1,9},{9,17},{17,25},{2,10},{10,18},{18,26},{... | collective-permute-start | bytes 1179656 | tf_op jit(solution)/shard_map/ppermute | solution.py:178
  174.6 12.8 %copy-start.6 = (bf16[6,3,128,128]{3,2,1,0:T(8,128)(2,1)S(1)}, bf16[6,3,128,128]{3,2,1,0:T(8,128)(2,1)}, u32[]{:S(2)}) copy-start(bf16[6,3,128,128]{3,2,1,0:T(8,128)(2,1)} %copy-done.5) | copy-start | bytes 1769476
  174.6 12.8 %copy-start.10 = (bf16[6,3,128,128]{3,2,1,0:T(8,128)(2,1)S(1)}, bf16[6,3,128,128]{3,2,1,0:T(8,128)(2,1)}, u32[]{:S(2)}) copy-start(bf16[6,3,128,128]{3,2,1,0:T(8,128)(2,1)} %copy-done.9) | copy-start | bytes 1769476
  (11 other events, 26.3 us)

commit v4 on v2

--- a/solution.py
+++ b/solution.py
@@ -20,16 +20,12 @@
     return jnp.dot(a, b, preferred_element_type=jnp.float32)
 
 
-def extended_sources(own, rx_lo, rx_hi, ry_lo, ry_hi, co_lo, co_hi):
+def extended_sources(own, rx_lo, rx_hi, ry_lo, ry_hi):
     sources = []
     for r in range(SIDE):
         for c in range(SIDE):
             if r in (0, SIDE - 1):
-                row, corner = (rx_lo, co_lo) if r == 0 else (rx_hi, co_hi)
-                if c in (0, SIDE - 1):
-                    sources.append((corner, 0 if c == 0 else 1))
-                else:
-                    sources.append((row, c - 1))
+                sources.append((rx_lo if r == 0 else rx_hi, c))
             elif c in (0, SIDE - 1):
                 sources.append((ry_lo if c == 0 else ry_hi, r - 1))
             else:
@@ -52,8 +48,6 @@
     rx_hi,
     ry_lo,
     ry_hi,
-    co_lo,
-    co_hi,
     adjacency,
     gain,
     w_mix,
@@ -63,6 +57,8 @@
     owner_row,
     w_coarse,
     u_ref,
+    left_ref,
+    right_ref,
     partial_ref,
     ext,
     enc,
@@ -72,7 +68,7 @@
     nodes = cluster_row.shape[1]
     devices = partial_ref.shape[1]
     for p, (ref, k) in enumerate(
-        extended_sources(own, rx_lo, rx_hi, ry_lo, ry_hi, co_lo, co_hi)
+        extended_sources(own, rx_lo, rx_hi, ry_lo, ry_hi)
     ):
         for t in range(steps):
             ext[p, :, t * BLK : (t + 1) * BLK] = ref[t, k]
@@ -111,7 +107,12 @@
         ).astype(jnp.float32).astype(jnp.bfloat16)
         u = (enc[b].astype(jnp.float32) + dot32(hot, base)).astype(jnp.bfloat16)
         for t in range(steps):
-            u_ref[t, b] = u[:, t * BLK : (t + 1) * BLK]
+            piece = u[:, t * BLK : (t + 1) * BLK]
+            u_ref[t, b] = piece
+            if b % GB == 0:
+                left_ref[t, b // GB] = piece
+            if b % GB == GB - 1:
+                right_ref[t, b // GB] = piece
 
 
 def decode_kernel(
@@ -121,8 +122,6 @@
     rx_hi,
     ry_lo,
     ry_hi,
-    co_lo,
-    co_hi,
     adjacency,
     region,
     owner_ext,
@@ -138,7 +137,7 @@
         reaches.append(dot32(region[t], w_region[...]).astype(jnp.bfloat16))
     reach = jnp.concatenate(reaches, axis=1)
     for p, (ref, k) in enumerate(
-        extended_sources(own, rx_lo, rx_hi, ry_lo, ry_hi, co_lo, co_hi)
+        extended_sources(own, rx_lo, rx_hi, ry_lo, ry_hi)
     ):
         hot = (
             lax.broadcasted_iota(jnp.int32, (BLK, devices), 1)
@@ -178,17 +177,25 @@
     return lax.ppermute(value, axis, pairs)
 
 
-def halo(field):
-    steps = field.shape[0]
-    square = field.reshape(steps, GB, GB, BLK, BLK)
-
-    ry_lo = shifted(square[:, :, GB - 1], "ry", True)
-    ry_hi = shifted(square[:, :, 0], "ry", False)
-    rx_lo = shifted(square[:, GB - 1], "rx", True)
-    rx_hi = shifted(square[:, 0], "rx", False)
-    co_lo = shifted(jnp.stack([ry_lo[:, GB - 1], ry_hi[:, GB - 1]], axis=1), "rx", True)
-    co_hi = shifted(jnp.stack([ry_lo[:, 0], ry_hi[:, 0]], axis=1), "rx", False)
-    return rx_lo, rx_hi, ry_lo, ry_hi, co_lo, co_hi
+def nothing(*arrays):
+    return sum(array.reshape(-1)[0].astype(jnp.float32) * 0.0 for array in arrays)
+
+
+def gated(value, gate):
+    return value if gate is None else (value.astype(jnp.float32) + gate).astype(value.dtype)
+
+
+def columns(left, right, gate=None):
+    return shifted(gated(right, gate), "ry", True), shifted(gated(left, gate), "ry", False)
+
+
+def rows(field, ry_lo, ry_hi, gate=None):
+    def wide(row):
+        middle = field[:, row * GB : (row + 1) * GB]
+        line = [ry_lo[:, row : row + 1], middle, ry_hi[:, row : row + 1]]
+        return gated(jnp.concatenate(line, axis=1), gate)
+
+    return shifted(wide(GB - 1), "rx", True), shifted(wide(0), "rx", False)
 
 
 def on_device(
@@ -224,14 +231,22 @@
         ),
         axis=1,
     )
-    marks = (owner_of + 1).reshape(GB, GB, BLK)
-    marks = jnp.concatenate(
-        [shifted(marks[:, -1:], "ry", True), marks, shifted(marks[:, :1], "ry", False)], axis=1
-    )
-    marks = jnp.concatenate(
-        [shifted(marks[-1:], "rx", True), marks, shifted(marks[:1], "rx", False)], axis=0
-    )
-    owner_ext = (marks - 1).reshape(SIDE * SIDE * BLK, 1)
+    ext_rows = jnp.arange(SIDE * SIDE, dtype=jnp.int32)
+    grid_row = lax.axis_index("rx") * GB + ext_rows // SIDE - 1
+    grid_col = lax.axis_index("ry") * GB + ext_rows % SIDE - 1
+    inside = (
+        (grid_row >= 0)
+        & (grid_row < row_devices * GB)
+        & (grid_col >= 0)
+        & (grid_col < col_devices * GB)
+    )
+    grid_row = jnp.clip(grid_row, 0, row_devices * GB - 1)
+    grid_col = jnp.clip(grid_col, 0, col_devices * GB - 1)
+    place = (
+        (grid_row // GB * col_devices + grid_col // GB) * blocks
+        + grid_row % GB * GB
+        + grid_col % GB
+    )
 
     chunk = steps_count // CHUNKS
     per = LANES_STEPS
@@ -245,13 +260,18 @@
     params = pltpu.CompilerParams(vmem_limit_bytes=48 * 1024 * 1024)
     cost = pl.CostEstimate(flops=5_000_000_000 // CHUNKS, bytes_accessed=16_000_000 // CHUNKS, transcendentals=0)
 
-    first = [halo(noisy[c * chunk : (c + 1) * chunk]) for c in range(CHUNKS)]
+    first = []
+    for c in range(CHUNKS):
+        gate = nothing(*first[-1][2:4]) if first else None
+        field = noisy[c * chunk : (c + 1) * chunk]
+        sides = columns(field[:, 0::GB], field[:, GB - 1 :: GB], gate)
+        first.append((*rows(field, *sides), *sides))
     fields, sums, second = [], [], []
     for c in range(CHUNKS):
         constants = (
             adjacency, gain, w_mix, weight_row, cluster_row, cluster_col, owner_row, w_coarse,
         )
-        u, partial = pl.pallas_call(
+        u, left, right, partial = pl.pallas_call(
             encode_kernel,
             grid_spec=pltpu.PrefetchScalarGridSpec(
                 num_scalar_prefetch=1,
@@ -261,6 +281,8 @@
                 + [whole(part) for part in constants],
                 out_specs=[
                     pl.BlockSpec((per, blocks, BLK, channels), lambda i, _: (i, 0, 0, 0)),
+                    pl.BlockSpec((per, GB, BLK, channels), lambda i, _: (i, 0, 0, 0)),
+                    pl.BlockSpec((per, GB, BLK, channels), lambda i, _: (i, 0, 0, 0)),
                     pl.BlockSpec((per, devices, channels), lambda i, _: (i, 0, 0)),
                 ],
                 scratch_shapes=[
@@ -270,6 +292,8 @@
             ),
             out_shape=[
                 jax.ShapeDtypeStruct((chunk, blocks, BLK, channels), jnp.bfloat16),
+                jax.ShapeDtypeStruct((chunk, GB, BLK, channels), jnp.bfloat16),
+                jax.ShapeDtypeStruct((chunk, GB, BLK, channels), jnp.bfloat16),
                 jax.ShapeDtypeStruct((chunk, devices, channels), jnp.float32),
             ],
             compiler_params=params,
@@ -278,22 +302,31 @@
         )(index, noisy, *first[c], *constants)
         fields.append(u)
         sums.append(partial)
-        second.append(halo(u))
+        second.append(columns(left, right))
+    for c in range(CHUNKS):
+        gate = nothing(sums[-1]) if c + 1 < CHUNKS else None
+        second[c] = (*rows(fields[c], *second[c], gate), *second[c])
+    gate = nothing(*second[0][2:4])
     mine = lax.all_to_all(
-        jnp.concatenate(sums, axis=0).transpose(1, 0, 2),
+        jnp.concatenate(sums, axis=0).transpose(1, 0, 2) + gate,
         ("rx", "ry"),
         split_axis=0,
         concat_axis=0,
         tiled=True,
     )
     own_region = (jnp.sum(mine, axis=0) / float(coarse)).astype(jnp.bfloat16)
-    region = lax.all_to_all(
-        jnp.broadcast_to(own_region[None], (devices, steps_count, channels)),
+    told = jnp.concatenate([own_region, owner_of.reshape(blocks, BLK).astype(jnp.bfloat16)], axis=0)
+    told = lax.all_to_all(
+        jnp.broadcast_to(told[None], (devices,) + told.shape),
         ("rx", "ry"),
         split_axis=0,
         concat_axis=0,
         tiled=True,
-    ).transpose(1, 0, 2)
+    )
+    region = told[:, :steps_count].transpose(1, 0, 2)
+    everyone = told[:, steps_count:].reshape(devices * blocks, BLK)
+    owner_ext = jnp.where(inside[:, None], everyone[place].astype(jnp.int32), -1)
+    owner_ext = owner_ext.reshape(SIDE * SIDE * BLK, 1)
 
     out = None
     for c in range(CHUNKS):

time: 230 us -> 219 us (0.952)
  starting transfers between devices: 94 us -> 57.9 us
  waiting for transfers between devices: 51.7 us -> 71.6 us
  local copies, waits for them, and re-layouts: 23.5 us -> 15 us
  other arithmetic: 2.92 us -> 10.9 us
  between operations: 0.87 us -> 3.62 us
  Pallas kernels: 54.7 us -> 57.4 us
    ppermute x28 -> x16, starting transfers between devices: 84.2 us -> 46.9 us  [shifted(): return lax.ppermute(value, axis, pairs)]
    ppermute x28 -> x16, waiting for transfers between devices: 47.5 us -> 63.3 us  [shifted(): return lax.ppermute(value, axis, pairs)]
    squeeze x8 -> x0, local copies, waits for them, and re-layouts: 11.6 us -> none  [the longest x4 5.94 us: halo(): rx_hi = shifted(square[:, 0], 'rx', False)]
    slice x10 -> x20, local copies, waits for them, and re-layouts: 3.67 us -> 10.9 us  [the longest x4 4.95 us: wide(): middle = field[:, row * GB:(row + 1) * GB]]
    concatenate x0 -> x7, other arithmetic: none -> 6.58 us  [the longest x6 6.57 us: wide(): return gated(jnp.concatenate(line, axis=1), gate)]
    all_to_all x2, waiting for transfers between devices: 4.25 us -> 8.29 us  [the longest x1 8.29 us: on_device(): lax.all_to_all(jnp.broadcast_to(told[None], (devices,) + told.shape), ('r...]
    convert_element_type x0 -> x4, other arithmetic: none -> 3.89 us  [the longest x3 3.89 us: gated(): (value.astype(jnp.float32) + gate).astype(value.dtype)]
    another operation x8 -> x0, other arithmetic: 2.64 us -> none  [the longest x4 1.7 us: halo(): jnp.stack([ry_lo[:, GB - 1], ry_hi[:, GB - 1]], axis=1)]
  transfers between devices with their start and end apart: 30 -> 18, of which waited for: 4 -> 8; matrix products, arithmetic and copies ran while one was open for 8% -> 10% of each run, Pallas kernels for 18% -> 20%
where the time goes in v4:
time: 219 us; the launch traced here: 216 us
  waiting for transfers between devices  71.6 us (33%)
  starting transfers between devices  57.9 us (26%)
  Pallas kernels  57.4 us (26%)
  local copies, waits for them, and re-layouts  15 us (7%)
  other arithmetic  10.9 us (5%)
  between operations  3.62 us (2%)
    ppermute x16, waiting for transfers between devices, shifted(): return lax.ppermute(value, axis, pairs)  63.3 us
    ppermute x16, starting transfers between devices, shifted(): return lax.ppermute(value, axis, pairs)  46.9 us
    pallas_call x2, Pallas kernels, on_device(): pl.pallas_call(encode_kernel, grid_spec=pltpu.PrefetchScalarGridSpec(num_...  30.7 us
    pallas_call x2, Pallas kernels, on_device(): pl.pallas_call(decode_kernel, grid_spec=pltpu.PrefetchScalarGridSpec(num_...  26.7 us
    all_to_all x1, waiting for transfers between devices, on_device(): lax.all_to_all(jnp.broadcast_to(told[None], (devices,) + told.shape), ('r...  8.29 us
    concatenate x6, other arithmetic, wide(): return gated(jnp.concatenate(line, axis=1), gate)  6.57 us
    all_to_all x1, starting transfers between devices, on_device(): lax.all_to_all(jnp.broadcast_to(told[None], (devices,) + told.shape), ('r...  6.08 us
    slice x4, local copies, waits for them, and re-layouts, wide(): middle = field[:, row * GB:(row + 1) * GB]  4.95 us
  transfers between devices with their start and end apart: 18, of which 8 were waited for; matrix products, arithmetic and copies ran while one was open for 10% of the time, Pallas kernels for 20%

profile of v4, /device:TPU:9, one launch (start us, length us, event | category | flops | bytes accessed | tf_op | source)
XLA Modules:
  0.0 216.4 jit_solution(4249935354939654257)
XLA Ops:
  0.0 2.2 %fusion.20 = (bf16[6,1152,128]{2,1,0:T(8,128)(2,1)S(1)}, bf16[6,1152,128]{2,1,0:T(8,128)(2,1)S(1)}) fusion(bf16[12,1152,128]{2,1,0:T(8,128)(2,1)} %bitcast.52), kind=kLoop, calls=%fused_computation.66 | loop fusion | bytes 7077888 | tf_op jit(solution)/shard_map/slice | solution.py:266
  2.2 0.0 copy-start.12
  2.3 0.5 fusion.22
  2.7 3.1 %collective-permute-start = (bf16[6,3,128,128]{3,2,1,0:T(8,128)(2,1)S(1)}, bf16[6,3,128,128]{3,2,1,0:T(8,128)(2,1)S(1)}, u32[]{:S(2)}, u32[]{:S(2)}) collective-permute-start(bf16[6,3,128,128]{3,2,1,0:T(8,128)(2,1)S(1)} %get-tuple-element.28), channel_id=1, source_target_pairs={{0,1},{1,2},{2,3},{3,4},{4,5},{5,6},{6,7},{8,9},{9,10},{10,11},{11... | collective-permute-start | bytes 1769480 | tf_op jit(solution)/shard_map/ppermute | solution.py:177
  5.9 3.0 %collective-permute-start.1 = (bf16[6,3,128,128]{3,2,1,0:T(8,128)(2,1)S(1)}, bf16[6,3,128,128]{3,2,1,0:T(8,128)(2,1)S(1)}, u32[]{:S(2)}, u32[]{:S(2)}) collective-permute-start(bf16[6,3,128,128]{3,2,1,0:T(8,128)(2,1)S(1)} %get-tuple-element.27), channel_id=1, source_target_pairs={{1,0},{2,1},{3,2},{4,3},{5,4},{6,5},{7,6},{9,8},{10,9},{11,10},{12... | collective-permute-start | bytes 1769480 | tf_op jit(solution)/shard_map/ppermute | solution.py:177
  8.9 0.2 reshape.305.cluster_col
  9.2 0.1 fusion.24
  9.2 21.2 %collective-permute-done.ry_lo = bf16[6,3,128,128]{3,2,1,0:T(8,128)(2,1)S(1)} collective-permute-done((bf16[6,3,128,128]{3,2,1,0:T(8,128)(2,1)S(1)}, bf16[6,3,128,128]{3,2,1,0:T(8,128)(2,1)S(1)}, u32[]{:S(2)}, u32[]{:S(2)}) %collective-permute-start) | collective-permute-done | bytes 589856 | tf_op jit(solution)/shard_map/ppermute | solution.py:177
  30.5 0.5 slice.160
  31.0 2.4 %collective-permute-done.1.ry_hi = bf16[6,3,128,128]{3,2,1,0:T(8,128)(2,1)S(1)} collective-permute-done((bf16[6,3,128,128]{3,2,1,0:T(8,128)(2,1)S(1)}, bf16[6,3,128,128]{3,2,1,0:T(8,128)(2,1)S(1)}, u32[]{:S(2)}, u32[]{:S(2)}) %collective-permute-start.1) | collective-permute-done | bytes 589856 | tf_op jit(solution)/shard_map/ppermute | solution.py:177
  33.4 0.5 slice.161
  35.1 0.3 add_convert_fusion.3
  35.4 1.9 collective-permute-start.2
  37.3 4.3 %collective-permute-start.3 = (bf16[6,3,128,128]{3,2,1,0:T(8,128)(2,1)S(1)}, bf16[6,3,128,128]{3,2,1,0:T(8,128)(2,1)S(1)}, u32[]{:S(2)}, u32[]{:S(2)}) collective-permute-start(bf16[6,3,128,128]{3,2,1,0:T(8,128)(2,1)S(1)} %get-tuple-element.34), channel_id=1, source_target_pairs={{1,0},{2,1},{3,2},{4,3},{5,4},{6,5},{7,6},{9,8},{10,9},{11,10},{12... | collective-permute-start | bytes 1769480 | tf_op jit(solution)/shard_map/ppermute | solution.py:177
  41.7 1.1 pad_maximum_fusion.4
  42.8 4.0 %collective-permute-start.10 = (bf16[6,5,128,128]{3,2,1,0:T(8,128)(2,1)}, bf16[6,5,128,128]{3,2,1,0:T(8,128)(2,1)}, u32[]{:S(2)}, u32[]{:S(2)}) collective-permute-start(bf16[6,5,128,128]{3,2,1,0:T(8,128)(2,1)} %pad_maximum_fusion.4), channel_id=1, source_target_pairs={{0,8},{8,16},{16,24},{1,9},{9,17},{17,25},{2,10},{10,18},{18,26},{... | collective-permute-start | bytes 2949128 | tf_op jit(solution)/shard_map/ppermute | solution.py:177
  46.8 1.1 pad_maximum_fusion.5
  47.9 1.9 collective-permute-start.11
  49.8 11.4 %collective-permute-done.2.ry_lo = bf16[6,3,128,128]{3,2,1,0:T(8,128)(2,1)S(1)} collective-permute-done((bf16[6,3,128,128]{3,2,1,0:T(8,128)(2,1)S(1)}, bf16[6,3,128,128]{3,2,1,0:T(8,128)(2,1)S(1)}, u32[]{:S(2)}, u32[]{:S(2)}) %collective-permute-start.2) | collective-permute-done | bytes 589856 | tf_op jit(solution)/shard_map/ppermute | solution.py:177
  61.3 4.8 %collective-permute-done.3.ry_hi = bf16[6,3,128,128]{3,2,1,0:T(8,128)(2,1)S(1)} collective-permute-done((bf16[6,3,128,128]{3,2,1,0:T(8,128)(2,1)S(1)}, bf16[6,3,128,128]{3,2,1,0:T(8,128)(2,1)S(1)}, u32[]{:S(2)}, u32[]{:S(2)}) %collective-permute-start.3) | collective-permute-done | bytes 589856 | tf_op jit(solution)/shard_map/ppermute | solution.py:177
  66.1 0.0 copy-start.13
  66.1 0.0 copy-start.7
  66.2 0.0 copy-start.8
  66.2 1.1 pad_maximum_fusion.1
  67.3 2.4 %collective-permute-start.5 = (bf16[6,5,128,128]{3,2,1,0:T(8,128)(2,1)}, bf16[6,5,128,128]{3,2,1,0:T(8,128)(2,1)}, u32[]{:S(2)}, u32[]{:S(2)}) collective-permute-start(bf16[6,5,128,128]{3,2,1,0:T(8,128)(2,1)} %pad_maximum_fusion.1), channel_id=1, source_target_pairs={{8,0},{16,8},{24,16},{9,1},{17,9},{25,17},{10,2},{18,10},{26,18},{... | collective-permute-start | bytes 2949128 | tf_op jit(solution)/shard_map/ppermute | solution.py:177
  69.7 1.1 pad_maximum_fusion
  70.7 3.1 %collective-permute-start.4 = (bf16[6,5,128,128]{3,2,1,0:T(8,128)(2,1)}, bf16[6,5,128,128]{3,2,1,0:T(8,128)(2,1)}, u32[]{:S(2)}, u32[]{:S(2)}) collective-permute-start(bf16[6,5,128,128]{3,2,1,0:T(8,128)(2,1)} %pad_maximum_fusion), channel_id=1, source_target_pairs={{0,8},{8,16},{16,24},{1,9},{9,17},{17,25},{2,10},{10,18},{18,26},{... | collective-permute-start | bytes 2949128 | tf_op jit(solution)/shard_map/ppermute | solution.py:177
  73.9 0.1 copy.27
  74.0 0.1 reshape.281.index
  74.1 0.2 select_reduce_fusion
  74.3 15.4 %encode.3 = (bf16[6,9,128,128]{3,2,1,0:T(8,128)(2,1)}, bf16[6,3,128,128]{3,2,1,0:T(8,128)(2,1)S(1)}, bf16[6,3,128,128]{3,2,1,0:T(8,128)(2,1)}, f32[6,32,128]{2,1,0:T(8,128)S(1)}) custom-call(s32[54]{0:T(128)S(1)} %reshape.281.index, bf16[12,9,128,128]{3,2,1,0:T(8,128)(2,1)} %bitcast.53, bf16[6,5,128,128]{3,2,1,0:T(8,128)(2,1)} %collective-permute-done.10.rx_lo, ...), custom_call_target="tpu_custom_call" | custom-call | flops 2500000000 | bytes 8000000 | tf_op jit(solution)/shard_map/encode/pallas_call | solution.py:274
  89.7 0.9 copy-done.6
  90.6 1.9 collective-permute-start.12
  92.5 4.3 %collective-permute-start.13 = (bf16[6,3,128,128]{3,2,1,0:T(8,128)(2,1)}, bf16[6,3,128,128]{3,2,1,0:T(8,128)(2,1)S(1)}, u32[]{:S(2)}, u32[]{:S(2)}) collective-permute-start(bf16[6,3,128,128]{3,2,1,0:T(8,128)(2,1)} %copy-done.6), channel_id=1, source_target_pairs={{1,0},{2,1},{3,2},{4,3},{5,4},{6,5},{7,6},{9,8},{10,9},{11,10},{12... | collective-permute-start | bytes 1769480 | tf_op jit(solution)/shard_map/ppermute | solution.py:177
  96.8 2.2 %fusion.21 = (bf16[6,3,128,128]{3,2,1,0:T(8,128)(2,1)S(1)}, bf16[6,3,128,128]{3,2,1,0:T(8,128)(2,1)}) fusion(bf16[6,9,128,128]{3,2,1,0:T(8,128)(2,1)} %get-tuple-element.20.own), kind=kLoop, calls=%fused_computation.67 | loop fusion | bytes 2359296 | tf_op jit(solution)/shard_map/slice | solution.py:194
  99.0 15.3 %encode.2 = (bf16[6,9,128,128]{3,2,1,0:T(8,128)(2,1)}, bf16[6,3,128,128]{3,2,1,0:T(8,128)(2,1)S(1)}, bf16[6,3,128,128]{3,2,1,0:T(8,128)(2,1)}, f32[6,32,128]{2,1,0:T(8,128)S(1)}) custom-call(s32[54]{0:T(128)S(1)} %reshape.281.index, bf16[12,9,128,128]{3,2,1,0:T(8,128)(2,1)} %bitcast.54, bf16[6,5,128,128]{3,2,1,0:T(8,128)(2,1)} %collective-permute-done.4.rx_lo, ...), custom_call_target="tpu_custom_call" | custom-call | flops 2500000000 | bytes 8000000 | tf_op jit(solution)/shard_map/encode/pallas_call | solution.py:274
  114.3 0.5 slice.184
  115.5 2.0 collective-permute-start.6
  117.6 0.7 collective-permute-done.12.ry_lo
  118.3 15.8 %collective-permute-done.13.ry_hi = bf16[6,3,128,128]{3,2,1,0:T(8,128)(2,1)S(1)} collective-permute-done((bf16[6,3,128,128]{3,2,1,0:T(8,128)(2,1)}, bf16[6,3,128,128]{3,2,1,0:T(8,128)(2,1)S(1)}, u32[]{:S(2)}, u32[]{:S(2)}) %collective-permute-start.13) | collective-permute-done | bytes 589856 | tf_op jit(solution)/shard_map/ppermute | solution.py:177
  134.2 1.3 add_convert_fusion
  135.4 2.4 %collective-permute-start.15 = (bf16[6,5,128,128]{3,2,1,0:T(8,128)(2,1)}, bf16[6,5,128,128]{3,2,1,0:T(8,128)(2,1)}, u32[]{:S(2)}, u32[]{:S(2)}) collective-permute-start(bf16[6,5,128,128]{3,2,1,0:T(8,128)(2,1)} %add_convert_fusion), channel_id=1, source_target_pairs={{8,0},{16,8},{24,16},{9,1},{17,9},{25,17},{10,2},{18,10},{26,18},{... | collective-permute-start | bytes 2949128 | tf_op jit(solution)/shard_map/ppermute | solution.py:177
  137.8 0.5 slice.178
  138.3 0.5 slice.179
  140.1 0.8 copy.30
  140.9 4.9 %all-to-all-start = ((f32[32,12,128]{2,1,0:T(8,128)}), f32[32,12,128]{2,1,0:T(8,128)S(1)}, u32[]{:S(2)}, u32[]{:S(2)}) async-start(f32[32,12,128]{2,1,0:T(8,128)} %copy.30), calls=%async_computation | async-start | bytes 524288 | tf_op jit(solution)/shard_map/all_to_all | solution.py:310
  145.8 3.1 %collective-permute-start.7 = (bf16[6,3,128,128]{3,2,1,0:T(8,128)(2,1)}, bf16[6,3,128,128]{3,2,1,0:T(8,128)(2,1)S(1)}, u32[]{:S(2)}, u32[]{:S(2)}) collective-permute-start(bf16[6,3,128,128]{3,2,1,0:T(8,128)(2,1)} %copy-done.5), channel_id=1, source_target_pairs={{1,0},{2,1},{3,2},{4,3},{5,4},{6,5},{7,6},{9,8},{10,9},{11,10},{12... | collective-permute-start | bytes 1769480 | tf_op jit(solution)/shard_map/ppermute | solution.py:177
  148.9 2.3 %add_convert_fusion.1 = bf16[6,5,128,128]{3,2,1,0:T(8,128)(2,1)} fusion(bf16[6,1,128,128]{3,2,1,0:T(8,128)(2,1)S(1)} %get-tuple-element.38, bf16[6,3,128,128]{3,2,1,0:T(8,128)(2,1)} %get-tuple-element.24, bf16[6,1,128,128]{3,2,1,0:T(8,128)(2,1)S(1)} %get-tuple-element.36, f32[]{:T(128)} %bitcast.19), kind=kLoop, calls=%fused_computation.2 | loop fusion | flops 2457600 | bytes 1966084 | tf_op jit(solution)/shard_map/convert_element_type | solution.py:185
  151.2 3.6 %collective-permute-start.14 = (bf16[6,5,128,128]{3,2,1,0:T(8,128)(2,1)}, bf16[6,5,128,128]{3,2,1,0:T(8,128)(2,1)}, u32[]{:S(2)}, u32[]{:S(2)}) collective-permute-start(bf16[6,5,128,128]{3,2,1,0:T(8,128)(2,1)} %add_convert_fusion.1), channel_id=1, source_target_pairs={{0,8},{8,16},{16,24},{1,9},{9,17},{17,25},{2,10},{10,18},{18,26},{... | collective-permute-start | bytes 2949128 | tf_op jit(solution)/shard_map/ppermute | solution.py:177
  154.9 2.2 %fusion.23 = (bf16[6,3,128,128]{3,2,1,0:T(8,128)(2,1)}, bf16[6,3,128,128]{3,2,1,0:T(8,128)(2,1)S(1)}) fusion(bf16[6,9,128,128]{3,2,1,0:T(8,128)(2,1)} %get-tuple-element.13.own), kind=kLoop, calls=%fused_computation.69 | loop fusion | bytes 2359296 | tf_op jit(solution)/shard_map/slice | solution.py:194
  157.2 6.9 %collective-permute-done.7.ry_hi = bf16[6,3,128,128]{3,2,1,0:T(8,128)(2,1)S(1)} collective-permute-done((bf16[6,3,128,128]{3,2,1,0:T(8,128)(2,1)}, bf16[6,3,128,128]{3,2,1,0:T(8,128)(2,1)S(1)}, u32[]{:S(2)}, u32[]{:S(2)}) %collective-permute-start.7) | collective-permute-done | bytes 589856 | tf_op jit(solution)/shard_map/ppermute | solution.py:177
  164.1 1.2 pad_maximum_fusion.3
  165.3 2.9 %collective-permute-start.9 = (bf16[6,5,128,128]{3,2,1,0:T(8,128)(2,1)}, bf16[6,5,128,128]{3,2,1,0:T(8,128)(2,1)}, u32[]{:S(2)}, u32[]{:S(2)}) collective-permute-start(bf16[6,5,128,128]{3,2,1,0:T(8,128)(2,1)} %pad_maximum_fusion.3), channel_id=1, source_target_pairs={{8,0},{16,8},{24,16},{9,1},{17,9},{25,17},{10,2},{18,10},{26,18},{... | collective-permute-start | bytes 2949128 | tf_op jit(solution)/shard_map/ppermute | solution.py:177
  168.2 1.1 pad_maximum_fusion.2
  169.2 2.9 %collective-permute-start.8 = (bf16[6,5,128,128]{3,2,1,0:T(8,128)(2,1)}, bf16[6,5,128,128]{3,2,1,0:T(8,128)(2,1)}, u32[]{:S(2)}, u32[]{:S(2)}) collective-permute-start(bf16[6,5,128,128]{3,2,1,0:T(8,128)(2,1)} %pad_maximum_fusion.2), channel_id=1, source_target_pairs={{0,8},{8,16},{16,24},{1,9},{9,17},{17,25},{2,10},{10,18},{18,26},{... | collective-permute-start | bytes 2949128 | tf_op jit(solution)/shard_map/ppermute | solution.py:177
  172.2 0.7 broadcast_in_dim.41
  172.9 6.1 %all-to-all-start.1 = ((bf16[32,21,128]{2,1,0:T(8,128)(2,1)}), bf16[32,21,128]{2,1,0:T(8,128)(2,1)S(1)}, u32[]{:S(2)}, u32[]{:S(2)}) async-start(bf16[32,21,128]{2,1,0:T(8,128)(2,1)} %broadcast_in_dim.41), calls=%async_computation.1 | async-start | bytes 393216 | tf_op jit(solution)/shard_map/all_to_all | solution.py:319
  179.1 8.3 %all-to-all-done.1 = bf16[32,21,128]{2,1,0:T(8,128)(2,1)S(1)} async-done(((bf16[32,21,128]{2,1,0:T(8,128)(2,1)}), bf16[32,21,128]{2,1,0:T(8,128)(2,1)S(1)}, u32[]{:S(2)}, u32[]{:S(2)}) %all-to-all-start.1) | async-done | bytes 172064 | tf_op jit(solution)/shard_map/all_to_all | solution.py:319
  187.5 0.6 gather_fusion
  188.1 0.1 select_bitcast_fusion
  188.2 0.5 copy.36
  188.7 0.9 slice.180
  189.7 13.4 %decode.2.rest_0_ = bf16[12,9,128,128]{3,2,1,0:T(8,128)(2,1)} custom-call(s32[54]{0:T(128)S(1)} %reshape.281.index, bf16[6,9,128,128]{3,2,1,0:T(8,128)(2,1)} %get-tuple-element.20.own, bf16[6,5,128,128]{3,2,1,0:T(8,128)(2,1)} %collective-permute-done.14.rx_lo, bf16[6,5,128,128]{3,2,1,0:T(8,128)(2,1)} %collective-permute-done.15.rx_hi, ...), custom_call_target="tpu_custom_call" | custom-call | flops 2500000000 | bytes 8000000 | tf_op jit(solution)/shard_map/decode/pallas_call | solution.py:336
  203.1 13.3 %decode.3 = bf16[12,9,128,128]{3,2,1,0:T(8,128)(2,1)} custom-call(s32[54]{0:T(128)S(1)} %reshape.281.index, bf16[6,9,128,128]{3,2,1,0:T(8,128)(2,1)} %get-tuple-element.13.own, bf16[6,5,128,128]{3,2,1,0:T(8,128)(2,1)} %collective-permute-done.8.rx_lo, bf16[6,5,128,128]{3,2,1,0:T(8,128)(2,1)} %collective-permute-done.9.rx_hi, ...), custom_call_target="tpu_custom_call", output_to_operand_aliasing={{}: (11, {})} | custom-call | flops 2500000000 | bytes 8000000 | tf_op jit(solution)/shard_map/decode/pallas_call | solution.py:336
  (59 shorter events, 0.6 us)
Async XLA Ops:
  2.2 6.7 %copy-start.12 = (s32[1152]{0:T(1024)S(1)}, s32[1152]{0:T(1024)}, u32[]{:S(2)}) copy-start(s32[1152]{0:T(1024)} %param.17) | copy-start | bytes 13828
  2.7 27.8 %collective-permute-start = (bf16[6,3,128,128]{3,2,1,0:T(8,128)(2,1)S(1)}, bf16[6,3,128,128]{3,2,1,0:T(8,128)(2,1)S(1)}, u32[]{:S(2)}, u32[]{:S(2)}) collective-permute-start(bf16[6,3,128,128]{3,2,1,0:T(8,128)(2,1)S(1)} %get-tuple-element.28), channel_id=1, source_target_pairs={{0,1},{1,2},{2,3},{3,4},{4,5},{5,6},{6,7},{8,9},{9,10},{10,11},{11... | collective-permute-start | bytes 1769480 | tf_op jit(solution)/shard_map/ppermute | solution.py:177
  5.9 27.5 %collective-permute-start.1 = (bf16[6,3,128,128]{3,2,1,0:T(8,128)(2,1)S(1)}, bf16[6,3,128,128]{3,2,1,0:T(8,128)(2,1)S(1)}, u32[]{:S(2)}, u32[]{:S(2)}) collective-permute-start(bf16[6,3,128,128]{3,2,1,0:T(8,128)(2,1)S(1)} %get-tuple-element.27), channel_id=1, source_target_pairs={{1,0},{2,1},{3,2},{4,3},{5,4},{6,5},{7,6},{9,8},{10,9},{11,10},{12... | collective-permute-start | bytes 1769480 | tf_op jit(solution)/shard_map/ppermute | solution.py:177
  35.4 25.8 %collective-permute-start.2 = (bf16[6,3,128,128]{3,2,1,0:T(8,128)(2,1)S(1)}, bf16[6,3,128,128]{3,2,1,0:T(8,128)(2,1)S(1)}, u32[]{:S(2)}, u32[]{:S(2)}) collective-permute-start(bf16[6,3,128,128]{3,2,1,0:T(8,128)(2,1)S(1)} %get-tuple-element.33), channel_id=1, source_target_pairs={{0,1},{1,2},{2,3},{3,4},{4,5},{5,6},{6,7},{8,9},{9,10},{10,11},{11... | collective-permute-start | bytes 1769480 | tf_op jit(solution)/shard_map/ppermute | solution.py:177
  37.3 28.8 %collective-permute-start.3 = (bf16[6,3,128,128]{3,2,1,0:T(8,128)(2,1)S(1)}, bf16[6,3,128,128]{3,2,1,0:T(8,128)(2,1)S(1)}, u32[]{:S(2)}, u32[]{:S(2)}) collective-permute-start(bf16[6,3,128,128]{3,2,1,0:T(8,128)(2,1)S(1)} %get-tuple-element.34), channel_id=1, source_target_pairs={{1,0},{2,1},{3,2},{4,3},{5,4},{6,5},{7,6},{9,8},{10,9},{11,10},{12... | collective-permute-start | bytes 1769480 | tf_op jit(solution)/shard_map/ppermute | solution.py:177
  42.8 31.5 %collective-permute-start.10 = (bf16[6,5,128,128]{3,2,1,0:T(8,128)(2,1)}, bf16[6,5,128,128]{3,2,1,0:T(8,128)(2,1)}, u32[]{:S(2)}, u32[]{:S(2)}) collective-permute-start(bf16[6,5,128,128]{3,2,1,0:T(8,128)(2,1)} %pad_maximum_fusion.4), channel_id=1, source_target_pairs={{0,8},{8,16},{16,24},{1,9},{9,17},{17,25},{2,10},{10,18},{18,26},{... | collective-permute-start | bytes 2949128 | tf_op jit(solution)/shard_map/ppermute | solution.py:177
  47.9 26.4 %collective-permute-start.11 = (bf16[6,5,128,128]{3,2,1,0:T(8,128)(2,1)}, bf16[6,5,128,128]{3,2,1,0:T(8,128)(2,1)}, u32[]{:S(2)}, u32[]{:S(2)}) collective-permute-start(bf16[6,5,128,128]{3,2,1,0:T(8,128)(2,1)} %pad_maximum_fusion.5), channel_id=1, source_target_pairs={{8,0},{16,8},{24,16},{9,1},{17,9},{25,17},{10,2},{18,10},{26,18},{... | collective-permute-start | bytes 2949128 | tf_op jit(solution)/shard_map/ppermute | solution.py:177
  66.1 7.8 %copy-start.13 = (s32[9,6]{0,1:T(8,128)S(1)}, s32[9,6]{0,1:T(8,128)}, u32[]{:S(2)}) copy-start(s32[9,6]{0,1:T(8,128)} %param.13) | copy-start | bytes 652
  66.1 8.0 %copy-start.14 = (bf16[1152]{0:T(1024)(128)(2,1)S(1)}, bf16[1152]{0:T(1024)(128)(2,1)}, u32[]{:S(2)}) copy-start(bf16[1152]{0:T(1024)(128)(2,1)} %param.16) | copy-start | bytes 6916
  66.1 8.0 %copy-start.4 = (s32[144,1]{0,1:T(1,128)S(1)}, s32[144,1]{0,1:T(1,128)}, u32[]{:S(2)}) copy-start(s32[144,1]{0,1:T(1,128)} %param.18) | copy-start | bytes 1732
  66.1 8.2 %copy-start.7 = (bf16[128,128]{1,0:T(8,128)(2,1)S(1)}, bf16[128,128]{1,0:T(8,128)(2,1)}, u32[]{:S(2)}) copy-start(bf16[128,128]{1,0:T(8,128)(2,1)} %w_mix.3) | copy-start | bytes 98308
  66.2 8.2 %copy-start.8 = (bf16[128,128]{1,0:T(8,128)(2,1)S(1)}, bf16[128,128]{1,0:T(8,128)(2,1)}, u32[]{:S(2)}) copy-start(bf16[128,128]{1,0:T(8,128)(2,1)} %w_coarse.3) | copy-start | bytes 98308
  66.2 8.2 %copy-start.9 = (f32[128]{0:T(128)S(1)}, f32[128]{0:T(128)}, u32[]{:S(2)}) copy-start(f32[128]{0:T(128)} %param.14) | copy-start | bytes 1540
  67.3 31.7 %collective-permute-start.5 = (bf16[6,5,128,128]{3,2,1,0:T(8,128)(2,1)}, bf16[6,5,128,128]{3,2,1,0:T(8,128)(2,1)}, u32[]{:S(2)}, u32[]{:S(2)}) collective-permute-start(bf16[6,5,128,128]{3,2,1,0:T(8,128)(2,1)} %pad_maximum_fusion.1), channel_id=1, source_target_pairs={{8,0},{16,8},{24,16},{9,1},{17,9},{25,17},{10,2},{18,10},{26,18},{... | collective-permute-start | bytes 2949128 | tf_op jit(solution)/shard_map/ppermute | solution.py:177
  70.7 28.3 %collective-permute-start.4 = (bf16[6,5,128,128]{3,2,1,0:T(8,128)(2,1)}, bf16[6,5,128,128]{3,2,1,0:T(8,128)(2,1)}, u32[]{:S(2)}, u32[]{:S(2)}) collective-permute-start(bf16[6,5,128,128]{3,2,1,0:T(8,128)(2,1)} %pad_maximum_fusion), channel_id=1, source_target_pairs={{0,8},{8,16},{16,24},{1,9},{9,17},{17,25},{2,10},{10,18},{18,26},{... | collective-permute-start | bytes 2949128 | tf_op jit(solution)/shard_map/ppermute | solution.py:177
  89.7 0.9 copy-start.6
  90.6 27.7 %collective-permute-start.12 = (bf16[6,3,128,128]{3,2,1,0:T(8,128)(2,1)}, bf16[6,3,128,128]{3,2,1,0:T(8,128)(2,1)S(1)}, u32[]{:S(2)}, u32[]{:S(2)}) collective-permute-start(bf16[6,3,128,128]{3,2,1,0:T(8,128)(2,1)} %get-tuple-element.18), channel_id=1, source_target_pairs={{0,1},{1,2},{2,3},{3,4},{4,5},{5,6},{6,7},{8,9},{9,10},{10,11},{11... | collective-permute-start | bytes 1769480 | tf_op jit(solution)/shard_map/ppermute | solution.py:177
  92.5 41.6 %collective-permute-start.13 = (bf16[6,3,128,128]{3,2,1,0:T(8,128)(2,1)}, bf16[6,3,128,128]{3,2,1,0:T(8,128)(2,1)S(1)}, u32[]{:S(2)}, u32[]{:S(2)}) collective-permute-start(bf16[6,3,128,128]{3,2,1,0:T(8,128)(2,1)} %copy-done.6), channel_id=1, source_target_pairs={{1,0},{2,1},{3,2},{4,3},{5,4},{6,5},{7,6},{9,8},{10,9},{11,10},{12... | collective-permute-start | bytes 1769480 | tf_op jit(solution)/shard_map/ppermute | solution.py:177
  114.3 21.1 %copy-start.5 = (bf16[6,3,128,128]{3,2,1,0:T(8,128)(2,1)}, bf16[6,3,128,128]{3,2,1,0:T(8,128)(2,1)S(1)}, u32[]{:S(2)}) copy-start(bf16[6,3,128,128]{3,2,1,0:T(8,128)(2,1)S(1)} %get-tuple-element.15) | copy-start | bytes 1769476
  115.5 41.6 %collective-permute-start.6 = (bf16[6,3,128,128]{3,2,1,0:T(8,128)(2,1)}, bf16[6,3,128,128]{3,2,1,0:T(8,128)(2,1)S(1)}, u32[]{:S(2)}, u32[]{:S(2)}) collective-permute-start(bf16[6,3,128,128]{3,2,1,0:T(8,128)(2,1)} %get-tuple-element.14), channel_id=1, source_target_pairs={{0,1},{1,2},{2,3},{3,4},{4,5},{5,6},{6,7},{8,9},{9,10},{10,11},{11... | collective-permute-start | bytes 1769480 | tf_op jit(solution)/shard_map/ppermute | solution.py:177
  135.4 54.2 %collective-permute-start.15 = (bf16[6,5,128,128]{3,2,1,0:T(8,128)(2,1)}, bf16[6,5,128,128]{3,2,1,0:T(8,128)(2,1)}, u32[]{:S(2)}, u32[]{:S(2)}) collective-permute-start(bf16[6,5,128,128]{3,2,1,0:T(8,128)(2,1)} %add_convert_fusion), channel_id=1, source_target_pairs={{8,0},{16,8},{24,16},{9,1},{17,9},{25,17},{10,2},{18,10},{26,18},{... | collective-permute-start | bytes 2949128 | tf_op jit(solution)/shard_map/ppermute | solution.py:177
  140.9 16.2 %all-to-all-start = ((f32[32,12,128]{2,1,0:T(8,128)}), f32[32,12,128]{2,1,0:T(8,128)S(1)}, u32[]{:S(2)}, u32[]{:S(2)}) async-start(f32[32,12,128]{2,1,0:T(8,128)} %copy.30), calls=%async_computation | async-start | bytes 524288 | tf_op jit(solution)/shard_map/all_to_all | solution.py:310
  145.8 18.2 %collective-permute-start.7 = (bf16[6,3,128,128]{3,2,1,0:T(8,128)(2,1)}, bf16[6,3,128,128]{3,2,1,0:T(8,128)(2,1)S(1)}, u32[]{:S(2)}, u32[]{:S(2)}) collective-permute-start(bf16[6,3,128,128]{3,2,1,0:T(8,128)(2,1)} %copy-done.5), channel_id=1, source_target_pairs={{1,0},{2,1},{3,2},{4,3},{5,4},{6,5},{7,6},{9,8},{10,9},{11,10},{12... | collective-permute-start | bytes 1769480 | tf_op jit(solution)/shard_map/ppermute | solution.py:177
  151.2 38.4 %collective-permute-start.14 = (bf16[6,5,128,128]{3,2,1,0:T(8,128)(2,1)}, bf16[6,5,128,128]{3,2,1,0:T(8,128)(2,1)}, u32[]{:S(2)}, u32[]{:S(2)}) collective-permute-start(bf16[6,5,128,128]{3,2,1,0:T(8,128)(2,1)} %add_convert_fusion.1), channel_id=1, source_target_pairs={{0,8},{8,16},{16,24},{1,9},{9,17},{17,25},{2,10},{10,18},{18,26},{... | collective-permute-start | bytes 2949128 | tf_op jit(solution)/shard_map/ppermute | solution.py:177
  157.1 7.0 %copy-start.10 = (bf16[6,3,128,128]{3,2,1,0:T(8,128)(2,1)S(1)}, bf16[6,3,128,128]{3,2,1,0:T(8,128)(2,1)}, u32[]{:S(2)}) copy-start(bf16[6,3,128,128]{3,2,1,0:T(8,128)(2,1)} %get-tuple-element.29) | copy-start | bytes 1769476
  164.1 5.1 %copy-start = (bf16[6,3,128,128]{3,2,1,0:T(8,128)(2,1)}, bf16[6,3,128,128]{3,2,1,0:T(8,128)(2,1)S(1)}, u32[]{:S(2)}) copy-start(bf16[6,3,128,128]{3,2,1,0:T(8,128)(2,1)S(1)} %collective-permute-done.7.ry_hi) | copy-start | bytes 1769476
  165.3 37.8 %collective-permute-start.9 = (bf16[6,5,128,128]{3,2,1,0:T(8,128)(2,1)}, bf16[6,5,128,128]{3,2,1,0:T(8,128)(2,1)}, u32[]{:S(2)}, u32[]{:S(2)}) collective-permute-start(bf16[6,5,128,128]{3,2,1,0:T(8,128)(2,1)} %pad_maximum_fusion.3), channel_id=1, source_target_pairs={{8,0},{16,8},{24,16},{9,1},{17,9},{25,17},{10,2},{18,10},{26,18},{... | collective-permute-start | bytes 2949128 | tf_op jit(solution)/shard_map/ppermute | solution.py:177
  169.2 20.4 %copy-start.2 = (bf16[128,128]{1,0:T(8,128)(2,1)S(1)}, bf16[128,128]{1,0:T(8,128)(2,1)}, u32[]{:S(2)}) copy-start(bf16[128,128]{1,0:T(8,128)(2,1)} %w_region.3) | copy-start | bytes 98308
  169.2 20.5 %copy-start.3 = (bf16[128,128]{1,0:T(8,128)(2,1)S(1)}, bf16[128,128]{1,0:T(8,128)(2,1)}, u32[]{:S(2)}) copy-start(bf16[128,128]{1,0:T(8,128)(2,1)} %w_out.3) | copy-start | bytes 98308
  169.2 33.9 %collective-permute-start.8 = (bf16[6,5,128,128]{3,2,1,0:T(8,128)(2,1)}, bf16[6,5,128,128]{3,2,1,0:T(8,128)(2,1)}, u32[]{:S(2)}, u32[]{:S(2)}) collective-permute-start(bf16[6,5,128,128]{3,2,1,0:T(8,128)(2,1)} %pad_maximum_fusion.2), channel_id=1, source_target_pairs={{0,8},{8,16},{16,24},{1,9},{9,17},{17,25},{2,10},{10,18},{18,26},{... | collective-permute-start | bytes 2949128 | tf_op jit(solution)/shard_map/ppermute | solution.py:177
  172.9 14.4 %all-to-all-start.1 = ((bf16[32,21,128]{2,1,0:T(8,128)(2,1)}), bf16[32,21,128]{2,1,0:T(8,128)(2,1)S(1)}, u32[]{:S(2)}, u32[]{:S(2)}) async-start(bf16[32,21,128]{2,1,0:T(8,128)(2,1)} %broadcast_in_dim.41), calls=%async_computation.1 | async-start | bytes 393216 | tf_op jit(solution)/shard_map/all_to_all | solution.py:319
  187.4 0.8 copy-start.11
  189.7 13.4 %copy-start.1 = (bf16[6,3,128,128]{3,2,1,0:T(8,128)(2,1)S(1)}, bf16[6,3,128,128]{3,2,1,0:T(8,128)(2,1)}, u32[]{:S(2)}) copy-start(bf16[6,3,128,128]{3,2,1,0:T(8,128)(2,1)} %copy-done) | copy-start | bytes 1769476

commit v5 on v3

--- a/solution.py
+++ b/solution.py
@@ -230,6 +230,23 @@
         ),
         axis=1,
     )
+    ext_rows = jnp.arange(SIDE * SIDE, dtype=jnp.int32)
+    grid_row = lax.axis_index("rx") * GB + ext_rows // SIDE - 1
+    grid_col = lax.axis_index("ry") * GB + ext_rows % SIDE - 1
+    inside = (
+        (grid_row >= 0)
+        & (grid_row < row_devices * GB)
+        & (grid_col >= 0)
+        & (grid_col < col_devices * GB)
+    )
+    grid_row = jnp.clip(grid_row, 0, row_devices * GB - 1)
+    grid_col = jnp.clip(grid_col, 0, col_devices * GB - 1)
+    place = (
+        (grid_row // GB * col_devices + grid_col // GB) * blocks
+        + grid_row % GB * GB
+        + grid_col % GB
+    )
+
     chunk = steps_count // CHUNKS
     per = LANES_STEPS
     grid = chunk // per
@@ -279,15 +296,6 @@
         fields.append(u)
         sums.append(partial)
         second.append(halo(u))
-    marks = (owner_of + 1).reshape(GB, GB, BLK) + nothing(sums[0]).astype(jnp.int32)
-    marks = jnp.concatenate(
-        [shifted(marks[:, -1:], "ry", True), marks, shifted(marks[:, :1], "ry", False)], axis=1
-    )
-    marks = jnp.concatenate(
-        [shifted(marks[-1:], "rx", True), marks, shifted(marks[:1], "rx", False)], axis=0
-    )
-    owner_ext = (marks - 1).reshape(SIDE * SIDE * BLK, 1)
-
     gate = nothing(*second[0][4:6])
     mine = lax.all_to_all(
         jnp.concatenate(sums, axis=0).transpose(1, 0, 2) + gate,
@@ -297,13 +305,18 @@
         tiled=True,
     )
     own_region = (jnp.sum(mine, axis=0) / float(coarse)).astype(jnp.bfloat16)
-    region = lax.all_to_all(
-        jnp.broadcast_to(own_region[None], (devices, steps_count, channels)),
+    told = jnp.concatenate([own_region, owner_of.reshape(blocks, BLK).astype(jnp.bfloat16)], axis=0)
+    told = lax.all_to_all(
+        jnp.broadcast_to(told[None], (devices,) + told.shape),
         ("rx", "ry"),
         split_axis=0,
         concat_axis=0,
         tiled=True,
-    ).transpose(1, 0, 2)
+    )
+    region = told[:, :steps_count].transpose(1, 0, 2)
+    everyone = told[:, steps_count:].reshape(devices * blocks, BLK)
+    owner_ext = jnp.where(inside[:, None], everyone[place].astype(jnp.int32), -1)
+    owner_ext = owner_ext.reshape(SIDE * SIDE * BLK, 1)
 
     out = None
     for c in range(CHUNKS):

time: 203 us -> 205 us (level)
  waiting for transfers between devices: 18.9 us -> 25.3 us
  starting transfers between devices: 89 us -> 83.1 us
  local copies, waits for them, and re-layouts: 26.5 us -> 29.5 us
    ppermute x28 -> x24, starting transfers between devices: 81 us -> 70.4 us  [shifted(): return lax.ppermute(value, axis, pairs)]
    unnamed x90 -> x83, local copies, waits for them, and re-layouts: 7.49 us -> 13 us
    ppermute x28 -> x24, waiting for transfers between devices: 16.7 us -> 21.2 us  [shifted(): return lax.ppermute(value, axis, pairs)]
    all_to_all x1, waiting for transfers between devices: 0.01 us -> 4.16 us  [on_device(): lax.all_to_all(jnp.broadcast_to(told[None], (devices,) + told.shape), ('r...]
    all_to_all x1, starting transfers between devices: 4.1 us -> 7.38 us  [on_device(): lax.all_to_all(jnp.broadcast_to(told[None], (devices,) + told.shape), ('r...]
    all_to_all x1, waiting for transfers between devices: 2.19 us -> 0.01 us  [on_device(): lax.all_to_all(jnp.concatenate(sums, axis=0).transpose(1, 0, 2) + gate, (...]
  transfers between devices with their start and end apart: 30 -> 26, of which waited for: 4 -> 4; matrix products, arithmetic and copies ran while one was open for 11% -> 9% of each run, Pallas kernels for 21% -> 21%
where the time goes in v5:
time: 205 us; the launch traced here: 202 us
  starting transfers between devices  83.1 us (41%)
  Pallas kernels  54.6 us (27%)
  local copies, waits for them, and re-layouts  29.5 us (14%)
  waiting for transfers between devices  25.3 us (12%)
  other arithmetic  5.81 us (3%)
  between operations  3.53 us (2%)
    ppermute x24, starting transfers between devices, shifted(): return lax.ppermute(value, axis, pairs)  70.4 us
    pallas_call x2, Pallas kernels, on_device(): pl.pallas_call(encode_kernel, grid_spec=pltpu.PrefetchScalarGridSpec(num_...  28.2 us
    pallas_call x2, Pallas kernels, on_device(): pl.pallas_call(decode_kernel, grid_spec=pltpu.PrefetchScalarGridSpec(num_...  26.4 us
    ppermute x24, waiting for transfers between devices, shifted(): return lax.ppermute(value, axis, pairs)  21.2 us
    unnamed x83, local copies, waits for them, and re-layouts  13 us
    all_to_all x1, starting transfers between devices, on_device(): lax.all_to_all(jnp.broadcast_to(told[None], (devices,) + told.shape), ('r...  7.38 us
    all_to_all x1, starting transfers between devices, on_device(): lax.all_to_all(jnp.concatenate(sums, axis=0).transpose(1, 0, 2) + gate, (...  5.33 us
    all_to_all x1, waiting for transfers between devices, on_device(): lax.all_to_all(jnp.broadcast_to(told[None], (devices,) + told.shape), ('r...  4.16 us
  transfers between devices with their start and end apart: 26, of which 4 were waited for; matrix products, arithmetic and copies ran while one was open for 9% of the time, Pallas kernels for 21%

profile of v5, /device:TPU:9, one launch (start us, length us, event | category | flops | bytes accessed | tf_op | source)
XLA Modules:
  0.0 201.8 jit_solution(8401886112813963870)
XLA Ops:
  0.0 3.4 %fusion.24 = (bf16[6,1152,128]{2,1,0:T(8,128)(2,1)S(1)}, bf16[6,1152,128]{2,1,0:T(8,128)(2,1)}) fusion(bf16[12,1152,128]{2,1,0:T(8,128)(2,1)} %bitcast.128), kind=kLoop, calls=%fused_computation.88 | loop fusion | bytes 7077888 | tf_op jit(solution)/shard_map/slice | solution.py:265
  3.4 1.2 slice_bitcast_fusion.13
  4.6 3.3 %collective-permute-start = (bf16[6,3,128,128]{3,2,1,0:T(8,128)(2,1)}, bf16[6,3,128,128]{3,2,1,0:T(8,128)(2,1)S(1)}, u32[]{:S(2)}, u32[]{:S(2)}) collective-permute-start(bf16[6,3,128,128]{3,2,1,0:T(8,128)(2,1)} %get-tuple-element.30), channel_id=1, source_target_pairs={{0,1},{1,2},{2,3},{3,4},{4,5},{5,6},{6,7},{8,9},{9,10},{10,11},{11... | collective-permute-start | bytes 1769480 | tf_op jit(solution)/shard_map/ppermute | solution.py:178
  7.9 3.0 %collective-permute-start.1 = (bf16[6,3,128,128]{3,2,1,0:T(8,128)(2,1)}, bf16[6,3,128,128]{3,2,1,0:T(8,128)(2,1)S(1)}, u32[]{:S(2)}, u32[]{:S(2)}) collective-permute-start(bf16[6,3,128,128]{3,2,1,0:T(8,128)(2,1)} %get-tuple-element.29), channel_id=1, source_target_pairs={{1,0},{2,1},{3,2},{4,3},{5,4},{6,5},{7,6},{9,8},{10,9},{11,10},{12... | collective-permute-start | bytes 1769480 | tf_op jit(solution)/shard_map/ppermute | solution.py:178
  10.9 1.2 slice_bitcast_fusion.4
  12.1 4.2 %collective-permute-start.14 = (bf16[6,3,128,128]{3,2,1,0:T(8,128)(2,1)}, bf16[6,3,128,128]{3,2,1,0:T(8,128)(2,1)S(1)}, u32[]{:S(2)}, u32[]{:S(2)}) collective-permute-start(bf16[6,3,128,128]{3,2,1,0:T(8,128)(2,1)} %get-tuple-element.20), channel_id=1, source_target_pairs={{0,8},{8,16},{16,24},{1,9},{9,17},{17,25},{2,10},{10,18},{18,26},{... | collective-permute-start | bytes 1769480 | tf_op jit(solution)/shard_map/ppermute | solution.py:178
  16.3 1.9 collective-permute-start.15
  18.9 13.9 %collective-permute-done.ry_lo = bf16[6,3,128,128]{3,2,1,0:T(8,128)(2,1)S(1)} collective-permute-done((bf16[6,3,128,128]{3,2,1,0:T(8,128)(2,1)}, bf16[6,3,128,128]{3,2,1,0:T(8,128)(2,1)S(1)}, u32[]{:S(2)}, u32[]{:S(2)}) %collective-permute-start) | collective-permute-done | bytes 589856 | tf_op jit(solution)/shard_map/ppermute | solution.py:178
  32.9 2.8 %collective-permute-done.1.ry_hi = bf16[6,3,128,128]{3,2,1,0:T(8,128)(2,1)S(1)} collective-permute-done((bf16[6,3,128,128]{3,2,1,0:T(8,128)(2,1)}, bf16[6,3,128,128]{3,2,1,0:T(8,128)(2,1)S(1)}, u32[]{:S(2)}, u32[]{:S(2)}) %collective-permute-start.1) | collective-permute-done | bytes 589856 | tf_op jit(solution)/shard_map/ppermute | solution.py:178
  35.7 3.5 %collective-permute-start.16 = (bf16[6,2,128,128]{3,2,1,0:T(8,128)(2,1)S(1)}, bf16[6,2,128,128]{3,2,1,0:T(8,128)(2,1)S(1)}, u32[]{:S(2)}, u32[]{:S(2)}) collective-permute-start(bf16[6,2,128,128]{3,2,1,0:T(8,128)(2,1)S(1)} %pad_maximum_fusion.4), channel_id=1, source_target_pairs={{0,8},{8,16},{16,24},{1,9},{9,17},{17,25},{2,10},{10,18},{18,26},{... | collective-permute-start | bytes 1179656 | tf_op jit(solution)/shard_map/ppermute | solution.py:178
  39.3 1.9 collective-permute-start.17
  44.0 2.4 %collective-permute-start.4 = (bf16[6,3,128,128]{3,2,1,0:T(8,128)(2,1)S(1)}, bf16[6,3,128,128]{3,2,1,0:T(8,128)(2,1)S(1)}, u32[]{:S(2)}, u32[]{:S(2)}) collective-permute-start(bf16[6,3,128,128]{3,2,1,0:T(8,128)(2,1)S(1)} %get-tuple-element.26), channel_id=1, source_target_pairs={{0,1},{1,2},{2,3},{3,4},{4,5},{5,6},{6,7},{8,9},{9,10},{10,11},{11... | collective-permute-start | bytes 1769480 | tf_op jit(solution)/shard_map/ppermute | solution.py:178
  46.4 1.4 fusion.1
  47.8 3.9 %collective-permute-start.5 = (bf16[6,3,128,128]{3,2,1,0:T(8,128)(2,1)S(1)}, bf16[6,3,128,128]{3,2,1,0:T(8,128)(2,1)S(1)}, u32[]{:S(2)}, u32[]{:S(2)}) collective-permute-start(bf16[6,3,128,128]{3,2,1,0:T(8,128)(2,1)S(1)} %get-tuple-element.25), channel_id=1, source_target_pairs={{1,0},{2,1},{3,2},{4,3},{5,4},{6,5},{7,6},{9,8},{10,9},{11,10},{12... | collective-permute-start | bytes 1769480 | tf_op jit(solution)/shard_map/ppermute | solution.py:178
  51.7 0.8 copy-done.26
  52.6 4.2 %collective-permute-start.2 = (bf16[6,3,128,128]{3,2,1,0:T(8,128)(2,1)}, bf16[6,3,128,128]{3,2,1,0:T(8,128)(2,1)S(1)}, u32[]{:S(2)}, u32[]{:S(2)}) collective-permute-start(bf16[6,3,128,128]{3,2,1,0:T(8,128)(2,1)} %get-tuple-element.28), channel_id=1, source_target_pairs={{0,8},{8,16},{16,24},{1,9},{9,17},{17,25},{2,10},{10,18},{18,26},{... | collective-permute-start | bytes 1769480 | tf_op jit(solution)/shard_map/ppermute | solution.py:178
  56.8 1.9 collective-permute-start.3
  58.8 1.1 copy-done.27
  59.8 14.1 %encode.3 = (bf16[6,9,128,128]{3,2,1,0:T(8,128)(2,1)S(1)}, f32[6,32,128]{2,1,0:T(8,128)S(1)}) custom-call(s32[54]{0:T(128)S(1)} %reshape.306.index, bf16[12,9,128,128]{3,2,1,0:T(8,128)(2,1)} %bitcast.129, bf16[6,3,128,128]{3,2,1,0:T(8,128)(2,1)S(1)} %collective-permute-done.14.rx_lo, bf16[6,3,128,128]{3,2,1,0:T(8,128)(2,1)S(1)} %copy-done.27, ...), custom_call_target="tpu_custom_call" | custom-call | flops 2500000000 | bytes 8000000 | tf_op jit(solution)/shard_map/encode/pallas_call | solution.py:271
  73.9 1.3 slice_bitcast_fusion.3
  75.2 2.0 %collective-permute-start.18 = (bf16[6,3,128,128]{3,2,1,0:T(8,128)(2,1)}, bf16[6,3,128,128]{3,2,1,0:T(8,128)(2,1)S(1)}, u32[]{:S(2)}, u32[]{:S(2)}) collective-permute-start(bf16[6,3,128,128]{3,2,1,0:T(8,128)(2,1)} %get-tuple-element.17), channel_id=1, source_target_pairs={{0,1},{1,2},{2,3},{3,4},{4,5},{5,6},{6,7},{8,9},{9,10},{10,11},{11... | collective-permute-start | bytes 1769480 | tf_op jit(solution)/shard_map/ppermute | solution.py:178
  77.4 0.7 copy-done.17
  78.4 1.9 collective-permute-start.7
  80.3 0.8 pad_maximum_fusion
  81.1 3.7 %collective-permute-start.6 = (bf16[6,2,128,128]{3,2,1,0:T(8,128)(2,1)}, bf16[6,2,128,128]{3,2,1,0:T(8,128)(2,1)S(1)}, u32[]{:S(2)}, u32[]{:S(2)}) collective-permute-start(bf16[6,2,128,128]{3,2,1,0:T(8,128)(2,1)} %pad_maximum_fusion), channel_id=1, source_target_pairs={{0,8},{8,16},{16,24},{1,9},{9,17},{17,25},{2,10},{10,18},{18,26},{... | collective-permute-start | bytes 1179656 | tf_op jit(solution)/shard_map/ppermute | solution.py:178
  84.9 0.8 copy-done.24
  85.7 4.4 %collective-permute-start.19 = (bf16[6,3,128,128]{3,2,1,0:T(8,128)(2,1)}, bf16[6,3,128,128]{3,2,1,0:T(8,128)(2,1)S(1)}, u32[]{:S(2)}, u32[]{:S(2)}) collective-permute-start(bf16[6,3,128,128]{3,2,1,0:T(8,128)(2,1)} %get-tuple-element.18), channel_id=1, source_target_pairs={{1,0},{2,1},{3,2},{4,3},{5,4},{6,5},{7,6},{9,8},{10,9},{11,10},{12... | collective-permute-start | bytes 1769480 | tf_op jit(solution)/shard_map/ppermute | solution.py:178
  90.2 0.7 copy-done.28
  91.0 1.1 copy-done.12
  92.0 1.1 copy-done.18
  93.1 1.1 copy-done.20
  94.2 1.1 copy-done.25
  95.2 1.0 copy-done.29
  96.2 14.1 %encode.2 = (bf16[6,9,128,128]{3,2,1,0:T(8,128)(2,1)S(1)}, f32[6,32,128]{2,1,0:T(8,128)S(1)}) custom-call(s32[54]{0:T(128)S(1)} %reshape.306.index, bf16[12,9,128,128]{3,2,1,0:T(8,128)(2,1)} %bitcast.130, bf16[6,3,128,128]{3,2,1,0:T(8,128)(2,1)S(1)} %copy-done.25, bf16[6,3,128,128]{3,2,1,0:T(8,128)(2,1)} %collective-permute-done.3.rx_hi, ...), custom_call_target="tpu_custom_call" | custom-call | flops 2500000000 | bytes 8000000 | tf_op jit(solution)/shard_map/encode/pallas_call | solution.py:271
  110.5 2.2 %collective-permute-start.21 = (bf16[6,2,128,128]{3,2,1,0:T(8,128)(2,1)S(1)}, bf16[6,2,128,128]{3,2,1,0:T(8,128)(2,1)S(1)}, u32[]{:S(2)}, u32[]{:S(2)}) collective-permute-start(bf16[6,2,128,128]{3,2,1,0:T(8,128)(2,1)S(1)} %pad_maximum_fusion.7), channel_id=1, source_target_pairs={{8,0},{16,8},{24,16},{9,1},{17,9},{25,17},{10,2},{18,10},{26,18},{... | collective-permute-start | bytes 1179656 | tf_op jit(solution)/shard_map/ppermute | solution.py:178
  112.8 3.9 %collective-permute-start.20 = (bf16[6,2,128,128]{3,2,1,0:T(8,128)(2,1)S(1)}, bf16[6,2,128,128]{3,2,1,0:T(8,128)(2,1)S(1)}, u32[]{:S(2)}, u32[]{:S(2)}) collective-permute-start(bf16[6,2,128,128]{3,2,1,0:T(8,128)(2,1)S(1)} %pad_maximum_fusion.6), channel_id=1, source_target_pairs={{0,8},{8,16},{16,24},{1,9},{9,17},{17,25},{2,10},{10,18},{18,26},{... | collective-permute-start | bytes 1179656 | tf_op jit(solution)/shard_map/ppermute | solution.py:178
  116.7 1.1 slice_bitcast_fusion.6
  117.8 4.5 %collective-permute-start.10 = (bf16[6,3,128,128]{3,2,1,0:T(8,128)(2,1)}, bf16[6,3,128,128]{3,2,1,0:T(8,128)(2,1)S(1)}, u32[]{:S(2)}, u32[]{:S(2)}) collective-permute-start(bf16[6,3,128,128]{3,2,1,0:T(8,128)(2,1)} %get-tuple-element.22), channel_id=1, source_target_pairs={{0,1},{1,2},{2,3},{3,4},{4,5},{5,6},{6,7},{8,9},{9,10},{10,11},{11... | collective-permute-start | bytes 1769480 | tf_op jit(solution)/shard_map/ppermute | solution.py:178
  122.4 1.1 slice_bitcast_fusion
  123.5 2.7 %collective-permute-start.22 = (bf16[6,3,128,128]{3,2,1,0:T(8,128)(2,1)}, bf16[6,3,128,128]{3,2,1,0:T(8,128)(2,1)}, u32[]{:S(2)}, u32[]{:S(2)}) collective-permute-start(bf16[6,3,128,128]{3,2,1,0:T(8,128)(2,1)} %get-tuple-element.16), channel_id=1, source_target_pairs={{0,8},{8,16},{16,24},{1,9},{9,17},{17,25},{2,10},{10,18},{18,26},{... | collective-permute-start | bytes 1769480 | tf_op jit(solution)/shard_map/ppermute | solution.py:178
  126.2 2.5 %collective-permute-start.23 = (bf16[6,3,128,128]{3,2,1,0:T(8,128)(2,1)}, bf16[6,3,128,128]{3,2,1,0:T(8,128)(2,1)}, u32[]{:S(2)}, u32[]{:S(2)}) collective-permute-start(bf16[6,3,128,128]{3,2,1,0:T(8,128)(2,1)} %get-tuple-element.15), channel_id=1, source_target_pairs={{8,0},{16,8},{24,16},{9,1},{17,9},{25,17},{10,2},{18,10},{26,18},{... | collective-permute-start | bytes 1769480 | tf_op jit(solution)/shard_map/ppermute | solution.py:178
  128.7 1.9 collective-permute-start.11
  130.6 0.6 slice.199
  131.7 0.7 copy-done.15
  133.8 0.8 copy.84
  134.7 5.3 %all-to-all-start = ((f32[32,12,128]{2,1,0:T(8,128)}), f32[32,12,128]{2,1,0:T(8,128)}, u32[]{:S(2)}, u32[]{:S(2)}) async-start(f32[32,12,128]{2,1,0:T(8,128)} %copy.84), calls=%async_computation | async-start | bytes 524288 | tf_op jit(solution)/shard_map/all_to_all | solution.py:300
  140.0 1.1 slice_bitcast_fusion.8
  141.1 3.3 %collective-permute-start.8 = (bf16[6,3,128,128]{3,2,1,0:T(8,128)(2,1)}, bf16[6,3,128,128]{3,2,1,0:T(8,128)(2,1)S(1)}, u32[]{:S(2)}, u32[]{:S(2)}) collective-permute-start(bf16[6,3,128,128]{3,2,1,0:T(8,128)(2,1)} %get-tuple-element.24), channel_id=1, source_target_pairs={{0,8},{8,16},{16,24},{1,9},{9,17},{17,25},{2,10},{10,18},{18,26},{... | collective-permute-start | bytes 1769480 | tf_op jit(solution)/shard_map/ppermute | solution.py:178
  144.5 4.4 %collective-permute-done.10.ry_lo = bf16[6,3,128,128]{3,2,1,0:T(8,128)(2,1)S(1)} collective-permute-done((bf16[6,3,128,128]{3,2,1,0:T(8,128)(2,1)}, bf16[6,3,128,128]{3,2,1,0:T(8,128)(2,1)S(1)}, u32[]{:S(2)}, u32[]{:S(2)}) %collective-permute-start.10) | collective-permute-done | bytes 589856 | tf_op jit(solution)/shard_map/ppermute | solution.py:178
  148.9 1.9 collective-permute-start.9
  150.9 1.0 reduce_sum.18
  151.9 0.7 broadcast_in_dim.41
  152.6 7.4 %all-to-all-start.1 = ((bf16[32,21,128]{2,1,0:T(8,128)(2,1)}), bf16[32,21,128]{2,1,0:T(8,128)(2,1)S(1)}, u32[]{:S(2)}, u32[]{:S(2)}) async-start(bf16[32,21,128]{2,1,0:T(8,128)(2,1)} %broadcast_in_dim.41), calls=%async_computation.1 | async-start | bytes 393216 | tf_op jit(solution)/shard_map/all_to_all | solution.py:309
  160.0 0.9 pad_maximum_fusion.3
  161.0 2.4 %collective-permute-start.13 = (bf16[6,2,128,128]{3,2,1,0:T(8,128)(2,1)}, bf16[6,2,128,128]{3,2,1,0:T(8,128)(2,1)}, u32[]{:S(2)}, u32[]{:S(2)}) collective-permute-start(bf16[6,2,128,128]{3,2,1,0:T(8,128)(2,1)} %pad_maximum_fusion.3), channel_id=1, source_target_pairs={{8,0},{16,8},{24,16},{9,1},{17,9},{25,17},{10,2},{18,10},{26,18},{... | collective-permute-start | bytes 1179656 | tf_op jit(solution)/shard_map/ppermute | solution.py:178
  163.4 0.8 pad_maximum_fusion.2
  164.2 4.2 %all-to-all-done.1 = bf16[32,21,128]{2,1,0:T(8,128)(2,1)S(1)} async-done(((bf16[32,21,128]{2,1,0:T(8,128)(2,1)}), bf16[32,21,128]{2,1,0:T(8,128)(2,1)S(1)}, u32[]{:S(2)}, u32[]{:S(2)}) %all-to-all-start.1) | async-done | bytes 172064 | tf_op jit(solution)/shard_map/all_to_all | solution.py:309
  168.5 0.6 gather_fusion
  169.1 2.6 %collective-permute-start.12 = (bf16[6,2,128,128]{3,2,1,0:T(8,128)(2,1)}, bf16[6,2,128,128]{3,2,1,0:T(8,128)(2,1)}, u32[]{:S(2)}, u32[]{:S(2)}) collective-permute-start(bf16[6,2,128,128]{3,2,1,0:T(8,128)(2,1)} %pad_maximum_fusion.2), channel_id=1, source_target_pairs={{0,8},{8,16},{16,24},{1,9},{9,17},{17,25},{2,10},{10,18},{18,26},{... | collective-permute-start | bytes 1179656 | tf_op jit(solution)/shard_map/ppermute | solution.py:178
  172.3 0.9 slice.200
  173.4 1.0 copy-done.14
  174.3 1.0 copy-done.16
  175.3 13.2 %decode.2.rest_0_ = bf16[12,9,128,128]{3,2,1,0:T(8,128)(2,1)} custom-call(s32[54]{0:T(128)S(1)} %reshape.306.index, bf16[6,9,128,128]{3,2,1,0:T(8,128)(2,1)} %copy-done.1, bf16[6,3,128,128]{3,2,1,0:T(8,128)(2,1)} %collective-permute-done.22.rx_lo, bf16[6,3,128,128]{3,2,1,0:T(8,128)(2,1)} %collective-permute-done.23.rx_hi, ...), custom_call_target="tpu_custom_call" | custom-call | flops 2500000000 | bytes 8000000 | tf_op jit(solution)/shard_map/decode/pallas_call | solution.py:326
  188.6 13.2 %decode.3 = bf16[12,9,128,128]{3,2,1,0:T(8,128)(2,1)} custom-call(s32[54]{0:T(128)S(1)} %reshape.306.index, bf16[6,9,128,128]{3,2,1,0:T(8,128)(2,1)} %copy-done, bf16[6,3,128,128]{3,2,1,0:T(8,128)(2,1)S(1)} %collective-permute-done.8.rx_lo, bf16[6,3,128,128]{3,2,1,0:T(8,128)(2,1)} %collective-permute-done.9.rx_hi, ...), custom_call_target="tpu_custom_call", output_to_operand_aliasing={{}: (13, {})} | custom-call | flops 2500000000 | bytes 8000000 | tf_op jit(solution)/shard_map/decode/pallas_call | solution.py:326
  (127 shorter events, 4.2 us)
Async XLA Ops:
  4.6 13.7 %copy-start.37 = (s32[1152]{0:T(1024)S(1)}, s32[1152]{0:T(1024)}, u32[]{:S(2)}) copy-start(s32[1152]{0:T(1024)} %param.17) | copy-start | bytes 13828
  4.6 13.9 %copy-start.38 = (s32[9,6]{0,1:T(8,128)S(1)}, s32[9,6]{0,1:T(8,128)}, u32[]{:S(2)}) copy-start(s32[9,6]{0,1:T(8,128)} %param.13) | copy-start | bytes 652
  4.6 14.1 %copy-start.39 = (bf16[1152]{0:T(1024)(128)(2,1)S(1)}, bf16[1152]{0:T(1024)(128)(2,1)}, u32[]{:S(2)}) copy-start(bf16[1152]{0:T(1024)(128)(2,1)} %param.16) | copy-start | bytes 6916
  4.6 14.2 %copy-start.23 = (s32[144,1]{0,1:T(1,128)S(1)}, s32[144,1]{0,1:T(1,128)}, u32[]{:S(2)}) copy-start(s32[144,1]{0,1:T(1,128)} %param.18) | copy-start | bytes 1732
  4.6 28.2 %collective-permute-start = (bf16[6,3,128,128]{3,2,1,0:T(8,128)(2,1)}, bf16[6,3,128,128]{3,2,1,0:T(8,128)(2,1)S(1)}, u32[]{:S(2)}, u32[]{:S(2)}) collective-permute-start(bf16[6,3,128,128]{3,2,1,0:T(8,128)(2,1)} %get-tuple-element.30), channel_id=1, source_target_pairs={{0,1},{1,2},{2,3},{3,4},{4,5},{5,6},{6,7},{8,9},{9,10},{10,11},{11... | collective-permute-start | bytes 1769480 | tf_op jit(solution)/shard_map/ppermute | solution.py:178
  7.9 27.7 %collective-permute-start.1 = (bf16[6,3,128,128]{3,2,1,0:T(8,128)(2,1)}, bf16[6,3,128,128]{3,2,1,0:T(8,128)(2,1)S(1)}, u32[]{:S(2)}, u32[]{:S(2)}) collective-permute-start(bf16[6,3,128,128]{3,2,1,0:T(8,128)(2,1)} %get-tuple-element.29), channel_id=1, source_target_pairs={{1,0},{2,1},{3,2},{4,3},{5,4},{6,5},{7,6},{9,8},{10,9},{11,10},{12... | collective-permute-start | bytes 1769480 | tf_op jit(solution)/shard_map/ppermute | solution.py:178
  12.1 35.7 %collective-permute-start.14 = (bf16[6,3,128,128]{3,2,1,0:T(8,128)(2,1)}, bf16[6,3,128,128]{3,2,1,0:T(8,128)(2,1)S(1)}, u32[]{:S(2)}, u32[]{:S(2)}) collective-permute-start(bf16[6,3,128,128]{3,2,1,0:T(8,128)(2,1)} %get-tuple-element.20), channel_id=1, source_target_pairs={{0,8},{8,16},{16,24},{1,9},{9,17},{17,25},{2,10},{10,18},{18,26},{... | collective-permute-start | bytes 1769480 | tf_op jit(solution)/shard_map/ppermute | solution.py:178
  16.3 35.4 %collective-permute-start.15 = (bf16[6,3,128,128]{3,2,1,0:T(8,128)(2,1)}, bf16[6,3,128,128]{3,2,1,0:T(8,128)(2,1)S(1)}, u32[]{:S(2)}, u32[]{:S(2)}) collective-permute-start(bf16[6,3,128,128]{3,2,1,0:T(8,128)(2,1)} %get-tuple-element.19), channel_id=1, source_target_pairs={{8,0},{16,8},{24,16},{9,1},{17,9},{25,17},{10,2},{18,10},{26,18},{... | collective-permute-start | bytes 1769480 | tf_op jit(solution)/shard_map/ppermute | solution.py:178
  18.5 40.2 %copy-start.11 = (s32[1152,1]{1,0:T(8,128)}, s32[1152,1]{1,0:T(8,128)S(1)}, u32[]{:S(2)}) copy-start(s32[1152,1]{1,0:T(8,128)S(1)} %reshape.333.cluster_col) | copy-start | bytes 13828
  18.7 24.9 %copy-start.35 = (bf16[6,1152,128]{2,1,0:T(8,128)(2,1)S(1)}, bf16[6,1152,128]{2,1,0:T(8,128)(2,1)}, u32[]{:S(2)}) copy-start(bf16[6,1152,128]{2,1,0:T(8,128)(2,1)} %get-tuple-element.14) | copy-start | bytes 5308420
  35.7 21.1 %collective-permute-start.16 = (bf16[6,2,128,128]{3,2,1,0:T(8,128)(2,1)S(1)}, bf16[6,2,128,128]{3,2,1,0:T(8,128)(2,1)S(1)}, u32[]{:S(2)}, u32[]{:S(2)}) collective-permute-start(bf16[6,2,128,128]{3,2,1,0:T(8,128)(2,1)S(1)} %pad_maximum_fusion.4), channel_id=1, source_target_pairs={{0,8},{8,16},{16,24},{1,9},{9,17},{17,25},{2,10},{10,18},{18,26},{... | collective-permute-start | bytes 1179656 | tf_op jit(solution)/shard_map/ppermute | solution.py:178
  39.3 19.4 %collective-permute-start.17 = (bf16[6,2,128,128]{3,2,1,0:T(8,128)(2,1)S(1)}, bf16[6,2,128,128]{3,2,1,0:T(8,128)(2,1)S(1)}, u32[]{:S(2)}, u32[]{:S(2)}) collective-permute-start(bf16[6,2,128,128]{3,2,1,0:T(8,128)(2,1)S(1)} %pad_maximum_fusion.5), channel_id=1, source_target_pairs={{8,0},{16,8},{24,16},{9,1},{17,9},{25,17},{10,2},{18,10},{26,18},{... | collective-permute-start | bytes 1179656 | tf_op jit(solution)/shard_map/ppermute | solution.py:178
  43.9 14.8 %copy-start.30 = (bf16[128,128]{1,0:T(8,128)(2,1)S(1)}, bf16[128,128]{1,0:T(8,128)(2,1)}, u32[]{:S(2)}) copy-start(bf16[128,128]{1,0:T(8,128)(2,1)} %w_mix.3) | copy-start | bytes 98308
  44.0 14.8 %copy-start.32 = (bf16[128,128]{1,0:T(8,128)(2,1)S(1)}, bf16[128,128]{1,0:T(8,128)(2,1)}, u32[]{:S(2)}) copy-start(bf16[128,128]{1,0:T(8,128)(2,1)} %w_coarse.3) | copy-start | bytes 98308
  44.0 14.8 %copy-start.34 = (f32[128]{0:T(128)S(1)}, f32[128]{0:T(128)}, u32[]{:S(2)}) copy-start(f32[128]{0:T(128)} %param.14) | copy-start | bytes 1540
  44.0 33.3 %collective-permute-start.4 = (bf16[6,3,128,128]{3,2,1,0:T(8,128)(2,1)S(1)}, bf16[6,3,128,128]{3,2,1,0:T(8,128)(2,1)S(1)}, u32[]{:S(2)}, u32[]{:S(2)}) collective-permute-start(bf16[6,3,128,128]{3,2,1,0:T(8,128)(2,1)S(1)} %get-tuple-element.26), channel_id=1, source_target_pairs={{0,1},{1,2},{2,3},{3,4},{4,5},{5,6},{6,7},{8,9},{9,10},{10,11},{11... | collective-permute-start | bytes 1769480 | tf_op jit(solution)/shard_map/ppermute | solution.py:178
  47.8 29.5 %collective-permute-start.5 = (bf16[6,3,128,128]{3,2,1,0:T(8,128)(2,1)S(1)}, bf16[6,3,128,128]{3,2,1,0:T(8,128)(2,1)S(1)}, u32[]{:S(2)}, u32[]{:S(2)}) collective-permute-start(bf16[6,3,128,128]{3,2,1,0:T(8,128)(2,1)S(1)} %get-tuple-element.25), channel_id=1, source_target_pairs={{1,0},{2,1},{3,2},{4,3},{5,4},{6,5},{7,6},{9,8},{10,9},{11,10},{12... | collective-permute-start | bytes 1769480 | tf_op jit(solution)/shard_map/ppermute | solution.py:178
  51.7 0.8 copy-start.26
  52.6 32.3 %collective-permute-start.2 = (bf16[6,3,128,128]{3,2,1,0:T(8,128)(2,1)}, bf16[6,3,128,128]{3,2,1,0:T(8,128)(2,1)S(1)}, u32[]{:S(2)}, u32[]{:S(2)}) collective-permute-start(bf16[6,3,128,128]{3,2,1,0:T(8,128)(2,1)} %get-tuple-element.28), channel_id=1, source_target_pairs={{0,8},{8,16},{16,24},{1,9},{9,17},{17,25},{2,10},{10,18},{18,26},{... | collective-permute-start | bytes 1769480 | tf_op jit(solution)/shard_map/ppermute | solution.py:178
  56.8 33.4 %collective-permute-start.3 = (bf16[6,3,128,128]{3,2,1,0:T(8,128)(2,1)}, bf16[6,3,128,128]{3,2,1,0:T(8,128)(2,1)}, u32[]{:S(2)}, u32[]{:S(2)}) collective-permute-start(bf16[6,3,128,128]{3,2,1,0:T(8,128)(2,1)} %get-tuple-element.27), channel_id=1, source_target_pairs={{8,0},{16,8},{24,16},{9,1},{17,9},{25,17},{10,2},{18,10},{26,18},{... | collective-permute-start | bytes 1769480 | tf_op jit(solution)/shard_map/ppermute | solution.py:178
  58.8 1.1 copy-start.27
  73.9 3.5 %copy-start.1 = (bf16[6,9,128,128]{3,2,1,0:T(8,128)(2,1)}, bf16[6,9,128,128]{3,2,1,0:T(8,128)(2,1)S(1)}, u32[]{:S(2)}) copy-start(bf16[6,9,128,128]{3,2,1,0:T(8,128)(2,1)S(1)} %get-tuple-element.12.own) | copy-start | bytes 5308420
  75.2 15.7 %copy-start.31 = (bf16[128,128]{1,0:T(8,128)(2,1)S(1)}, bf16[128,128]{1,0:T(8,128)(2,1)}, u32[]{:S(2)}) copy-start(bf16[128,128]{1,0:T(8,128)(2,1)} %w_mix.3) | copy-start | bytes 98308
  75.2 15.7 %copy-start.33 = (bf16[128,128]{1,0:T(8,128)(2,1)S(1)}, bf16[128,128]{1,0:T(8,128)(2,1)}, u32[]{:S(2)}) copy-start(bf16[128,128]{1,0:T(8,128)(2,1)} %w_coarse.3) | copy-start | bytes 98308
  75.2 35.1 %collective-permute-start.18 = (bf16[6,3,128,128]{3,2,1,0:T(8,128)(2,1)}, bf16[6,3,128,128]{3,2,1,0:T(8,128)(2,1)S(1)}, u32[]{:S(2)}, u32[]{:S(2)}) collective-permute-start(bf16[6,3,128,128]{3,2,1,0:T(8,128)(2,1)} %get-tuple-element.17), channel_id=1, source_target_pairs={{0,1},{1,2},{2,3},{3,4},{4,5},{5,6},{6,7},{8,9},{9,10},{10,11},{11... | collective-permute-start | bytes 1769480 | tf_op jit(solution)/shard_map/ppermute | solution.py:178
  77.3 0.8 copy-start.17
  77.3 1.0 copy-start.19
  78.4 11.8 %collective-permute-start.7 = (bf16[6,2,128,128]{3,2,1,0:T(8,128)(2,1)S(1)}, bf16[6,2,128,128]{3,2,1,0:T(8,128)(2,1)S(1)}, u32[]{:S(2)}, u32[]{:S(2)}) collective-permute-start(bf16[6,2,128,128]{3,2,1,0:T(8,128)(2,1)S(1)} %pad_maximum_fusion.1), channel_id=1, source_target_pairs={{8,0},{16,8},{24,16},{9,1},{17,9},{25,17},{10,2},{18,10},{26,18},{... | collective-permute-start | bytes 1179656 | tf_op jit(solution)/shard_map/ppermute | solution.py:178
  81.1 9.1 %collective-permute-start.6 = (bf16[6,2,128,128]{3,2,1,0:T(8,128)(2,1)}, bf16[6,2,128,128]{3,2,1,0:T(8,128)(2,1)S(1)}, u32[]{:S(2)}, u32[]{:S(2)}) collective-permute-start(bf16[6,2,128,128]{3,2,1,0:T(8,128)(2,1)} %pad_maximum_fusion), channel_id=1, source_target_pairs={{0,8},{8,16},{16,24},{1,9},{9,17},{17,25},{2,10},{10,18},{18,26},{... | collective-permute-start | bytes 1179656 | tf_op jit(solution)/shard_map/ppermute | solution.py:178
  84.9 0.8 copy-start.24
  85.7 24.7 %collective-permute-start.19 = (bf16[6,3,128,128]{3,2,1,0:T(8,128)(2,1)}, bf16[6,3,128,128]{3,2,1,0:T(8,128)(2,1)S(1)}, u32[]{:S(2)}, u32[]{:S(2)}) collective-permute-start(bf16[6,3,128,128]{3,2,1,0:T(8,128)(2,1)} %get-tuple-element.18), channel_id=1, source_target_pairs={{1,0},{2,1},{3,2},{4,3},{5,4},{6,5},{7,6},{9,8},{10,9},{11,10},{12... | collective-permute-start | bytes 1769480 | tf_op jit(solution)/shard_map/ppermute | solution.py:178
  91.0 1.1 copy-start.12
  92.0 1.1 copy-start.18
  93.1 1.1 copy-start.20
  94.2 1.1 copy-start.25
  95.2 1.0 copy-start.29
  110.4 29.7 %copy-start = (bf16[6,9,128,128]{3,2,1,0:T(8,128)(2,1)}, bf16[6,9,128,128]{3,2,1,0:T(8,128)(2,1)S(1)}, u32[]{:S(2)}) copy-start(bf16[6,9,128,128]{3,2,1,0:T(8,128)(2,1)S(1)} %get-tuple-element.9.own) | copy-start | bytes 5308420
  110.4 7.5 %copy-start.3 = (bf16[6,3,128,128]{3,2,1,0:T(8,128)(2,1)}, bf16[6,3,128,128]{3,2,1,0:T(8,128)(2,1)S(1)}, u32[]{:S(2)}) copy-start(bf16[6,3,128,128]{3,2,1,0:T(8,128)(2,1)S(1)} %collective-permute-done.18.ry_lo) | copy-start | bytes 1769476
  110.4 7.4 %copy-start.5 = (bf16[6,3,128,128]{3,2,1,0:T(8,128)(2,1)}, bf16[6,3,128,128]{3,2,1,0:T(8,128)(2,1)S(1)}, u32[]{:S(2)}) copy-start(bf16[6,3,128,128]{3,2,1,0:T(8,128)(2,1)S(1)} %collective-permute-done.19.ry_hi) | copy-start | bytes 1769476
  110.5 11.9 %copy-start.2 = (bf16[6,9,128,128]{3,2,1,0:T(8,128)(2,1)S(1)}, bf16[6,9,128,128]{3,2,1,0:T(8,128)(2,1)}, u32[]{:S(2)}) copy-start(bf16[6,9,128,128]{3,2,1,0:T(8,128)(2,1)} %copy-done.1) | copy-start | bytes 5308420
  110.5 18.1 %collective-permute-start.21 = (bf16[6,2,128,128]{3,2,1,0:T(8,128)(2,1)S(1)}, bf16[6,2,128,128]{3,2,1,0:T(8,128)(2,1)S(1)}, u32[]{:S(2)}, u32[]{:S(2)}) collective-permute-start(bf16[6,2,128,128]{3,2,1,0:T(8,128)(2,1)S(1)} %pad_maximum_fusion.7), channel_id=1, source_target_pairs={{8,0},{16,8},{24,16},{9,1},{17,9},{25,17},{10,2},{18,10},{26,18},{... | collective-permute-start | bytes 1179656 | tf_op jit(solution)/shard_map/ppermute | solution.py:178
  112.8 18.4 %collective-permute-start.20 = (bf16[6,2,128,128]{3,2,1,0:T(8,128)(2,1)S(1)}, bf16[6,2,128,128]{3,2,1,0:T(8,128)(2,1)S(1)}, u32[]{:S(2)}, u32[]{:S(2)}) collective-permute-start(bf16[6,2,128,128]{3,2,1,0:T(8,128)(2,1)S(1)} %pad_maximum_fusion.6), channel_id=1, source_target_pairs={{0,8},{8,16},{16,24},{1,9},{9,17},{17,25},{2,10},{10,18},{18,26},{... | collective-permute-start | bytes 1179656 | tf_op jit(solution)/shard_map/ppermute | solution.py:178
  117.8 31.1 %collective-permute-start.10 = (bf16[6,3,128,128]{3,2,1,0:T(8,128)(2,1)}, bf16[6,3,128,128]{3,2,1,0:T(8,128)(2,1)S(1)}, u32[]{:S(2)}, u32[]{:S(2)}) collective-permute-start(bf16[6,3,128,128]{3,2,1,0:T(8,128)(2,1)} %get-tuple-element.22), channel_id=1, source_target_pairs={{0,1},{1,2},{2,3},{3,4},{4,5},{5,6},{6,7},{8,9},{9,10},{10,11},{11... | collective-permute-start | bytes 1769480 | tf_op jit(solution)/shard_map/ppermute | solution.py:178
  123.5 45.5 %collective-permute-start.22 = (bf16[6,3,128,128]{3,2,1,0:T(8,128)(2,1)}, bf16[6,3,128,128]{3,2,1,0:T(8,128)(2,1)}, u32[]{:S(2)}, u32[]{:S(2)}) collective-permute-start(bf16[6,3,128,128]{3,2,1,0:T(8,128)(2,1)} %get-tuple-element.16), channel_id=1, source_target_pairs={{0,8},{8,16},{16,24},{1,9},{9,17},{17,25},{2,10},{10,18},{18,26},{... | collective-permute-start | bytes 1769480 | tf_op jit(solution)/shard_map/ppermute | solution.py:178
  126.2 47.1 %collective-permute-start.23 = (bf16[6,3,128,128]{3,2,1,0:T(8,128)(2,1)}, bf16[6,3,128,128]{3,2,1,0:T(8,128)(2,1)}, u32[]{:S(2)}, u32[]{:S(2)}) collective-permute-start(bf16[6,3,128,128]{3,2,1,0:T(8,128)(2,1)} %get-tuple-element.15), channel_id=1, source_target_pairs={{8,0},{16,8},{24,16},{9,1},{17,9},{25,17},{10,2},{18,10},{26,18},{... | collective-permute-start | bytes 1769480 | tf_op jit(solution)/shard_map/ppermute | solution.py:178
  128.7 12.4 %copy-start.13 = (bf16[6,2,128,128]{3,2,1,0:T(8,128)(2,1)}, bf16[6,2,128,128]{3,2,1,0:T(8,128)(2,1)S(1)}, u32[]{:S(2)}) copy-start(bf16[6,2,128,128]{3,2,1,0:T(8,128)(2,1)S(1)} %collective-permute-done.21.co_hi) | copy-start | bytes 1179652
  128.7 31.3 %collective-permute-start.11 = (bf16[6,3,128,128]{3,2,1,0:T(8,128)(2,1)}, bf16[6,3,128,128]{3,2,1,0:T(8,128)(2,1)S(1)}, u32[]{:S(2)}, u32[]{:S(2)}) collective-permute-start(bf16[6,3,128,128]{3,2,1,0:T(8,128)(2,1)} %get-tuple-element.21), channel_id=1, source_target_pairs={{1,0},{2,1},{3,2},{4,3},{5,4},{6,5},{7,6},{9,8},{10,9},{11,10},{12... | collective-permute-start | bytes 1769480 | tf_op jit(solution)/shard_map/ppermute | solution.py:178
  134.7 16.2 %all-to-all-start = ((f32[32,12,128]{2,1,0:T(8,128)}), f32[32,12,128]{2,1,0:T(8,128)}, u32[]{:S(2)}, u32[]{:S(2)}) async-start(f32[32,12,128]{2,1,0:T(8,128)} %copy.84), calls=%async_computation | async-start | bytes 524288 | tf_op jit(solution)/shard_map/all_to_all | solution.py:300
  141.1 47.4 %collective-permute-start.8 = (bf16[6,3,128,128]{3,2,1,0:T(8,128)(2,1)}, bf16[6,3,128,128]{3,2,1,0:T(8,128)(2,1)S(1)}, u32[]{:S(2)}, u32[]{:S(2)}) collective-permute-start(bf16[6,3,128,128]{3,2,1,0:T(8,128)(2,1)} %get-tuple-element.24), channel_id=1, source_target_pairs={{0,8},{8,16},{16,24},{1,9},{9,17},{17,25},{2,10},{10,18},{18,26},{... | collective-permute-start | bytes 1769480 | tf_op jit(solution)/shard_map/ppermute | solution.py:178
  148.9 15.3 %copy-start.7 = (bf16[6,3,128,128]{3,2,1,0:T(8,128)(2,1)}, bf16[6,3,128,128]{3,2,1,0:T(8,128)(2,1)S(1)}, u32[]{:S(2)}) copy-start(bf16[6,3,128,128]{3,2,1,0:T(8,128)(2,1)S(1)} %collective-permute-done.10.ry_lo) | copy-start | bytes 1769476
  148.9 39.6 %collective-permute-start.9 = (bf16[6,3,128,128]{3,2,1,0:T(8,128)(2,1)}, bf16[6,3,128,128]{3,2,1,0:T(8,128)(2,1)}, u32[]{:S(2)}, u32[]{:S(2)}) collective-permute-start(bf16[6,3,128,128]{3,2,1,0:T(8,128)(2,1)} %get-tuple-element.23), channel_id=1, source_target_pairs={{8,0},{16,8},{24,16},{9,1},{17,9},{25,17},{10,2},{18,10},{26,18},{... | collective-permute-start | bytes 1769480 | tf_op jit(solution)/shard_map/ppermute | solution.py:178
  152.6 15.8 %all-to-all-start.1 = ((bf16[32,21,128]{2,1,0:T(8,128)(2,1)}), bf16[32,21,128]{2,1,0:T(8,128)(2,1)S(1)}, u32[]{:S(2)}, u32[]{:S(2)}) async-start(bf16[32,21,128]{2,1,0:T(8,128)(2,1)} %broadcast_in_dim.41), calls=%async_computation.1 | async-start | bytes 393216 | tf_op jit(solution)/shard_map/all_to_all | solution.py:309
  160.0 11.8 %copy-start.9 = (bf16[6,3,128,128]{3,2,1,0:T(8,128)(2,1)}, bf16[6,3,128,128]{3,2,1,0:T(8,128)(2,1)S(1)}, u32[]{:S(2)}) copy-start(bf16[6,3,128,128]{3,2,1,0:T(8,128)(2,1)S(1)} %collective-permute-done.11.ry_hi) | copy-start | bytes 1769476
  161.0 12.3 %copy-start.4 = (bf16[6,3,128,128]{3,2,1,0:T(8,128)(2,1)S(1)}, bf16[6,3,128,128]{3,2,1,0:T(8,128)(2,1)}, u32[]{:S(2)}) copy-start(bf16[6,3,128,128]{3,2,1,0:T(8,128)(2,1)} %copy-done.3) | copy-start | bytes 1769476
  161.0 12.3 %copy-start.6 = (bf16[6,3,128,128]{3,2,1,0:T(8,128)(2,1)S(1)}, bf16[6,3,128,128]{3,2,1,0:T(8,128)(2,1)}, u32[]{:S(2)}) copy-start(bf16[6,3,128,128]{3,2,1,0:T(8,128)(2,1)} %copy-done.5) | copy-start | bytes 1769476
  161.0 12.4 %copy-start.21 = (bf16[128,128]{1,0:T(8,128)(2,1)S(1)}, bf16[128,128]{1,0:T(8,128)(2,1)}, u32[]{:S(2)}) copy-start(bf16[128,128]{1,0:T(8,128)(2,1)} %w_region.3) | copy-start | bytes 98308
  161.0 12.4 %copy-start.22 = (bf16[128,128]{1,0:T(8,128)(2,1)S(1)}, bf16[128,128]{1,0:T(8,128)(2,1)}, u32[]{:S(2)}) copy-start(bf16[128,128]{1,0:T(8,128)(2,1)} %w_out.3) | copy-start | bytes 98308
  161.0 27.6 %collective-permute-start.13 = (bf16[6,2,128,128]{3,2,1,0:T(8,128)(2,1)}, bf16[6,2,128,128]{3,2,1,0:T(8,128)(2,1)}, u32[]{:S(2)}, u32[]{:S(2)}) collective-permute-start(bf16[6,2,128,128]{3,2,1,0:T(8,128)(2,1)} %pad_maximum_fusion.3), channel_id=1, source_target_pairs={{8,0},{16,8},{24,16},{9,1},{17,9},{25,17},{10,2},{18,10},{26,18},{... | collective-permute-start | bytes 1179656 | tf_op jit(solution)/shard_map/ppermute | solution.py:178
  168.4 3.4 %copy-start.36 = (bf16[32,21,128]{2,1,0:T(8,128)(2,1)}, bf16[32,21,128]{2,1,0:T(8,128)(2,1)S(1)}, u32[]{:S(2)}) copy-start(bf16[32,21,128]{2,1,0:T(8,128)(2,1)S(1)} %all-to-all-done.1) | copy-start | bytes 516100
  169.1 19.5 %collective-permute-start.12 = (bf16[6,2,128,128]{3,2,1,0:T(8,128)(2,1)}, bf16[6,2,128,128]{3,2,1,0:T(8,128)(2,1)}, u32[]{:S(2)}, u32[]{:S(2)}) collective-permute-start(bf16[6,2,128,128]{3,2,1,0:T(8,128)(2,1)} %pad_maximum_fusion.2), channel_id=1, source_target_pairs={{0,8},{8,16},{16,24},{1,9},{9,17},{17,25},{2,10},{10,18},{18,26},{... | collective-permute-start | bytes 1179656 | tf_op jit(solution)/shard_map/ppermute | solution.py:178
  173.3 1.0 copy-start.14
  174.3 1.0 copy-start.16
  175.3 13.2 %copy-start.8 = (bf16[6,3,128,128]{3,2,1,0:T(8,128)(2,1)S(1)}, bf16[6,3,128,128]{3,2,1,0:T(8,128)(2,1)}, u32[]{:S(2)}) copy-start(bf16[6,3,128,128]{3,2,1,0:T(8,128)(2,1)} %copy-done.7) | copy-start | bytes 1769476
  175.3 13.2 %copy-start.10 = (bf16[6,3,128,128]{3,2,1,0:T(8,128)(2,1)S(1)}, bf16[6,3,128,128]{3,2,1,0:T(8,128)(2,1)}, u32[]{:S(2)}) copy-start(bf16[6,3,128,128]{3,2,1,0:T(8,128)(2,1)} %copy-done.9) | copy-start | bytes 1769476
  (2 other events, 1.5 us)
